TPU v7x, 32 devices: a whole 2x2x4 slice. The times are simulated.
32 devices in a mesh: parts: 2 (over y), pre: 4 (over z), tp: 4 (over x, core).
Axes of the slice: x: 2, y: 2, z: 4, core: 2. Of those that a mesh axis runs over, the one named last changes fastest.
Arguments:
- queries: bfloat16 [4096, 4096], P(('parts', 'pre'), 'tp'), parts along dimension 0, may hold values from -4.5 to 4.5
- new_keys: bfloat16 [4096, 1024], P(('parts', 'pre'), 'tp'), parts along dimension 0, may hold values from -4.5 to 4.5
- new_values: bfloat16 [4096, 1024], P(('parts', 'pre'), 'tp'), parts along dimension 0, may hold values from -4 to 4
- lengths: int32 [8], P('parts'), parts along dimension 0, may hold values from 1 to 1024, 2048 in all
- block_slot: int32 [256], P('parts'), parts along dimension 0, may hold values from 0 to 127, as said below
Outputs:
- attended: bfloat16 [4096, 4096], P(('parts', 'pre'), 'tp'), parts along dimension 0
- kv_cache: bfloat16 [256, 16, 2048], P(('parts', 'pre'), None, 'tp'), parts along dimension 0
There are 2 independent parts, one for each index of `parts`. A program takes and returns all parts, laid end to end along the dimension named above; each array names one. Nothing has to cross between parts.
Inputs may be any that keep to these rules, and one draw needn't show every extreme that they name: `block_slot`: A permutation of the 128 slots. The 32 blocks held by one index of pre (blocks of its own rows) take exactly 8 slots of every decode owner.
All inputs are finite; a program needn't handle non-finite values.
Results may differ from a plain program's by a relative error of at most 0.0036.
Values may be sent and summed in bfloat16 or wider, within the bound.
No kernel may reach another device: no remote copies, remote signals or barrier semaphores. Data moves between devices by JAX's collectives and lax.ppermute only.
A program may use at most 64 MiB of HBM per device.

v0:
```python
import functools
import math

import jax
import jax.numpy as jnp
from jax import lax
from jax.experimental import pallas as pl
from jax.experimental.pallas import tpu as pltpu
from jax.sharding import PartitionSpec as P

HD = 128
BLK = 16
GROUP = 4
TILE = 256
ONES = 16
MASKED = -1e30
EXP_SCALE = math.log2(math.e) * HD ** (-0.5)

VMEM = pl.BlockSpec(memory_space=pltpu.VMEM)
SMEM = pl.BlockSpec(memory_space=pltpu.SMEM)
HBM = pl.BlockSpec(memory_space=pltpu.HBM)


def start_of(lengths_ref, position):
    end = jnp.int32(0)
    start = jnp.int32(0)
    for r in range(lengths_ref.shape[0]):
        end = end + lengths_ref[r]
        start = jnp.where(end <= position, end, start)
    return start


def row_starts(lengths_ref, positions):
    end = jnp.int32(0)
    starts = jnp.zeros_like(positions)
    for r in range(lengths_ref.shape[0]):
        end = end + lengths_ref[r]
        starts = jnp.where(positions >= end, end, starts)
    return starts


def fill_bias(bias_ref, lengths_ref, row_first, key_first, low, high, causal):
    shape = (high - low, TILE)
    positions = row_first + lax.broadcasted_iota(jnp.int32, (8, TILE), 1)
    starts = row_starts(lengths_ref, positions)
    keys = key_first + low + lax.broadcasted_iota(jnp.int32, shape, 0)
    keys = keys.reshape((high - low) // 8, 8, TILE)
    allowed = keys >= starts[None]
    if causal:
        allowed = allowed & (keys <= positions[None])
    bias_ref[low:high] = jnp.where(allowed, 0.0, MASKED).reshape(shape)


def turn_values(v_ref, turned):
    for g in range(turned.shape[0]):
        turned[g, :HD] = v_ref[:, g * HD : (g + 1) * HD].T
        turned[g, HD:] = jnp.ones((ONES, turned.shape[2]), turned.dtype)


def lanes_of(tile, j):
    return slice((tile * GROUP + j) * TILE, (tile * GROUP + j + 1) * TILE)


def weigh(q_ref, k_ref, bias_ref, old_top, tile, low, high, g, emit):
    keys = k_ref[low:high, g * HD : (g + 1) * HD]
    heads = range(g * GROUP, (g + 1) * GROUP)
    queries = jnp.concatenate(
        [q_ref[tile * TILE : (tile + 1) * TILE, h * HD : (h + 1) * HD] for h in heads], axis=0
    )
    all_scores = lax.dot_general(
        keys, queries, (((1,), (1,)), ((), ())), preferred_element_type=jnp.float32
    )
    for j in range(GROUP):
        scores = all_scores[:, j * TILE : (j + 1) * TILE] + bias_ref[low:high]
        scores = scores.reshape((high - low) // 8, 8, TILE)
        highest = jnp.max(jnp.max(scores, axis=0), axis=0, keepdims=True)
        top = jnp.broadcast_to(highest, (8, TILE))
        factor = None
        if old_top is not None:
            old = old_top[g, :, lanes_of(tile, j)]
            top = jnp.maximum(old, top)
            factor = jnp.exp2((old - top) * EXP_SCALE)
        weights = jnp.exp2((scores - top[None]) * EXP_SCALE)
        emit(j, weights.reshape(high - low, TILE).astype(jnp.bfloat16), top, factor)


def mix(values, weights, g, tile, old, emit):
    all_added = jnp.dot(values, weights, preferred_element_type=jnp.float32)
    for j in range(GROUP):
        at = lanes_of(tile, j)
        added = all_added[:, j * TILE : (j + 1) * TILE]
        value, total = added[:HD], added[HD : HD + 8]
        if old is not None:
            acc_ref, sum_ref, factor_ref = old
            factor = factor_ref[g, :, at]
            total = total + sum_ref[g, :, at] * factor
            kept = acc_ref[g, :, at].reshape(HD // 8, 8, TILE) * factor[None]
            value = value + kept.reshape(HD, TILE)
        emit(g, j, value, total)


def keep(state, tile):
    def emit(g, j, value, total):
        for ref, array in zip(state, (value, total)):
            ref[g, :, lanes_of(tile, j)] = array

    return emit


def finish(out_ref, row):
    def emit(g, j, value, total):
        head = g * GROUP + j
        value = value.reshape(HD // 8, 8, TILE) * (1.0 / total)[None]
        value = value.reshape(HD, TILE).astype(out_ref.dtype).T
        out_ref[row : row + TILE, head * HD : (head + 1) * HD] = value

    return emit


def block_of(k_ref, v_ref, row):
    parts = []
    for g in range(k_ref.shape[1] // HD):
        span = slice(g * HD, (g + 1) * HD)
        parts += [k_ref[pl.ds(row, BLK), span], v_ref[pl.ds(row, BLK), span]]
    return jnp.concatenate(parts, axis=1)


def own_slot(slot, me, blocks):
    local = slot - me * blocks
    return jnp.where((local >= 0) & (local < blocks), local, blocks)


def own_kernel(
    pre, lengths_ref, slot_ref, q_hbm, k_hbm, v_hbm,
    q_ref, acc_ref, sum_ref, top_ref, cache_ref, *refs,
):
    sent_hbm, (k_ref, v_ref, turned, bias, sent, counts, sems, load_sems) = refs[:-8], refs[-8:]
    loads = [
        pltpu.make_async_copy(src, dst, load_sems.at[n])
        for n, (src, dst) in enumerate(((k_hbm, k_ref), (v_hbm, v_ref), (q_hbm, q_ref)))
    ]
    for load in loads:
        load.start()
    rows = q_ref.shape[0]
    blocks = rows // BLK
    per_peer = blocks // pre
    me = lax.axis_index("pre")
    first = me * rows
    for owner in range(pre):
        counts[owner] = 0
    loads[0].wait()
    loads[1].wait()

    def step(b, _):
        slot = slot_ref[me * blocks + b]
        owner = slot // blocks
        n = counts[owner]
        counts[owner] = n + 1
        distance = lax.rem(owner - me + pre, pre)
        at = jnp.where(distance > 1, (distance - 2) * per_peer + n, (pre - 2) * per_peer)
        block = block_of(k_ref, v_ref, pl.multiple_of(b * BLK, BLK))
        sent[at] = block
        cache_ref[own_slot(slot, me, blocks)] = block
        return 0

    lax.fori_loop(0, blocks, step, 0, unroll=8)
    stores = [
        pltpu.make_async_copy(sent.at[n * per_peer : (n + 1) * per_peer], ref, sems.at[n])
        for n, ref in enumerate(sent_hbm)
    ]
    for store in stores:
        store.start()
    turn_values(v_ref, turned)
    loads[2].wait()
    for tile in range(rows // TILE):
        high = (tile + 1) * TILE
        fill_bias(bias, lengths_ref, first + tile * TILE, first, 0, high, True)
        for g in range(turned.shape[0]):
            all_weights = []

            def emit(j, weights, top, factor):
                all_weights.append(weights)
                top_ref[g, :, lanes_of(tile, j)] = top

            weigh(q_ref, k_ref, bias, None, tile, 0, high, g, emit)
            all_weights = jnp.concatenate(all_weights, axis=1)
            mix(turned[g, :, :high], all_weights, g, tile, None, keep((acc_ref, sum_ref), tile))
    for store in stores:
        store.wait()


def lowest_key(lengths_ref, hop, tile, rows):
    first = lax.axis_index("pre") * rows
    key_first = first - hop * rows
    low = jnp.maximum(start_of(lengths_ref, first + tile * TILE) - key_first, 0)
    return jnp.where(key_first >= 0, jnp.minimum(low, rows), rows)


def where_seen(low, rows, act):
    for at in range(0, rows, TILE):
        pl.when((low >= at) & (low < at + TILE))(functools.partial(act, at))


def scores_kernel(hop, lengths_ref, q_ref, k_ref, old_top, weights_ref, factor_ref, *refs):
    *top_refs, bias = refs
    rows = q_ref.shape[0]
    first = lax.axis_index("pre") * rows
    for tile in range(rows // TILE):

        def act(at):
            fill_bias(
                bias, lengths_ref, first + tile * TILE, first - hop * rows, at, rows, False
            )
            for g in range(weights_ref.shape[1]):

                def emit(j, weights, top, factor):
                    weights_ref[tile, g, at:rows, j * TILE : (j + 1) * TILE] = weights
                    for top_ref in top_refs:
                        top_ref[g, :, lanes_of(tile, j)] = top
                    factor_ref[g, :, lanes_of(tile, j)] = factor

                weigh(q_ref, k_ref, bias, old_top, tile, at, rows, g, emit)

        where_seen(lowest_key(lengths_ref, hop, tile, rows), rows, act)


def values_kernel(
    hop, first_out, last, lengths_ref, v_ref, weights_ref, factor_ref, acc_in, sum_in, *refs
):
    refs = refs if first_out else refs[1:]
    out_hbm, *state, turned, out_buf, sems = refs
    rows = v_ref.shape[0]
    tiles = rows // TILE
    kv_count = turned.shape[0]
    lows = [lowest_key(lengths_ref, hop, tile, rows) for tile in range(tiles)]
    pl.when(lows[0] < rows)(functools.partial(turn_values, v_ref, turned))
    stores = []
    for tile, low in enumerate(lows):
        end_it = finish(out_buf, tile * TILE)

        def act(at):
            def emit(*result):
                if not last:
                    keep(state, tile)(*result)
                end_it(*result)

            for g in range(kv_count):
                weights = weights_ref[tile, g, at:rows]
                old = (acc_in, sum_in, factor_ref)
                mix(turned[g, :, at:rows], weights, g, tile, old, emit)

        where_seen(low, rows, act)
        span = slice(tile * TILE, (tile + 1) * TILE)
        store = pltpu.make_async_copy(out_buf.at[span], out_hbm.at[span], sems.at[tile])
        stores.append(store)
        if first_out:

            @pl.when(low == rows)
            def _():
                for g in range(kv_count):
                    for j in range(GROUP):
                        end_it(g, j, *(ref[g, :, lanes_of(tile, j)] for ref in (acc_in, sum_in)))

            store.start()
        else:
            pl.when(low < rows)(store.start)
    for low, store in zip(lows, stores):
        if first_out:
            store.wait()
        else:
            pl.when(low < rows)(store.wait)


def place_forwarded(cache, slot_ref, k_ref, v_ref, distance, pre, blocks):
    me = lax.axis_index("pre")
    source = lax.rem(me - distance + pre, pre)

    def step(b, _):
        at = own_slot(slot_ref[source * blocks + b], me, blocks)
        cache[at] = block_of(k_ref, v_ref, pl.multiple_of(b * BLK, BLK))
        return 0

    def run():
        lax.fori_loop(0, blocks, step, 0, unroll=8)

    if distance < 2:
        run()
    else:
        pl.when(me >= distance - 1)(run)


def place_packed(cache, slot_ref, got_ref, distance, forwarded, pre, blocks):
    me = lax.axis_index("pre")
    source = lax.rem(me - distance + pre, pre)
    most = got_ref.shape[0] - 1

    def step(b, n):
        at = own_slot(slot_ref[source * blocks + b], me, blocks)
        cache[at] = got_ref[jnp.minimum(n, most)]
        return n + jnp.where(at < blocks, 1, 0)

    def run():
        lax.fori_loop(0, blocks, step, jnp.int32(0), unroll=8)

    if forwarded:
        pl.when(me < distance - 1)(run)
    else:
        run()


def place_near_kernel(pre, slot_ref, cache_in, k_ref, v_ref, cache_ref):
    cache_ref[...] = cache_in[...]
    place_forwarded(cache_ref, slot_ref, k_ref, v_ref, 1, pre, k_ref.shape[0] // BLK)


def place_far_kernel(pre, hops, slot_ref, cache_in, *refs):
    got, chain, (cache_hbm, cache, sem) = refs[: pre - 2], refs[pre - 2 : -3], refs[-3:]
    blocks = cache_hbm.shape[0]
    cache[...] = cache_in[...]
    for distance in range(2, pre):
        n = distance - 2
        if distance <= hops:
            k_ref, v_ref = chain[2 * n], chain[2 * n + 1]
            place_forwarded(cache, slot_ref, k_ref, v_ref, distance, pre, blocks)
        place_packed(cache, slot_ref, got[n], distance, distance <= hops, pre, blocks)
    store = pltpu.make_async_copy(cache.at[0:blocks], cache_hbm, sem)
    store.start()
    store.wait()


def on_device(queries, new_keys, new_values, lengths, block_slot):
    rows, q_width = queries.shape
    kv_width = new_keys.shape[1]
    kv_count = kv_width // HD
    blocks = rows // BLK
    pre = lax.axis_size("pre")
    per_peer = blocks // pre
    hops = pre // 2
    tiles = rows // TILE
    bf16, f32 = jnp.bfloat16, jnp.float32
    shape = jax.ShapeDtypeStruct
    params = pltpu.CompilerParams(vmem_limit_bytes=24 * 2**20)
    own_params = pltpu.CompilerParams(vmem_limit_bytes=44 * 2**20)
    ring = [(i, (i + 1) % pre) for i in range(pre)]
    acc_shape = shape((kv_count, HD, GROUP * rows), f32)
    stat_shape = shape((kv_count, 8, GROUP * rows), f32)
    weights_shape = shape((tiles, kv_count, rows, GROUP * TILE), bf16)
    attended_shape = shape(queries.shape, bf16)
    cache_shape = shape((blocks, BLK, 2 * kv_width), bf16)
    open_cache = shape((blocks + 1, BLK, 2 * kv_width), bf16)
    turned = pltpu.VMEM((kv_count, HD + ONES, rows), bf16)
    bias = pltpu.VMEM((rows, TILE), f32)

    def cost(share, moved):
        pairs = int(rows * rows * share)
        return pl.CostEstimate(
            flops=4 * pairs * q_width,
            bytes_accessed=moved * 2**20,
            transcendentals=pairs * kv_count * GROUP,
        )

    def after(array, *others):
        return lax.optimization_barrier((array, *others))[0]

    k, v = lax.ppermute(new_keys, "pre", ring), lax.ppermute(new_values, "pre", ring)

    packed = shape((per_peer, BLK, 2 * kv_width), bf16)
    in_hbm = (
        pltpu.with_memory_space_constraint(x, pltpu.HBM) for x in (queries, new_keys, new_values)
    )
    q, acc, total, top, cache, *sent = pl.pallas_call(
        functools.partial(own_kernel, pre),
        out_shape=(attended_shape, acc_shape, stat_shape, stat_shape, open_cache)
        + (packed,) * (pre - 2),
        in_specs=[SMEM, SMEM] + [HBM] * 3,
        out_specs=(VMEM,) * 5 + (HBM,) * (pre - 2),
        scratch_shapes=[
            pltpu.VMEM((rows, kv_width), bf16),
            pltpu.VMEM((rows, kv_width), bf16),
            turned,
            bias,
            pltpu.VMEM(((pre - 2) * per_peer + 1, BLK, 2 * kv_width), bf16),
            pltpu.SMEM((pre,), jnp.int32),
            pltpu.SemaphoreType.DMA((pre - 2,)),
            pltpu.SemaphoreType.DMA((3,)),
        ],
        cost_estimate=cost(1, 4),
        compiler_params=own_params,
        name="own_attention",
    )(lengths, block_slot, *in_hbm)
    got = [
        lax.ppermute(sent[d - 2], "pre", [((i - d) % pre, i) for i in range(d - 1)])
        for d in range(2, hops + 1)
    ]

    k = after(k, top)
    chain = []
    attended = None
    for hop in range(1, hops + 1):
        first_out, last = hop == 1, hop == hops
        onward = [(i, i + 1) for i in range(hop - 1, pre - 1)]
        next_k = None if last else lax.ppermute(k, "pre", onward)
        weights, factor, *tops = pl.pallas_call(
            functools.partial(scores_kernel, hop),
            out_shape=(weights_shape, stat_shape) + (() if last else (stat_shape,)),
            in_specs=[SMEM] + [VMEM] * 3,
            out_specs=(VMEM,) * (2 if last else 3),
            scratch_shapes=[bias],
            cost_estimate=cost(0.5, 3),
            compiler_params=params,
            name="scores",
        )(lengths, q, k, top)
        v = after(v, factor)
        if last:
            for d in range(hops + 1, pre):
                pairs = [(i, (i + d) % pre) for i in range(pre)]
                got.append(lax.ppermute(after(sent[d - 2], factor), "pre", pairs))
        chain += [k, v]
        next_v = None if last else lax.ppermute(v, "pre", onward)
        attended, *state = pl.pallas_call(
            functools.partial(values_kernel, hop, first_out, last),
            out_shape=(attended_shape,) + (() if last else (acc_shape, stat_shape)),
            in_specs=[SMEM] + [VMEM] * 5 + ([] if first_out else [HBM]),
            out_specs=(HBM,) + (() if last else (VMEM, VMEM)),
            scratch_shapes=[
                turned,
                pltpu.VMEM((rows, q_width), bf16),
                pltpu.SemaphoreType.DMA((tiles,)),
            ],
            input_output_aliases={} if first_out else {6: 0},
            cost_estimate=cost(0.5, 3),
            compiler_params=params,
            name="values",
        )(lengths, v, weights, factor, acc, total, *([] if first_out else [attended]))
        if first_out:
            cache = pl.pallas_call(
                functools.partial(place_near_kernel, pre),
                out_shape=open_cache,
                in_specs=[SMEM] + [VMEM] * 3,
                out_specs=VMEM,
                cost_estimate=cost(0, 2),
                compiler_params=params,
                name="place_near",
            )(block_slot, cache, *chain)
        if not last:
            (top,) = tops
            acc, total = state
            k, v = after(next_k, total), next_v

    rest = got + chain[2:]
    cache = pl.pallas_call(
        functools.partial(place_far_kernel, pre, hops),
        out_shape=cache_shape,
        in_specs=[SMEM] + [VMEM] * (1 + len(rest)),
        out_specs=HBM,
        scratch_shapes=[pltpu.VMEM(open_cache.shape, bf16), pltpu.SemaphoreType.DMA],
        cost_estimate=cost(0, 2),
        compiler_params=params,
        name="place_far",
    )(block_slot, cache, *rest)
    return (attended, cache)


def solution(mesh):
    placed = (
        P(("parts", "pre"), "tp"),
        P(("parts", "pre"), "tp"),
        P(("parts", "pre"), "tp"),
        P("parts"),
        P("parts"),
    )
    return jax.shard_map(
        on_device,
        mesh=mesh,
        in_specs=placed,
        out_specs=(P(("parts", "pre"), "tp"), P(("parts", "pre"), None, "tp")),
        check_vma=False,
    )
```

profile of v0, /device:TPU:0, one launch (start us, length us, event | category | flops | bytes accessed | tf_op | source)
XLA Modules:
  0.0 33.2 jit_solution(8014202229479487553)
XLA Ops:
  0.6 3.1 %collective-permute-start.1 = (bf16[512,256]{1,0:T(8,128)(2,1)}, bf16[512,256]{1,0:T(8,128)(2,1)S(1)}, u32[]{:S(2)}, u32[]{:S(2)}) collective-permute-start(bf16[512,256]{1,0:T(8,128)(2,1)} %k_hbm.1), channel_id=1, source_target_pairs={{0,4},{4,8},{8,12},{12,0},{1,5},{5,9},{9,13},{13,1},{2,6},{6,10},{... | collective-permute-start | bytes 786440 | tf_op jit(solution)/shard_map/ppermute | solution.py:365
  3.7 1.6 %collective-permute-start = (bf16[512,256]{1,0:T(8,128)(2,1)}, bf16[512,256]{1,0:T(8,128)(2,1)S(1)}, u32[]{:S(2)}, u32[]{:S(2)}) collective-permute-start(bf16[512,256]{1,0:T(8,128)(2,1)} %v_hbm.1), channel_id=1, source_target_pairs={{0,4},{4,8},{8,12},{12,0},{1,5},{5,9},{9,13},{13,1},{2,6},{6,10},{... | collective-permute-start | bytes 786440 | tf_op jit(solution)/shard_map/ppermute | solution.py:365
  5.3 0.0 copy-start
  5.3 0.7 %copy-done = s32[4]{0:T(128)S(1)} copy-done((s32[4]{0:T(128)S(1)}, s32[4]{0:T(128)}, u32[]{:S(2)}) %copy-start) | copy-done | bytes 40
  5.9 0.0 copy-start.1
  5.9 0.7 %copy-done.1 = s32[128]{0:T(128)S(1)} copy-done((s32[128]{0:T(128)S(1)}, s32[128]{0:T(128)}, u32[]{:S(2)}) %copy-start.1) | copy-done | bytes 536
  6.6 5.3 %own_attention.1 = (bf16[512,1024]{1,0:T(8,128)(2,1)S(1)}, f32[2,128,2048]{2,1,0:T(8,128)S(1)}, f32[2,8,2048]{2,1,0:T(8,128)S(1)}, f32[2,8,2048]{2,1,0:T(8,128)S...) custom-call(s32[4]{0:T(128)S(1)} %copy-done, ...), custom_call_target="tpu_custom_call" | custom-call | flops 1073741824 | bytes 4194304 | tf_op jit(solution)/shard_map/own_attention/pallas_call | solution.py:371
  11.9 1.2 %collective-permute-done.1.k_ref = bf16[512,256]{1,0:T(8,128)(2,1)S(1)} collective-permute-done((bf16[512,256]{1,0:T(8,128)(2,1)}, bf16[512,256]{1,0:T(8,128)(2,1)S(1)}, u32[]{:S(2)}, u32[]{:S(2)}) %collective-permute-start.1) | collective-permute-done | bytes 262176 | tf_op jit(solution)/shard_map/ppermute | solution.py:365
  13.1 2.3 %collective-permute-start.3 = (bf16[512,256]{1,0:T(8,128)(2,1)S(1)}, bf16[512,256]{1,0:T(8,128)(2,1)S(1)}, u32[]{:S(2)}, u32[]{:S(2)}) collective-permute-start(bf16[512,256]{1,0:T(8,128)(2,1)S(1)} %collective-permute-done.1.k_ref), channel_id=1, source_target_pairs={{0,4},{4,8},{8,12},{1,5},{5,9},{9,13},{2,6},{6,10},{10,14},{3,7},{... | collective-permute-start | bytes 786440 | tf_op jit(solution)/shard_map/ppermute | solution.py:402
  15.4 0.6 %scores.2 = (bf16[2,2,512,1024]{3,2,1,0:T(8,128)(2,1)S(1)}, f32[2,8,2048]{2,1,0:T(8,128)S(1)}, f32[2,8,2048]{2,1,0:T(8,128)S(1)}) custom-call(s32[4]{0:T(128)S(1)} %copy-done, bf16[512,1024]{1,0:T(8,128)(2,1)S(1)} %get-tuple-element.22.q_ref, bf16[512,256]{1,0:T(8,128)(2,1)S(1)} %collective-permute-done.1.k_ref, f32[2,8,2048]{2,1,0:T(8,128)S(1)} %get-tuple-element.23.old_top), custom_call_target="tpu_custom_call" | custom-call | flops 536870912 | bytes 3145728 | tf_op jit(solution)/shard_map/scores/pallas_call | solution.py:403
  16.0 1.9 %collective-permute-done.v_ref = bf16[512,256]{1,0:T(8,128)(2,1)S(1)} collective-permute-done((bf16[512,256]{1,0:T(8,128)(2,1)}, bf16[512,256]{1,0:T(8,128)(2,1)S(1)}, u32[]{:S(2)}, u32[]{:S(2)}) %collective-permute-start) | collective-permute-done | bytes 262176 | tf_op jit(solution)/shard_map/ppermute | solution.py:365
  17.9 2.8 %collective-permute-start.2 = (bf16[512,256]{1,0:T(8,128)(2,1)S(1)}, bf16[512,256]{1,0:T(8,128)(2,1)S(1)}, u32[]{:S(2)}, u32[]{:S(2)}) collective-permute-start(bf16[512,256]{1,0:T(8,128)(2,1)S(1)} %collective-permute-done.v_ref), channel_id=1, source_target_pairs={{0,4},{4,8},{8,12},{1,5},{5,9},{9,13},{2,6},{6,10},{10,14},{3,7},{... | collective-permute-start | bytes 786440 | tf_op jit(solution)/shard_map/ppermute | solution.py:419
  20.7 1.3 %collective-permute-start.4 = (bf16[8,16,512]{2,1,0:T(8,128)(2,1)S(1)}, bf16[8,16,512]{2,1,0:T(8,128)(2,1)S(1)}, u32[]{:S(2)}, u32[]{:S(2)}) collective-permute-start(bf16[8,16,512]{2,1,0:T(8,128)(2,1)S(1)} %get-tuple-element.39), channel_id=1, source_target_pairs={{8,0},{9,1},{10,2},{11,3},{24,16},{25,17},{26,18},{27,19}} | collective-permute-start | bytes 393224 | tf_op jit(solution)/shard_map/ppermute | solution.py:392
  22.0 1.8 %values.2 = (bf16[512,1024]{1,0:T(8,128)(2,1)}, f32[2,128,2048]{2,1,0:T(8,128)S(1)}, f32[2,8,2048]{2,1,0:T(8,128)S(1)}) custom-call(s32[4]{0:T(128)S(1)} %copy-done, bf16[512,256]{1,0:T(8,128)(2,1)S(1)} %collective-permute-done.v_ref, bf16[2,2,512,1024]{3,2,1,0:T(8,128)(2,1)S(1)} %get-tuple-element.27.weights_ref, ...), custom_call_target="tpu_custom_call" | custom-call | flops 536870912 | bytes 3145728 | tf_op jit(solution)/shard_map/values/pallas_call | solution.py:420
  23.9 0.0 collective-permute-done.3.k_ref.refs_2_
  23.9 0.8 %scores.3 = (bf16[2,2,512,1024]{3,2,1,0:T(8,128)(2,1)S(1)}, f32[2,8,2048]{2,1,0:T(8,128)S(1)}) custom-call(s32[4]{0:T(128)S(1)} %copy-done, bf16[512,1024]{1,0:T(8,128)(2,1)S(1)} %get-tuple-element.22.q_ref, bf16[512,256]{1,0:T(8,128)(2,1)S(1)} %collective-permute-done.3.k_ref.refs_2_, f32[2,8,2048]{2,1,0:T(8,128)S(1)} %get-tuple-element.32.old_top), custom_call_target="tpu_custom_call" | custom-call | flops 536870912 | bytes 3145728 | tf_op jit(solution)/shard_map/scores/pallas_call | solution.py:403
  24.6 4.1 %collective-permute-start.5 = (bf16[8,16,512]{2,1,0:T(8,128)(2,1)S(1)}, bf16[8,16,512]{2,1,0:T(8,128)(2,1)S(1)}, u32[]{:S(2)}, u32[]{:S(2)}) collective-permute-start(bf16[8,16,512]{2,1,0:T(8,128)(2,1)S(1)} %get-tuple-element.41), channel_id=1, source_target_pairs={{0,12},{4,0},{8,4},{12,8},{1,13},{5,1},{9,5},{13,9},{2,14},{6,2},{... | collective-permute-start | bytes 393224 | tf_op jit(solution)/shard_map/ppermute | solution.py:417
  28.8 0.8 %place_near.1.cache_in = bf16[33,16,512]{2,1,0:T(8,128)(2,1)S(1)} custom-call(s32[128]{0:T(128)S(1)} %copy-done.1, bf16[33,16,512]{2,1,0:T(8,128)(2,1)S(1)} %get-tuple-element.38.cache_in, bf16[512,256]{1,0:T(8,128)(2,1)S(1)} %collective-permute-done.1.k_ref, bf16[512,256]{1,0:T(8,128)(2,1)S(1)} %collective-permute-done.v_ref), custom_call_target="tpu_custom_call" | custom-call | bytes 2097152 | tf_op jit(solution)/shard_map/place_near/pallas_call | solution.py:436
  29.5 0.0 collective-permute-done.2.v_ref.refs_3_
  29.6 0.6 %values.3 = bf16[512,1024]{1,0:T(8,128)(2,1)} custom-call(s32[4]{0:T(128)S(1)} %copy-done, bf16[512,256]{1,0:T(8,128)(2,1)S(1)} %collective-permute-done.2.v_ref.refs_3_, bf16[2,2,512,1024]{3,2,1,0:T(8,128)(2,1)S(1)} %get-tuple-element.35.weights_ref, f32[2,8,2048]{2,1,0:T(8,128)S(1)} %get-tuple-element.33.factor_ref, ...), custom_call_target="tpu_custom_call", output_to_operand_aliasing={{}: (6, {})} | custom-call | flops 536870912 | bytes 3145728 | tf_op jit(solution)/shard_map/values/pallas_call | solution.py:420
  30.2 0.0 collective-permute-done.4.refs_0_
  30.2 1.1 %collective-permute-done.5.refs_1_ = bf16[8,16,512]{2,1,0:T(8,128)(2,1)S(1)} collective-permute-done((bf16[8,16,512]{2,1,0:T(8,128)(2,1)S(1)}, bf16[8,16,512]{2,1,0:T(8,128)(2,1)S(1)}, u32[]{:S(2)}, u32[]{:S(2)}) %collective-permute-start.5) | collective-permute-done | bytes 131104 | tf_op jit(solution)/shard_map/ppermute | solution.py:417
  31.3 1.8 %place_far.1 = bf16[32,16,512]{2,1,0:T(8,128)(2,1)} custom-call(s32[128]{0:T(128)S(1)} %copy-done.1, bf16[33,16,512]{2,1,0:T(8,128)(2,1)S(1)} %place_near.1.cache_in, bf16[8,16,512]{2,1,0:T(8,128)(2,1)S(1)} %collective-permute-done.4.refs_0_, bf16[8,16,512]{2,1,0:T(8,128)(2,1)S(1)} %collective-permute-done.5.refs_1_, ...), custom_call_target="tpu_custom_call" | custom-call | bytes 2097152 | tf_op jit(solution)/shard_map/place_far/pallas_call | solution.py:451
Async XLA Ops:
  0.6 12.4 %collective-permute-start.1 = (bf16[512,256]{1,0:T(8,128)(2,1)}, bf16[512,256]{1,0:T(8,128)(2,1)S(1)}, u32[]{:S(2)}, u32[]{:S(2)}) collective-permute-start(bf16[512,256]{1,0:T(8,128)(2,1)} %k_hbm.1), channel_id=1, source_target_pairs={{0,4},{4,8},{8,12},{12,0},{1,5},{5,9},{9,13},{13,1},{2,6},{6,10},{... | collective-permute-start | bytes 786440 | tf_op jit(solution)/shard_map/ppermute | solution.py:365
  3.7 14.2 %collective-permute-start = (bf16[512,256]{1,0:T(8,128)(2,1)}, bf16[512,256]{1,0:T(8,128)(2,1)S(1)}, u32[]{:S(2)}, u32[]{:S(2)}) collective-permute-start(bf16[512,256]{1,0:T(8,128)(2,1)} %v_hbm.1), channel_id=1, source_target_pairs={{0,4},{4,8},{8,12},{12,0},{1,5},{5,9},{9,13},{13,1},{2,6},{6,10},{... | collective-permute-start | bytes 786440 | tf_op jit(solution)/shard_map/ppermute | solution.py:365
  5.3 0.7 %copy-start = (s32[4]{0:T(128)S(1)}, s32[4]{0:T(128)}, u32[]{:S(2)}) copy-start(s32[4]{0:T(128)} %lengths_ref.9) | copy-start | bytes 52
  5.9 0.7 %copy-start.1 = (s32[128]{0:T(128)S(1)}, s32[128]{0:T(128)}, u32[]{:S(2)}) copy-start(s32[128]{0:T(128)} %slot_ref.5) | copy-start | bytes 1540
  13.1 10.8 %collective-permute-start.3 = (bf16[512,256]{1,0:T(8,128)(2,1)S(1)}, bf16[512,256]{1,0:T(8,128)(2,1)S(1)}, u32[]{:S(2)}, u32[]{:S(2)}) collective-permute-start(bf16[512,256]{1,0:T(8,128)(2,1)S(1)} %collective-permute-done.1.k_ref), channel_id=1, source_target_pairs={{0,4},{4,8},{8,12},{1,5},{5,9},{9,13},{2,6},{6,10},{10,14},{3,7},{... | collective-permute-start | bytes 786440 | tf_op jit(solution)/shard_map/ppermute | solution.py:402
  17.9 11.7 %collective-permute-start.2 = (bf16[512,256]{1,0:T(8,128)(2,1)S(1)}, bf16[512,256]{1,0:T(8,128)(2,1)S(1)}, u32[]{:S(2)}, u32[]{:S(2)}) collective-permute-start(bf16[512,256]{1,0:T(8,128)(2,1)S(1)} %collective-permute-done.v_ref), channel_id=1, source_target_pairs={{0,4},{4,8},{8,12},{1,5},{5,9},{9,13},{2,6},{6,10},{10,14},{3,7},{... | collective-permute-start | bytes 786440 | tf_op jit(solution)/shard_map/ppermute | solution.py:419
  20.7 9.5 %collective-permute-start.4 = (bf16[8,16,512]{2,1,0:T(8,128)(2,1)S(1)}, bf16[8,16,512]{2,1,0:T(8,128)(2,1)S(1)}, u32[]{:S(2)}, u32[]{:S(2)}) collective-permute-start(bf16[8,16,512]{2,1,0:T(8,128)(2,1)S(1)} %get-tuple-element.39), channel_id=1, source_target_pairs={{8,0},{9,1},{10,2},{11,3},{24,16},{25,17},{26,18},{27,19}} | collective-permute-start | bytes 393224 | tf_op jit(solution)/shard_map/ppermute | solution.py:392
  24.6 6.7 %collective-permute-start.5 = (bf16[8,16,512]{2,1,0:T(8,128)(2,1)S(1)}, bf16[8,16,512]{2,1,0:T(8,128)(2,1)S(1)}, u32[]{:S(2)}, u32[]{:S(2)}) collective-permute-start(bf16[8,16,512]{2,1,0:T(8,128)(2,1)S(1)} %get-tuple-element.41), channel_id=1, source_target_pairs={{0,12},{4,0},{8,4},{12,8},{1,13},{5,1},{9,5},{13,9},{2,14},{6,2},{... | collective-permute-start | bytes 393224 | tf_op jit(solution)/shard_map/ppermute | solution.py:417
where the time goes:
time: 33.6 us; the launch traced here: 33.2 us
  starting transfers between devices  15.3 us (46%)
  Pallas kernels  11.6 us (35%)
  waiting for transfers between devices  4.16 us (12%)
  local copies, waits for them, and re-layouts  1.31 us (4%)
  between operations  0.89 us (3%)
    pallas_call x1, Pallas kernels, on_device(): pl.pallas_call(functools.partial(own_kernel, pre), out_shape=(attended_sh...  5.3 us
    ppermute x1, starting transfers between devices, on_device(): got.append(lax.ppermute(after(sent[d - 2], factor), 'pre', pairs))  4.14 us
    ppermute x1, starting transfers between devices, on_device(): lax.ppermute(new_keys, 'pre', ring)  3.08 us
    ppermute x1, starting transfers between devices, on_device(): next_v = None if last else lax.ppermute(v, 'pre', onward)  2.84 us
    pallas_call x2, Pallas kernels, on_device(): pl.pallas_call(functools.partial(values_kernel, hop, first_out, last), ou...  2.44 us
    ppermute x1, starting transfers between devices, on_device(): next_k = None if last else lax.ppermute(k, 'pre', onward)  2.33 us
    ppermute x1, waiting for transfers between devices, on_device(): lax.ppermute(new_values, 'pre', ring)  1.85 us
    pallas_call x1, Pallas kernels, on_device(): pl.pallas_call(functools.partial(place_far_kernel, pre, hops), out_shape=...  1.76 us
  transfers between devices with their start and end apart: 6, of which 3 were waited for; matrix products, arithmetic and copies ran while one was open for 0% of the time, Pallas kernels for 30%

commit v1 on v0

--- a/solution.py
+++ b/solution.py
@@ -224,14 +224,82 @@
         where_seen(lowest_key(lengths_ref, hop, tile, rows), rows, act)
 
 
+def place_forwarded(cache, slot_ref, k_ref, v_ref, distance, pre, blocks):
+    me = lax.axis_index("pre")
+    source = lax.rem(me - distance + pre, pre)
+
+    def step(b, _):
+        at = own_slot(slot_ref[source * blocks + b], me, blocks)
+        cache[at] = block_of(k_ref, v_ref, pl.multiple_of(b * BLK, BLK))
+        return 0
+
+    def run():
+        lax.fori_loop(0, blocks, step, 0, unroll=8)
+
+    if distance < 2:
+        run()
+    else:
+        pl.when(me >= distance - 1)(run)
+
+
+def place_packed(cache, slot_ref, got_ref, distance, pre, blocks):
+    me = lax.axis_index("pre")
+    source = lax.rem(me - distance + pre, pre)
+    most = got_ref.shape[0] - 1
+
+    def step(b, n):
+        at = own_slot(slot_ref[source * blocks + b], me, blocks)
+        cache[at] = got_ref[jnp.minimum(n, most)]
+        return n + jnp.where(at < blocks, 1, 0)
+
+    @pl.when(me < distance - 1)
+    def _():
+        lax.fori_loop(0, blocks, step, jnp.int32(0), unroll=8)
+
+
+def list_places(places_ref, slot_ref, hops, pre, blocks):
+    me = lax.axis_index("pre")
+    per_peer = blocks // pre
+    for distance in range(hops + 1, pre):
+        source = lax.rem(me - distance + pre, pre)
+        base = (distance - hops - 1) * (per_peer + 1)
+
+        def step(b, n):
+            at = own_slot(slot_ref[source * blocks + b], me, blocks)
+            places_ref[base + n] = at
+            return n + jnp.where(at < blocks, 1, 0)
+
+        lax.fori_loop(0, blocks, step, jnp.int32(0), unroll=8)
+
+
 def values_kernel(
-    hop, first_out, last, lengths_ref, v_ref, weights_ref, factor_ref, acc_in, sum_in, *refs
+    hop, hops, pre, lengths_ref, slot_ref, v_ref, k_ref, weights_ref, factor_ref,
+    acc_in, sum_in, cache_in, *refs,
 ):
-    refs = refs if first_out else refs[1:]
-    out_hbm, *state, turned, out_buf, sems = refs
+    first_out, last = hop == 1, hop == hops
+    refs = list(refs)
+    if not first_out:
+        got_ref, _ = refs.pop(0), refs.pop(0)
+    out_hbm, cache_out = refs.pop(0), refs.pop(0)
+    state = () if last else (refs.pop(0), refs.pop(0))
+    places_ref = refs.pop(0) if first_out else None
+    turned, out_buf, sems, *rest = refs
     rows = v_ref.shape[0]
+    blocks = rows // BLK
     tiles = rows // TILE
     kv_count = turned.shape[0]
+
+    cache = rest[0] if last else cache_out
+    cache[...] = cache_in[...]
+    place_forwarded(cache, slot_ref, k_ref, v_ref, hop, pre, blocks)
+    if first_out:
+        list_places(places_ref, slot_ref, hops, pre, blocks)
+    else:
+        place_packed(cache, slot_ref, got_ref, hop, pre, blocks)
+    if last:
+        cache_store = pltpu.make_async_copy(cache.at[0:blocks], cache_out, sems.at[tiles])
+        cache_store.start()
+
     lows = [lowest_key(lengths_ref, hop, tile, rows) for tile in range(tiles)]
     pl.when(lows[0] < rows)(functools.partial(turn_values, v_ref, turned))
     stores = []
@@ -269,63 +337,24 @@
             store.wait()
         else:
             pl.when(low < rows)(store.wait)
-
-
-def place_forwarded(cache, slot_ref, k_ref, v_ref, distance, pre, blocks):
-    me = lax.axis_index("pre")
-    source = lax.rem(me - distance + pre, pre)
-
-    def step(b, _):
-        at = own_slot(slot_ref[source * blocks + b], me, blocks)
-        cache[at] = block_of(k_ref, v_ref, pl.multiple_of(b * BLK, BLK))
-        return 0
-
-    def run():
-        lax.fori_loop(0, blocks, step, 0, unroll=8)
-
-    if distance < 2:
-        run()
-    else:
-        pl.when(me >= distance - 1)(run)
-
-
-def place_packed(cache, slot_ref, got_ref, distance, forwarded, pre, blocks):
-    me = lax.axis_index("pre")
-    source = lax.rem(me - distance + pre, pre)
-    most = got_ref.shape[0] - 1
-
-    def step(b, n):
-        at = own_slot(slot_ref[source * blocks + b], me, blocks)
-        cache[at] = got_ref[jnp.minimum(n, most)]
-        return n + jnp.where(at < blocks, 1, 0)
-
-    def run():
-        lax.fori_loop(0, blocks, step, jnp.int32(0), unroll=8)
-
-    if forwarded:
-        pl.when(me < distance - 1)(run)
-    else:
-        run()
-
-
-def place_near_kernel(pre, slot_ref, cache_in, k_ref, v_ref, cache_ref):
-    cache_ref[...] = cache_in[...]
-    place_forwarded(cache_ref, slot_ref, k_ref, v_ref, 1, pre, k_ref.shape[0] // BLK)
-
-
-def place_far_kernel(pre, hops, slot_ref, cache_in, *refs):
-    got, chain, (cache_hbm, cache, sem) = refs[: pre - 2], refs[pre - 2 : -3], refs[-3:]
-    blocks = cache_hbm.shape[0]
-    cache[...] = cache_in[...]
-    for distance in range(2, pre):
-        n = distance - 2
-        if distance <= hops:
-            k_ref, v_ref = chain[2 * n], chain[2 * n + 1]
-            place_forwarded(cache, slot_ref, k_ref, v_ref, distance, pre, blocks)
-        place_packed(cache, slot_ref, got[n], distance, distance <= hops, pre, blocks)
-    store = pltpu.make_async_copy(cache.at[0:blocks], cache_hbm, sem)
-    store.start()
-    store.wait()
+    if last:
+        cache_store.wait()
+
+
+def place_last_kernel(places_ref, cache_in, *refs):
+    *got, cache_hbm, sems = refs
+    per_peer = got[0].shape[0]
+    copies = []
+    for i, got_ref in enumerate(got):
+        for n in range(per_peer):
+            at = places_ref[i * (per_peer + 1) + n]
+            copy = pltpu.make_async_copy(
+                got_ref.at[n], cache_hbm.at[at], sems.at[i * per_peer + n]
+            )
+            copy.start()
+            copies.append(copy)
+    for copy in copies:
+        copy.wait()
 
 
 def on_device(queries, new_keys, new_values, lengths, block_slot):
@@ -394,7 +423,6 @@
     ]
 
     k = after(k, top)
-    chain = []
     attended = None
     for hop in range(1, hops + 1):
         first_out, last = hop == 1, hop == hops
@@ -415,49 +443,48 @@
             for d in range(hops + 1, pre):
                 pairs = [(i, (i + d) % pre) for i in range(pre)]
                 got.append(lax.ppermute(after(sent[d - 2], factor), "pre", pairs))
-        chain += [k, v]
         next_v = None if last else lax.ppermute(v, "pre", onward)
-        attended, *state = pl.pallas_call(
-            functools.partial(values_kernel, hop, first_out, last),
-            out_shape=(attended_shape,) + (() if last else (acc_shape, stat_shape)),
-            in_specs=[SMEM] + [VMEM] * 5 + ([] if first_out else [HBM]),
-            out_specs=(HBM,) + (() if last else (VMEM, VMEM)),
+        places = shape(((pre - 1 - hops) * (per_peer + 1),), jnp.int32)
+        carry = () if last else (acc_shape, stat_shape)
+        extra = [] if first_out else [got[hop - 2], attended]
+        attended, cache, *state = pl.pallas_call(
+            functools.partial(values_kernel, hop, hops, pre),
+            out_shape=(attended_shape, cache_shape if last else open_cache)
+            + carry
+            + ((places,) if first_out else ()),
+            in_specs=[SMEM, SMEM] + [VMEM] * 7 + ([] if first_out else [VMEM, HBM]),
+            out_specs=(HBM, HBM if last else VMEM)
+            + (VMEM,) * len(carry)
+            + ((SMEM,) if first_out else ()),
             scratch_shapes=[
                 turned,
                 pltpu.VMEM((rows, q_width), bf16),
-                pltpu.SemaphoreType.DMA((tiles,)),
-            ],
-            input_output_aliases={} if first_out else {6: 0},
+                pltpu.SemaphoreType.DMA((tiles + 1,)),
+            ]
+            + ([pltpu.VMEM(open_cache.shape, bf16)] if last else []),
+            input_output_aliases={} if first_out else {10: 0},
             cost_estimate=cost(0.5, 3),
             compiler_params=params,
             name="values",
-        )(lengths, v, weights, factor, acc, total, *([] if first_out else [attended]))
+        )(lengths, block_slot, v, k, weights, factor, acc, total, cache, *extra)
         if first_out:
-            cache = pl.pallas_call(
-                functools.partial(place_near_kernel, pre),
-                out_shape=open_cache,
-                in_specs=[SMEM] + [VMEM] * 3,
-                out_specs=VMEM,
-                cost_estimate=cost(0, 2),
-                compiler_params=params,
-                name="place_near",
-            )(block_slot, cache, *chain)
+            far_places = state.pop()
         if not last:
             (top,) = tops
             acc, total = state
             k, v = after(next_k, total), next_v
 
-    rest = got + chain[2:]
     cache = pl.pallas_call(
-        functools.partial(place_far_kernel, pre, hops),
+        place_last_kernel,
         out_shape=cache_shape,
-        in_specs=[SMEM] + [VMEM] * (1 + len(rest)),
+        in_specs=[SMEM, HBM] + [VMEM] * (pre - 1 - hops),
         out_specs=HBM,
-        scratch_shapes=[pltpu.VMEM(open_cache.shape, bf16), pltpu.SemaphoreType.DMA],
-        cost_estimate=cost(0, 2),
+        scratch_shapes=[pltpu.SemaphoreType.DMA(((pre - 1 - hops) * per_peer,))],
+        input_output_aliases={1: 0},
+        cost_estimate=cost(0, 1),
         compiler_params=params,
-        name="place_far",
-    )(block_slot, cache, *rest)
+        name="place_last",
+    )(far_places, cache, *got[hops - 1 :])
     return (attended, cache)
 
 

time: 33.6 us -> 33.1 us (0.985); the launches traced: 33.2 us -> 33.2 us
  starting transfers between devices: 15.3 us -> 14.4 us
  Pallas kernels: 11.6 us -> 12.3 us
    ppermute x1, starting transfers between devices: 4.14 us -> 2.12 us  [on_device(): got.append(lax.ppermute(after(sent[d - 2], factor), 'pre', pairs))]
    ppermute x1, starting transfers between devices: 2.84 us -> 4.01 us  [on_device(): next_v = None if last else lax.ppermute(v, 'pre', onward)]
    ppermute x1, waiting for transfers between devices: 0.01 us -> 1.06 us  [on_device(): lax.ppermute(sent[d - 2], 'pre', [((i - d) % pre, i) for i in range(d - 1)])]
    ppermute x1, waiting for transfers between devices: 1.12 us -> 0.24 us  [on_device(): got.append(lax.ppermute(after(sent[d - 2], factor), 'pre', pairs))]
    pallas_call x4 -> x3, Pallas kernels: 4.95 us -> 5.63 us  [the longest x2 4.37 us: on_device(): pl.pallas_call(functools.partial(values_kernel, hop, hops, pre), out_shap...]
  transfers between devices with their start and end apart: 6 -> 6, of which waited for: 3 -> 4; matrix products, arithmetic and copies ran while one was open for 0% -> 0% of each run, Pallas kernels for 30% -> 33%
where the time goes in v1:
time: 33.1 us; the launch traced here: 33.2 us
  starting transfers between devices  14.4 us (44%)
  Pallas kernels  12.3 us (37%)
  waiting for transfers between devices  4.33 us (13%)
  local copies, waits for them, and re-layouts  1.31 us (4%)
  between operations  0.87 us (3%)
    pallas_call x1, Pallas kernels, on_device(): pl.pallas_call(functools.partial(own_kernel, pre), out_shape=(attended_sh...  5.3 us
    pallas_call x2, Pallas kernels, on_device(): pl.pallas_call(functools.partial(values_kernel, hop, hops, pre), out_shap...  4.37 us
    ppermute x1, starting transfers between devices, on_device(): next_v = None if last else lax.ppermute(v, 'pre', onward)  4.01 us
    ppermute x1, starting transfers between devices, on_device(): lax.ppermute(new_keys, 'pre', ring)  3.08 us
    ppermute x1, starting transfers between devices, on_device(): next_k = None if last else lax.ppermute(k, 'pre', onward)  2.33 us
    ppermute x1, starting transfers between devices, on_device(): got.append(lax.ppermute(after(sent[d - 2], factor), 'pre', pairs))  2.12 us
    ppermute x1, waiting for transfers between devices, on_device(): lax.ppermute(new_values, 'pre', ring)  1.85 us
    ppermute x1, starting transfers between devices, on_device(): lax.ppermute(new_values, 'pre', ring)  1.58 us
  transfers between devices with their start and end apart: 6, of which 4 were waited for; matrix products, arithmetic and copies ran while one was open for 0% of the time, Pallas kernels for 33%

profile of v1, /device:TPU:0, one launch (start us, length us, event | category | flops | bytes accessed | tf_op | source)
XLA Modules:
  0.0 33.2 jit_solution(4417805078749615824)
XLA Ops:
  0.6 3.1 %collective-permute-start.1 = (bf16[512,256]{1,0:T(8,128)(2,1)}, bf16[512,256]{1,0:T(8,128)(2,1)S(1)}, u32[]{:S(2)}, u32[]{:S(2)}) collective-permute-start(bf16[512,256]{1,0:T(8,128)(2,1)} %k_hbm.1), channel_id=1, source_target_pairs={{0,4},{4,8},{8,12},{12,0},{1,5},{5,9},{9,13},{13,1},{2,6},{6,10},{... | collective-permute-start | bytes 786440 | tf_op jit(solution)/shard_map/ppermute | solution.py:394
  3.7 1.6 %collective-permute-start = (bf16[512,256]{1,0:T(8,128)(2,1)}, bf16[512,256]{1,0:T(8,128)(2,1)S(1)}, u32[]{:S(2)}, u32[]{:S(2)}) collective-permute-start(bf16[512,256]{1,0:T(8,128)(2,1)} %v_hbm.1), channel_id=1, source_target_pairs={{0,4},{4,8},{8,12},{12,0},{1,5},{5,9},{9,13},{13,1},{2,6},{6,10},{... | collective-permute-start | bytes 786440 | tf_op jit(solution)/shard_map/ppermute | solution.py:394
  5.3 0.0 copy-start
  5.3 0.7 %copy-done = s32[4]{0:T(128)S(1)} copy-done((s32[4]{0:T(128)S(1)}, s32[4]{0:T(128)}, u32[]{:S(2)}) %copy-start) | copy-done | bytes 40
  5.9 0.0 copy-start.1
  5.9 0.7 %copy-done.1 = s32[128]{0:T(128)S(1)} copy-done((s32[128]{0:T(128)S(1)}, s32[128]{0:T(128)}, u32[]{:S(2)}) %copy-start.1) | copy-done | bytes 536
  6.6 5.3 %own_attention.1 = (bf16[512,1024]{1,0:T(8,128)(2,1)S(1)}, f32[2,128,2048]{2,1,0:T(8,128)S(1)}, f32[2,8,2048]{2,1,0:T(8,128)S(1)}, f32[2,8,2048]{2,1,0:T(8,128)S...) custom-call(s32[4]{0:T(128)S(1)} %copy-done, ...), custom_call_target="tpu_custom_call" | custom-call | flops 1073741824 | bytes 4194304 | tf_op jit(solution)/shard_map/own_attention/pallas_call | solution.py:400
  11.9 1.2 %collective-permute-done.1.k_ref = bf16[512,256]{1,0:T(8,128)(2,1)S(1)} collective-permute-done((bf16[512,256]{1,0:T(8,128)(2,1)}, bf16[512,256]{1,0:T(8,128)(2,1)S(1)}, u32[]{:S(2)}, u32[]{:S(2)}) %collective-permute-start.1) | collective-permute-done | bytes 262176 | tf_op jit(solution)/shard_map/ppermute | solution.py:394
  13.1 2.3 %collective-permute-start.3 = (bf16[512,256]{1,0:T(8,128)(2,1)S(1)}, bf16[512,256]{1,0:T(8,128)(2,1)S(1)}, u32[]{:S(2)}, u32[]{:S(2)}) collective-permute-start(bf16[512,256]{1,0:T(8,128)(2,1)S(1)} %collective-permute-done.1.k_ref), channel_id=1, source_target_pairs={{0,4},{4,8},{8,12},{1,5},{5,9},{9,13},{2,6},{6,10},{10,14},{3,7},{... | collective-permute-start | bytes 786440 | tf_op jit(solution)/shard_map/ppermute | solution.py:430
  15.4 0.6 %scores.2 = (bf16[2,2,512,1024]{3,2,1,0:T(8,128)(2,1)S(1)}, f32[2,8,2048]{2,1,0:T(8,128)S(1)}, f32[2,8,2048]{2,1,0:T(8,128)S(1)}) custom-call(s32[4]{0:T(128)S(1)} %copy-done, bf16[512,1024]{1,0:T(8,128)(2,1)S(1)} %get-tuple-element.26.q_ref, bf16[512,256]{1,0:T(8,128)(2,1)S(1)} %collective-permute-done.1.k_ref, f32[2,8,2048]{2,1,0:T(8,128)S(1)} %get-tuple-element.27.old_top), custom_call_target="tpu_custom_call" | custom-call | flops 536870912 | bytes 3145728 | tf_op jit(solution)/shard_map/scores/pallas_call | solution.py:431
  16.0 1.9 %collective-permute-done.v_ref = bf16[512,256]{1,0:T(8,128)(2,1)S(1)} collective-permute-done((bf16[512,256]{1,0:T(8,128)(2,1)}, bf16[512,256]{1,0:T(8,128)(2,1)S(1)}, u32[]{:S(2)}, u32[]{:S(2)}) %collective-permute-start) | collective-permute-done | bytes 262176 | tf_op jit(solution)/shard_map/ppermute | solution.py:394
  17.9 4.0 %collective-permute-start.2 = (bf16[512,256]{1,0:T(8,128)(2,1)S(1)}, bf16[512,256]{1,0:T(8,128)(2,1)S(1)}, u32[]{:S(2)}, u32[]{:S(2)}) collective-permute-start(bf16[512,256]{1,0:T(8,128)(2,1)S(1)} %collective-permute-done.v_ref), channel_id=1, source_target_pairs={{0,4},{4,8},{8,12},{1,5},{5,9},{9,13},{2,6},{6,10},{10,14},{3,7},{... | collective-permute-start | bytes 786440 | tf_op jit(solution)/shard_map/ppermute | solution.py:446
  21.9 1.3 %collective-permute-start.4 = (bf16[8,16,512]{2,1,0:T(8,128)(2,1)S(1)}, bf16[8,16,512]{2,1,0:T(8,128)(2,1)S(1)}, u32[]{:S(2)}, u32[]{:S(2)}) collective-permute-start(bf16[8,16,512]{2,1,0:T(8,128)(2,1)S(1)} %get-tuple-element.43), channel_id=1, source_target_pairs={{8,0},{9,1},{10,2},{11,3},{24,16},{25,17},{26,18},{27,19}} | collective-permute-start | bytes 393224 | tf_op jit(solution)/shard_map/ppermute | solution.py:421
  23.2 2.8 %values.2 = (bf16[512,1024]{1,0:T(8,128)(2,1)}, bf16[33,16,512]{2,1,0:T(8,128)(2,1)S(1)}, f32[2,128,2048]{2,1,0:T(8,128)S(1)}, f32[2,8,2048]{2,1,0:T(8,128)S(1)}, s32[9]{0:T(128)S(1)}) custom-call(s32[4]{0:T(128)S(1)} %copy-done, s32[128]{0:T(128)S(1)} %copy-done.1, bf16[512,256]{1,0:T(8,128)(2,1)S(1)} %collective-permute-done.v_ref, ...), custom_call_target="tpu_custom_call" | custom-call | flops 536870912 | bytes 3145728 | tf_op jit(solution)/shard_map/values/pallas_call | solution.py:450
  26.0 0.0 collective-permute-done.3.k_ref
  26.0 0.8 %scores.3 = (bf16[2,2,512,1024]{3,2,1,0:T(8,128)(2,1)S(1)}, f32[2,8,2048]{2,1,0:T(8,128)S(1)}) custom-call(s32[4]{0:T(128)S(1)} %copy-done, bf16[512,1024]{1,0:T(8,128)(2,1)S(1)} %get-tuple-element.26.q_ref, bf16[512,256]{1,0:T(8,128)(2,1)S(1)} %collective-permute-done.3.k_ref, f32[2,8,2048]{2,1,0:T(8,128)S(1)} %get-tuple-element.37.old_top), custom_call_target="tpu_custom_call" | custom-call | flops 536870912 | bytes 3145728 | tf_op jit(solution)/shard_map/scores/pallas_call | solution.py:431
  26.8 2.1 %collective-permute-start.5 = (bf16[8,16,512]{2,1,0:T(8,128)(2,1)S(1)}, bf16[8,16,512]{2,1,0:T(8,128)(2,1)S(1)}, u32[]{:S(2)}, u32[]{:S(2)}) collective-permute-start(bf16[8,16,512]{2,1,0:T(8,128)(2,1)S(1)} %get-tuple-element.49), channel_id=1, source_target_pairs={{0,12},{4,0},{8,4},{12,8},{1,13},{5,1},{9,5},{13,9},{2,14},{6,2},{... | collective-permute-start | bytes 393224 | tf_op jit(solution)/shard_map/ppermute | solution.py:445
  28.9 0.0 collective-permute-done.2.v_ref
  28.9 1.1 %collective-permute-done.4.refs_0_ = bf16[8,16,512]{2,1,0:T(8,128)(2,1)S(1)} collective-permute-done((bf16[8,16,512]{2,1,0:T(8,128)(2,1)S(1)}, bf16[8,16,512]{2,1,0:T(8,128)(2,1)S(1)}, u32[]{:S(2)}, u32[]{:S(2)}) %collective-permute-start.4) | collective-permute-done | bytes 131104 | tf_op jit(solution)/shard_map/ppermute | solution.py:421
  29.9 1.6 %values.3 = (bf16[512,1024]{1,0:T(8,128)(2,1)}, bf16[32,16,512]{2,1,0:T(8,128)(2,1)}) custom-call(s32[4]{0:T(128)S(1)} %copy-done, s32[128]{0:T(128)S(1)} %copy-done.1, bf16[512,256]{1,0:T(8,128)(2,1)S(1)} %collective-permute-done.2.v_ref, bf16[512,256]{1,0:T(8,128)(2,1)S(1)} %collective-permute-done.3.k_ref, ...), custom_call_target="tpu_custom_call", output_to_operand_aliasing={{0}: (10, {})} | custom-call | flops 536870912 | bytes 3145728 | tf_op jit(solution)/shard_map/values/pallas_call | solution.py:450
  31.5 0.2 collective-permute-done.5.refs_0_
  31.8 1.3 %place_last.1 = bf16[32,16,512]{2,1,0:T(8,128)(2,1)} custom-call(s32[9]{0:T(128)S(1)} %get-tuple-element.46.places_ref, bf16[32,16,512]{2,1,0:T(8,128)(2,1)} %get-tuple-element.47.cache_in, bf16[8,16,512]{2,1,0:T(8,128)(2,1)S(1)} %collective-permute-done.5.refs_0_), custom_call_target="tpu_custom_call", output_to_operand_aliasing={{}: (1, {})} | custom-call | bytes 1048576 | tf_op jit(solution)/shard_map/place_last/pallas_call | solution.py:477
Async XLA Ops:
  0.6 12.4 %collective-permute-start.1 = (bf16[512,256]{1,0:T(8,128)(2,1)}, bf16[512,256]{1,0:T(8,128)(2,1)S(1)}, u32[]{:S(2)}, u32[]{:S(2)}) collective-permute-start(bf16[512,256]{1,0:T(8,128)(2,1)} %k_hbm.1), channel_id=1, source_target_pairs={{0,4},{4,8},{8,12},{12,0},{1,5},{5,9},{9,13},{13,1},{2,6},{6,10},{... | collective-permute-start | bytes 786440 | tf_op jit(solution)/shard_map/ppermute | solution.py:394
  3.7 14.2 %collective-permute-start = (bf16[512,256]{1,0:T(8,128)(2,1)}, bf16[512,256]{1,0:T(8,128)(2,1)S(1)}, u32[]{:S(2)}, u32[]{:S(2)}) collective-permute-start(bf16[512,256]{1,0:T(8,128)(2,1)} %v_hbm.1), channel_id=1, source_target_pairs={{0,4},{4,8},{8,12},{12,0},{1,5},{5,9},{9,13},{13,1},{2,6},{6,10},{... | collective-permute-start | bytes 786440 | tf_op jit(solution)/shard_map/ppermute | solution.py:394
  5.3 0.7 %copy-start = (s32[4]{0:T(128)S(1)}, s32[4]{0:T(128)}, u32[]{:S(2)}) copy-start(s32[4]{0:T(128)} %lengths_ref.9) | copy-start | bytes 52
  5.9 0.7 %copy-start.1 = (s32[128]{0:T(128)S(1)}, s32[128]{0:T(128)}, u32[]{:S(2)}) copy-start(s32[128]{0:T(128)} %slot_ref.5) | copy-start | bytes 1540
  13.1 12.9 %collective-permute-start.3 = (bf16[512,256]{1,0:T(8,128)(2,1)S(1)}, bf16[512,256]{1,0:T(8,128)(2,1)S(1)}, u32[]{:S(2)}, u32[]{:S(2)}) collective-permute-start(bf16[512,256]{1,0:T(8,128)(2,1)S(1)} %collective-permute-done.1.k_ref), channel_id=1, source_target_pairs={{0,4},{4,8},{8,12},{1,5},{5,9},{9,13},{2,6},{6,10},{10,14},{3,7},{... | collective-permute-start | bytes 786440 | tf_op jit(solution)/shard_map/ppermute | solution.py:430
  17.9 11.0 %collective-permute-start.2 = (bf16[512,256]{1,0:T(8,128)(2,1)S(1)}, bf16[512,256]{1,0:T(8,128)(2,1)S(1)}, u32[]{:S(2)}, u32[]{:S(2)}) collective-permute-start(bf16[512,256]{1,0:T(8,128)(2,1)S(1)} %collective-permute-done.v_ref), channel_id=1, source_target_pairs={{0,4},{4,8},{8,12},{1,5},{5,9},{9,13},{2,6},{6,10},{10,14},{3,7},{... | collective-permute-start | bytes 786440 | tf_op jit(solution)/shard_map/ppermute | solution.py:446
  21.9 8.1 %collective-permute-start.4 = (bf16[8,16,512]{2,1,0:T(8,128)(2,1)S(1)}, bf16[8,16,512]{2,1,0:T(8,128)(2,1)S(1)}, u32[]{:S(2)}, u32[]{:S(2)}) collective-permute-start(bf16[8,16,512]{2,1,0:T(8,128)(2,1)S(1)} %get-tuple-element.43), channel_id=1, source_target_pairs={{8,0},{9,1},{10,2},{11,3},{24,16},{25,17},{26,18},{27,19}} | collective-permute-start | bytes 393224 | tf_op jit(solution)/shard_map/ppermute | solution.py:421
  26.8 5.0 %collective-permute-start.5 = (bf16[8,16,512]{2,1,0:T(8,128)(2,1)S(1)}, bf16[8,16,512]{2,1,0:T(8,128)(2,1)S(1)}, u32[]{:S(2)}, u32[]{:S(2)}) collective-permute-start(bf16[8,16,512]{2,1,0:T(8,128)(2,1)S(1)} %get-tuple-element.49), channel_id=1, source_target_pairs={{0,12},{4,0},{8,4},{12,8},{1,13},{5,1},{9,5},{13,9},{2,14},{6,2},{... | collective-permute-start | bytes 393224 | tf_op jit(solution)/shard_map/ppermute | solution.py:445

commit v2 on v1

--- a/solution.py
+++ b/solution.py
@@ -131,7 +131,7 @@
 
 
 def own_kernel(
-    pre, lengths_ref, slot_ref, q_hbm, k_hbm, v_hbm,
+    pre, hops, lengths_ref, slot_ref, q_hbm, k_hbm, v_hbm,
     q_ref, acc_ref, sum_ref, top_ref, cache_ref, *refs,
 ):
     sent_hbm, (k_ref, v_ref, turned, bias, sent, counts, sems, load_sems) = refs[:-8], refs[-8:]
@@ -157,7 +157,8 @@
         n = counts[owner]
         counts[owner] = n + 1
         distance = lax.rem(owner - me + pre, pre)
-        at = jnp.where(distance > 1, (distance - 2) * per_peer + n, (pre - 2) * per_peer)
+        spare = (pre - 1 - hops) * per_peer
+        at = jnp.where(distance > hops, (distance - hops - 1) * per_peer + n, spare)
         block = block_of(k_ref, v_ref, pl.multiple_of(b * BLK, BLK))
         sent[at] = block
         cache_ref[own_slot(slot, me, blocks)] = block
@@ -224,7 +225,7 @@
         where_seen(lowest_key(lengths_ref, hop, tile, rows), rows, act)
 
 
-def place_forwarded(cache, slot_ref, k_ref, v_ref, distance, pre, blocks):
+def place_blocks(cache, slot_ref, k_ref, v_ref, distance, pre, blocks):
     me = lax.axis_index("pre")
     source = lax.rem(me - distance + pre, pre)
 
@@ -233,28 +234,7 @@
         cache[at] = block_of(k_ref, v_ref, pl.multiple_of(b * BLK, BLK))
         return 0
 
-    def run():
-        lax.fori_loop(0, blocks, step, 0, unroll=8)
-
-    if distance < 2:
-        run()
-    else:
-        pl.when(me >= distance - 1)(run)
-
-
-def place_packed(cache, slot_ref, got_ref, distance, pre, blocks):
-    me = lax.axis_index("pre")
-    source = lax.rem(me - distance + pre, pre)
-    most = got_ref.shape[0] - 1
-
-    def step(b, n):
-        at = own_slot(slot_ref[source * blocks + b], me, blocks)
-        cache[at] = got_ref[jnp.minimum(n, most)]
-        return n + jnp.where(at < blocks, 1, 0)
-
-    @pl.when(me < distance - 1)
-    def _():
-        lax.fori_loop(0, blocks, step, jnp.int32(0), unroll=8)
+    lax.fori_loop(0, blocks, step, 0, unroll=8)
 
 
 def list_places(places_ref, slot_ref, hops, pre, blocks):
@@ -279,7 +259,7 @@
     first_out, last = hop == 1, hop == hops
     refs = list(refs)
     if not first_out:
-        got_ref, _ = refs.pop(0), refs.pop(0)
+        refs.pop(0)
     out_hbm, cache_out = refs.pop(0), refs.pop(0)
     state = () if last else (refs.pop(0), refs.pop(0))
     places_ref = refs.pop(0) if first_out else None
@@ -291,11 +271,9 @@
 
     cache = rest[0] if last else cache_out
     cache[...] = cache_in[...]
-    place_forwarded(cache, slot_ref, k_ref, v_ref, hop, pre, blocks)
+    place_blocks(cache, slot_ref, k_ref, v_ref, hop, pre, blocks)
     if first_out:
         list_places(places_ref, slot_ref, hops, pre, blocks)
-    else:
-        place_packed(cache, slot_ref, got_ref, hop, pre, blocks)
     if last:
         cache_store = pltpu.make_async_copy(cache.at[0:blocks], cache_out, sems.at[tiles])
         cache_store.start()
@@ -398,36 +376,31 @@
         pltpu.with_memory_space_constraint(x, pltpu.HBM) for x in (queries, new_keys, new_values)
     )
     q, acc, total, top, cache, *sent = pl.pallas_call(
-        functools.partial(own_kernel, pre),
+        functools.partial(own_kernel, pre, hops),
         out_shape=(attended_shape, acc_shape, stat_shape, stat_shape, open_cache)
-        + (packed,) * (pre - 2),
+        + (packed,) * (pre - 1 - hops),
         in_specs=[SMEM, SMEM] + [HBM] * 3,
-        out_specs=(VMEM,) * 5 + (HBM,) * (pre - 2),
+        out_specs=(VMEM,) * 5 + (HBM,) * (pre - 1 - hops),
         scratch_shapes=[
             pltpu.VMEM((rows, kv_width), bf16),
             pltpu.VMEM((rows, kv_width), bf16),
             turned,
             bias,
-            pltpu.VMEM(((pre - 2) * per_peer + 1, BLK, 2 * kv_width), bf16),
+            pltpu.VMEM(((pre - 1 - hops) * per_peer + 1, BLK, 2 * kv_width), bf16),
             pltpu.SMEM((pre,), jnp.int32),
-            pltpu.SemaphoreType.DMA((pre - 2,)),
+            pltpu.SemaphoreType.DMA((pre - 1 - hops,)),
             pltpu.SemaphoreType.DMA((3,)),
         ],
         cost_estimate=cost(1, 4),
         compiler_params=own_params,
         name="own_attention",
     )(lengths, block_slot, *in_hbm)
-    got = [
-        lax.ppermute(sent[d - 2], "pre", [((i - d) % pre, i) for i in range(d - 1)])
-        for d in range(2, hops + 1)
-    ]
-
+    got = []
     k = after(k, top)
     attended = None
     for hop in range(1, hops + 1):
         first_out, last = hop == 1, hop == hops
-        onward = [(i, i + 1) for i in range(hop - 1, pre - 1)]
-        next_k = None if last else lax.ppermute(k, "pre", onward)
+        next_k = None if last else lax.ppermute(k, "pre", ring)
         weights, factor, *tops = pl.pallas_call(
             functools.partial(scores_kernel, hop),
             out_shape=(weights_shape, stat_shape) + (() if last else (stat_shape,)),
@@ -442,17 +415,17 @@
         if last:
             for d in range(hops + 1, pre):
                 pairs = [(i, (i + d) % pre) for i in range(pre)]
-                got.append(lax.ppermute(after(sent[d - 2], factor), "pre", pairs))
-        next_v = None if last else lax.ppermute(v, "pre", onward)
+                got.append(lax.ppermute(after(sent[d - hops - 1], factor), "pre", pairs))
+        next_v = None if last else lax.ppermute(v, "pre", ring)
         places = shape(((pre - 1 - hops) * (per_peer + 1),), jnp.int32)
         carry = () if last else (acc_shape, stat_shape)
-        extra = [] if first_out else [got[hop - 2], attended]
+        extra = [] if first_out else [attended]
         attended, cache, *state = pl.pallas_call(
             functools.partial(values_kernel, hop, hops, pre),
             out_shape=(attended_shape, cache_shape if last else open_cache)
             + carry
             + ((places,) if first_out else ()),
-            in_specs=[SMEM, SMEM] + [VMEM] * 7 + ([] if first_out else [VMEM, HBM]),
+            in_specs=[SMEM, SMEM] + [VMEM] * 7 + ([] if first_out else [HBM]),
             out_specs=(HBM, HBM if last else VMEM)
             + (VMEM,) * len(carry)
             + ((SMEM,) if first_out else ()),
@@ -462,7 +435,7 @@
                 pltpu.SemaphoreType.DMA((tiles + 1,)),
             ]
             + ([pltpu.VMEM(open_cache.shape, bf16)] if last else []),
-            input_output_aliases={} if first_out else {10: 0},
+            input_output_aliases={} if first_out else {9: 0},
             cost_estimate=cost(0.5, 3),
             compiler_params=params,
             name="values",
@@ -484,7 +457,7 @@
         cost_estimate=cost(0, 1),
         compiler_params=params,
         name="place_last",
-    )(far_places, cache, *got[hops - 1 :])
+    )(far_places, cache, *got)
     return (attended, cache)
 
 

time: 33.1 us -> 33.5 us (1.012)
  waiting for transfers between devices: 4.33 us -> 12.1 us
  starting transfers between devices: 14.4 us -> 7.05 us
    ppermute x4 -> x3, starting transfers between devices: 9.75 us -> 2.4 us  [the longest x1 2.11 us: on_device(): got.append(lax.ppermute(after(sent[d - hops - 1], factor), 'pre', pairs))]
    ppermute x4 -> x3, waiting for transfers between devices: 1.3 us -> 5.93 us  [the longest x1 2.8 us: on_device(): next_k = None if last else lax.ppermute(k, 'pre', ring)]
    ppermute x1, waiting for transfers between devices: 1.85 us -> 4.77 us  [on_device(): lax.ppermute(new_values, 'pre', ring)]
  transfers between devices with their start and end apart: 6 -> 5, of which waited for: 4 -> 5; matrix products, arithmetic and copies ran while one was open for 0% -> 0% of each run, Pallas kernels for 33% -> 32%
where the time goes in v2:
time: 33.5 us; the launch traced here: 33.3 us
  waiting for transfers between devices  12.1 us (36%)
  Pallas kernels  12 us (36%)
  starting transfers between devices  7.05 us (21%)
  local copies, waits for them, and re-layouts  1.31 us (4%)
  between operations  0.84 us (3%)
    pallas_call x1, Pallas kernels, on_device(): pl.pallas_call(functools.partial(own_kernel, pre, hops), out_shape=(atten...  5.08 us
    ppermute x1, waiting for transfers between devices, on_device(): lax.ppermute(new_values, 'pre', ring)  4.77 us
    pallas_call x2, Pallas kernels, on_device(): pl.pallas_call(functools.partial(values_kernel, hop, hops, pre), out_shap...  4.35 us
    ppermute x1, starting transfers between devices, on_device(): lax.ppermute(new_keys, 'pre', ring)  3.08 us
    ppermute x1, waiting for transfers between devices, on_device(): next_k = None if last else lax.ppermute(k, 'pre', ring)  2.8 us
    ppermute x1, waiting for transfers between devices, on_device(): next_v = None if last else lax.ppermute(v, 'pre', ring)  2.77 us
    ppermute x1, starting transfers between devices, on_device(): got.append(lax.ppermute(after(sent[d - hops - 1], factor), 'pre', pairs))  2.11 us
    ppermute x1, starting transfers between devices, on_device(): lax.ppermute(new_values, 'pre', ring)  1.58 us
  transfers between devices with their start and end apart: 5, of which 5 were waited for; matrix products, arithmetic and copies ran while one was open for 0% of the time, Pallas kernels for 32%

profile of v2, /device:TPU:0, one launch (start us, length us, event | category | flops | bytes accessed | tf_op | source)
XLA Modules:
  0.0 33.3 jit_solution(18235873864840568918)
XLA Ops:
  0.6 3.1 %collective-permute-start.1 = (bf16[512,256]{1,0:T(8,128)(2,1)}, bf16[512,256]{1,0:T(8,128)(2,1)S(1)}, u32[]{:S(2)}, u32[]{:S(2)}) collective-permute-start(bf16[512,256]{1,0:T(8,128)(2,1)} %k_hbm.1), channel_id=1, source_target_pairs={{0,4},{4,8},{8,12},{12,0},{1,5},{5,9},{9,13},{13,1},{2,6},{6,10},{... | collective-permute-start | bytes 786440 | tf_op jit(solution)/shard_map/ppermute | solution.py:372
  3.7 1.6 %collective-permute-start = (bf16[512,256]{1,0:T(8,128)(2,1)}, bf16[512,256]{1,0:T(8,128)(2,1)S(1)}, u32[]{:S(2)}, u32[]{:S(2)}) collective-permute-start(bf16[512,256]{1,0:T(8,128)(2,1)} %v_hbm.1), channel_id=1, source_target_pairs={{0,4},{4,8},{8,12},{12,0},{1,5},{5,9},{9,13},{13,1},{2,6},{6,10},{... | collective-permute-start | bytes 786440 | tf_op jit(solution)/shard_map/ppermute | solution.py:372
  5.3 0.0 copy-start
  5.3 0.7 %copy-done = s32[4]{0:T(128)S(1)} copy-done((s32[4]{0:T(128)S(1)}, s32[4]{0:T(128)}, u32[]{:S(2)}) %copy-start) | copy-done | bytes 40
  5.9 0.0 copy-start.1
  5.9 0.7 %copy-done.1 = s32[128]{0:T(128)S(1)} copy-done((s32[128]{0:T(128)S(1)}, s32[128]{0:T(128)}, u32[]{:S(2)}) %copy-start.1) | copy-done | bytes 536
  6.6 5.1 %own_attention.1 = (bf16[512,1024]{1,0:T(8,128)(2,1)S(1)}, f32[2,128,2048]{2,1,0:T(8,128)S(1)}, f32[2,8,2048]{2,1,0:T(8,128)S(1)}, f32[2,8,2048]{2,1,0:T(8,128)S...) custom-call(s32[4]{0:T(128)S(1)} %copy-done, s32[128]{0:T(128)S(1)} %copy-done.1, ...), custom_call_target="tpu_custom_call" | custom-call | flops 1073741824 | bytes 4194304 | tf_op jit(solution)/shard_map/own_attention/pallas_call | solution.py:378
  11.7 1.4 %collective-permute-done.1.k_ref = bf16[512,256]{1,0:T(8,128)(2,1)S(1)} collective-permute-done((bf16[512,256]{1,0:T(8,128)(2,1)}, bf16[512,256]{1,0:T(8,128)(2,1)S(1)}, u32[]{:S(2)}, u32[]{:S(2)}) %collective-permute-start.1) | collective-permute-done | bytes 262176 | tf_op jit(solution)/shard_map/ppermute | solution.py:372
  13.1 0.3 collective-permute-start.3
  13.3 0.6 %scores.2 = (bf16[2,2,512,1024]{3,2,1,0:T(8,128)(2,1)S(1)}, f32[2,8,2048]{2,1,0:T(8,128)S(1)}, f32[2,8,2048]{2,1,0:T(8,128)S(1)}) custom-call(s32[4]{0:T(128)S(1)} %copy-done, bf16[512,1024]{1,0:T(8,128)(2,1)S(1)} %get-tuple-element.25.q_ref, bf16[512,256]{1,0:T(8,128)(2,1)S(1)} %collective-permute-done.1.k_ref, f32[2,8,2048]{2,1,0:T(8,128)S(1)} %get-tuple-element.26.old_top), custom_call_target="tpu_custom_call" | custom-call | flops 536870912 | bytes 3145728 | tf_op jit(solution)/shard_map/scores/pallas_call | solution.py:404
  13.9 4.8 %collective-permute-done.v_ref = bf16[512,256]{1,0:T(8,128)(2,1)S(1)} collective-permute-done((bf16[512,256]{1,0:T(8,128)(2,1)}, bf16[512,256]{1,0:T(8,128)(2,1)S(1)}, u32[]{:S(2)}, u32[]{:S(2)}) %collective-permute-start) | collective-permute-done | bytes 262176 | tf_op jit(solution)/shard_map/ppermute | solution.py:372
  18.7 0.0 collective-permute-start.2
  18.7 2.8 %values.2 = (bf16[512,1024]{1,0:T(8,128)(2,1)}, bf16[33,16,512]{2,1,0:T(8,128)(2,1)S(1)}, f32[2,128,2048]{2,1,0:T(8,128)S(1)}, f32[2,8,2048]{2,1,0:T(8,128)S(1)}, s32[9]{0:T(128)S(1)}) custom-call(s32[4]{0:T(128)S(1)} %copy-done, s32[128]{0:T(128)S(1)} %copy-done.1, bf16[512,256]{1,0:T(8,128)(2,1)S(1)} %collective-permute-done.v_ref, ...), custom_call_target="tpu_custom_call" | custom-call | flops 536870912 | bytes 3145728 | tf_op jit(solution)/shard_map/values/pallas_call | solution.py:423
  21.5 2.8 %collective-permute-done.3.k_ref = bf16[512,256]{1,0:T(8,128)(2,1)S(1)} collective-permute-done((bf16[512,256]{1,0:T(8,128)(2,1)S(1)}, bf16[512,256]{1,0:T(8,128)(2,1)S(1)}, u32[]{:S(2)}, u32[]{:S(2)}) %collective-permute-start.3) | collective-permute-done | bytes 262176 | tf_op jit(solution)/shard_map/ppermute | solution.py:403
  24.3 0.8 %scores.3 = (bf16[2,2,512,1024]{3,2,1,0:T(8,128)(2,1)S(1)}, f32[2,8,2048]{2,1,0:T(8,128)S(1)}) custom-call(s32[4]{0:T(128)S(1)} %copy-done, bf16[512,1024]{1,0:T(8,128)(2,1)S(1)} %get-tuple-element.25.q_ref, bf16[512,256]{1,0:T(8,128)(2,1)S(1)} %collective-permute-done.3.k_ref, f32[2,8,2048]{2,1,0:T(8,128)S(1)} %get-tuple-element.36.old_top), custom_call_target="tpu_custom_call" | custom-call | flops 536870912 | bytes 3145728 | tf_op jit(solution)/shard_map/scores/pallas_call | solution.py:404
  25.1 2.1 %collective-permute-start.4 = (bf16[8,16,512]{2,1,0:T(8,128)(2,1)S(1)}, bf16[8,16,512]{2,1,0:T(8,128)(2,1)S(1)}, u32[]{:S(2)}, u32[]{:S(2)}) collective-permute-start(bf16[8,16,512]{2,1,0:T(8,128)(2,1)S(1)} %get-tuple-element.47), channel_id=1, source_target_pairs={{0,12},{4,0},{8,4},{12,8},{1,13},{5,1},{9,5},{13,9},{2,14},{6,2},{... | collective-permute-start | bytes 393224 | tf_op jit(solution)/shard_map/ppermute | solution.py:418
  27.2 2.8 %collective-permute-done.2.v_ref = bf16[512,256]{1,0:T(8,128)(2,1)S(1)} collective-permute-done((bf16[512,256]{1,0:T(8,128)(2,1)S(1)}, bf16[512,256]{1,0:T(8,128)(2,1)S(1)}, u32[]{:S(2)}, u32[]{:S(2)}) %collective-permute-start.2) | collective-permute-done | bytes 262176 | tf_op jit(solution)/shard_map/ppermute | solution.py:419
  30.0 1.6 %values.3 = (bf16[512,1024]{1,0:T(8,128)(2,1)}, bf16[32,16,512]{2,1,0:T(8,128)(2,1)}) custom-call(s32[4]{0:T(128)S(1)} %copy-done, s32[128]{0:T(128)S(1)} %copy-done.1, bf16[512,256]{1,0:T(8,128)(2,1)S(1)} %collective-permute-done.2.v_ref, bf16[512,256]{1,0:T(8,128)(2,1)S(1)} %collective-permute-done.3.k_ref, ...), custom_call_target="tpu_custom_call", output_to_operand_aliasing={{0}: (9, {})} | custom-call | flops 536870912 | bytes 3145728 | tf_op jit(solution)/shard_map/values/pallas_call | solution.py:423
  31.6 0.4 %collective-permute-done.4.refs_0_ = bf16[8,16,512]{2,1,0:T(8,128)(2,1)S(1)} collective-permute-done((bf16[8,16,512]{2,1,0:T(8,128)(2,1)S(1)}, bf16[8,16,512]{2,1,0:T(8,128)(2,1)S(1)}, u32[]{:S(2)}, u32[]{:S(2)}) %collective-permute-start.4) | collective-permute-done | bytes 131104 | tf_op jit(solution)/shard_map/ppermute | solution.py:418
  31.9 1.3 %place_last.1 = bf16[32,16,512]{2,1,0:T(8,128)(2,1)} custom-call(s32[9]{0:T(128)S(1)} %get-tuple-element.44.places_ref, bf16[32,16,512]{2,1,0:T(8,128)(2,1)} %get-tuple-element.45.cache_in, bf16[8,16,512]{2,1,0:T(8,128)(2,1)S(1)} %collective-permute-done.4.refs_0_), custom_call_target="tpu_custom_call", output_to_operand_aliasing={{}: (1, {})} | custom-call | bytes 1048576 | tf_op jit(solution)/shard_map/place_last/pallas_call | solution.py:450
Async XLA Ops:
  0.6 12.4 %collective-permute-start.1 = (bf16[512,256]{1,0:T(8,128)(2,1)}, bf16[512,256]{1,0:T(8,128)(2,1)S(1)}, u32[]{:S(2)}, u32[]{:S(2)}) collective-permute-start(bf16[512,256]{1,0:T(8,128)(2,1)} %k_hbm.1), channel_id=1, source_target_pairs={{0,4},{4,8},{8,12},{12,0},{1,5},{5,9},{9,13},{13,1},{2,6},{6,10},{... | collective-permute-start | bytes 786440 | tf_op jit(solution)/shard_map/ppermute | solution.py:372
  3.7 15.0 %collective-permute-start = (bf16[512,256]{1,0:T(8,128)(2,1)}, bf16[512,256]{1,0:T(8,128)(2,1)S(1)}, u32[]{:S(2)}, u32[]{:S(2)}) collective-permute-start(bf16[512,256]{1,0:T(8,128)(2,1)} %v_hbm.1), channel_id=1, source_target_pairs={{0,4},{4,8},{8,12},{12,0},{1,5},{5,9},{9,13},{13,1},{2,6},{6,10},{... | collective-permute-start | bytes 786440 | tf_op jit(solution)/shard_map/ppermute | solution.py:372
  5.3 0.7 %copy-start = (s32[4]{0:T(128)S(1)}, s32[4]{0:T(128)}, u32[]{:S(2)}) copy-start(s32[4]{0:T(128)} %lengths_ref.9) | copy-start | bytes 52
  5.9 0.7 %copy-start.1 = (s32[128]{0:T(128)S(1)}, s32[128]{0:T(128)}, u32[]{:S(2)}) copy-start(s32[128]{0:T(128)} %slot_ref.5) | copy-start | bytes 1540
  13.1 11.2 %collective-permute-start.3 = (bf16[512,256]{1,0:T(8,128)(2,1)S(1)}, bf16[512,256]{1,0:T(8,128)(2,1)S(1)}, u32[]{:S(2)}, u32[]{:S(2)}) collective-permute-start(bf16[512,256]{1,0:T(8,128)(2,1)S(1)} %collective-permute-done.1.k_ref), channel_id=1, source_target_pairs={{0,4},{4,8},{8,12},{12,0},{1,5},{5,9},{9,13},{13,1},{2,6},{6,10},{... | collective-permute-start | bytes 786440 | tf_op jit(solution)/shard_map/ppermute | solution.py:403
  18.7 11.3 %collective-permute-start.2 = (bf16[512,256]{1,0:T(8,128)(2,1)S(1)}, bf16[512,256]{1,0:T(8,128)(2,1)S(1)}, u32[]{:S(2)}, u32[]{:S(2)}) collective-permute-start(bf16[512,256]{1,0:T(8,128)(2,1)S(1)} %collective-permute-done.v_ref), channel_id=1, source_target_pairs={{0,4},{4,8},{8,12},{12,0},{1,5},{5,9},{9,13},{13,1},{2,6},{6,10},{... | collective-permute-start | bytes 786440 | tf_op jit(solution)/shard_map/ppermute | solution.py:419
  25.1 6.8 %collective-permute-start.4 = (bf16[8,16,512]{2,1,0:T(8,128)(2,1)S(1)}, bf16[8,16,512]{2,1,0:T(8,128)(2,1)S(1)}, u32[]{:S(2)}, u32[]{:S(2)}) collective-permute-start(bf16[8,16,512]{2,1,0:T(8,128)(2,1)S(1)} %get-tuple-element.47), channel_id=1, source_target_pairs={{0,12},{4,0},{8,4},{12,8},{1,13},{5,1},{9,5},{13,9},{2,14},{6,2},{... | collective-permute-start | bytes 393224 | tf_op jit(solution)/shard_map/ppermute | solution.py:418

commit v3 on v2

--- a/solution.py
+++ b/solution.py
@@ -239,17 +239,28 @@
 
 def list_places(places_ref, slot_ref, hops, pre, blocks):
     me = lax.axis_index("pre")
-    per_peer = blocks // pre
-    for distance in range(hops + 1, pre):
+    stride = blocks // pre + 1
+    for i, distance in enumerate(range(hops, pre)):
         source = lax.rem(me - distance + pre, pre)
-        base = (distance - hops - 1) * (per_peer + 1)
 
         def step(b, n):
             at = own_slot(slot_ref[source * blocks + b], me, blocks)
-            places_ref[base + n] = at
+            places_ref[i * stride + n] = at
+            if i == 0:
+                places_ref[(pre - hops) * stride + n] = b
             return n + jnp.where(at < blocks, 1, 0)
 
         lax.fori_loop(0, blocks, step, jnp.int32(0), unroll=8)
+
+
+def place_listed(cache, places_ref, k_ref, v_ref, got_refs):
+    per_peer = got_refs[0].shape[0]
+    stride = per_peer + 1
+    for n in range(per_peer):
+        b = places_ref[(len(got_refs) + 1) * stride + n]
+        cache[places_ref[n]] = block_of(k_ref, v_ref, pl.multiple_of(b * BLK, BLK))
+        for i, got_ref in enumerate(got_refs):
+            cache[places_ref[(i + 1) * stride + n]] = got_ref[n]
 
 
 def values_kernel(
@@ -260,6 +271,7 @@
     refs = list(refs)
     if not first_out:
         refs.pop(0)
+    got_refs = [refs.pop(0) for _ in range(hops + 1, pre)] if last else []
     out_hbm, cache_out = refs.pop(0), refs.pop(0)
     state = () if last else (refs.pop(0), refs.pop(0))
     places_ref = refs.pop(0) if first_out else None
@@ -271,7 +283,10 @@
 
     cache = rest[0] if last else cache_out
     cache[...] = cache_in[...]
-    place_blocks(cache, slot_ref, k_ref, v_ref, hop, pre, blocks)
+    if last:
+        place_listed(cache, slot_ref, k_ref, v_ref, got_refs)
+    else:
+        place_blocks(cache, slot_ref, k_ref, v_ref, hop, pre, blocks)
     if first_out:
         list_places(places_ref, slot_ref, hops, pre, blocks)
     if last:
@@ -317,22 +332,6 @@
             pl.when(low < rows)(store.wait)
     if last:
         cache_store.wait()
-
-
-def place_last_kernel(places_ref, cache_in, *refs):
-    *got, cache_hbm, sems = refs
-    per_peer = got[0].shape[0]
-    copies = []
-    for i, got_ref in enumerate(got):
-        for n in range(per_peer):
-            at = places_ref[i * (per_peer + 1) + n]
-            copy = pltpu.make_async_copy(
-                got_ref.at[n], cache_hbm.at[at], sems.at[i * per_peer + n]
-            )
-            copy.start()
-            copies.append(copy)
-    for copy in copies:
-        copy.wait()
 
 
 def on_device(queries, new_keys, new_values, lengths, block_slot):
@@ -417,15 +416,18 @@
                 pairs = [(i, (i + d) % pre) for i in range(pre)]
                 got.append(lax.ppermute(after(sent[d - hops - 1], factor), "pre", pairs))
         next_v = None if last else lax.ppermute(v, "pre", ring)
-        places = shape(((pre - 1 - hops) * (per_peer + 1),), jnp.int32)
+        places = shape(((pre - hops + 1) * (per_peer + 1),), jnp.int32)
         carry = () if last else (acc_shape, stat_shape)
-        extra = [] if first_out else [attended]
+        extra = ([] if first_out else [attended]) + (got if last else [])
         attended, cache, *state = pl.pallas_call(
             functools.partial(values_kernel, hop, hops, pre),
             out_shape=(attended_shape, cache_shape if last else open_cache)
             + carry
             + ((places,) if first_out else ()),
-            in_specs=[SMEM, SMEM] + [VMEM] * 7 + ([] if first_out else [HBM]),
+            in_specs=[SMEM, SMEM]
+            + [VMEM] * 7
+            + ([] if first_out else [HBM])
+            + ([VMEM] * len(got) if last else []),
             out_specs=(HBM, HBM if last else VMEM)
             + (VMEM,) * len(carry)
             + ((SMEM,) if first_out else ()),
@@ -439,7 +441,7 @@
             cost_estimate=cost(0.5, 3),
             compiler_params=params,
             name="values",
-        )(lengths, block_slot, v, k, weights, factor, acc, total, cache, *extra)
+        )(lengths, far_places if last else block_slot, v, k, weights, factor, acc, total, cache, *extra)
         if first_out:
             far_places = state.pop()
         if not last:
@@ -447,17 +449,6 @@
             acc, total = state
             k, v = after(next_k, total), next_v
 
-    cache = pl.pallas_call(
-        place_last_kernel,
-        out_shape=cache_shape,
-        in_specs=[SMEM, HBM] + [VMEM] * (pre - 1 - hops),
-        out_specs=HBM,
-        scratch_shapes=[pltpu.SemaphoreType.DMA(((pre - 1 - hops) * per_peer,))],
-        input_output_aliases={1: 0},
-        cost_estimate=cost(0, 1),
-        compiler_params=params,
-        name="place_last",
-    )(far_places, cache, *got)
     return (attended, cache)
 
 

time: 33.5 us -> 33.7 us (level)
  waiting for transfers between devices: 12.1 us -> 13.6 us
  Pallas kernels: 12 us -> 10.8 us
    ppermute x1, waiting for transfers between devices: 0.36 us -> 2.03 us  [on_device(): got.append(lax.ppermute(after(sent[d - hops - 1], factor), 'pre', pairs))]
    pallas_call x1 -> x0, Pallas kernels: 1.26 us -> none  [on_device(): pl.pallas_call(place_last_kernel, out_shape=cache_shape, in_specs=[SMEM,...]
  transfers between devices with their start and end apart: 5 -> 5, of which waited for: 5 -> 5; matrix products, arithmetic and copies ran while one was open for 0% -> 0% of each run, Pallas kernels for 32% -> 28%
where the time goes in v3:
time: 33.7 us; the launch traced here: 33.6 us
  waiting for transfers between devices  13.6 us (40%)
  Pallas kernels  10.8 us (32%)
  starting transfers between devices  7.1 us (21%)
  local copies, waits for them, and re-layouts  1.31 us (4%)
  between operations  0.83 us (2%)
    pallas_call x1, Pallas kernels, on_device(): pl.pallas_call(functools.partial(own_kernel, pre, hops), out_shape=(atten...  5.08 us
    ppermute x1, waiting for transfers between devices, on_device(): lax.ppermute(new_values, 'pre', ring)  4.77 us
    pallas_call x2, Pallas kernels, on_device(): pl.pallas_call(functools.partial(values_kernel, hop, hops, pre), out_shap...  4.36 us
    ppermute x1, starting transfers between devices, on_device(): lax.ppermute(new_keys, 'pre', ring)  3.08 us
    ppermute x1, waiting for transfers between devices, on_device(): next_v = None if last else lax.ppermute(v, 'pre', ring)  2.72 us
    ppermute x1, waiting for transfers between devices, on_device(): next_k = None if last else lax.ppermute(k, 'pre', ring)  2.64 us
    ppermute x1, starting transfers between devices, on_device(): got.append(lax.ppermute(after(sent[d - hops - 1], factor), 'pre', pairs))  2.16 us
    ppermute x1, waiting for transfers between devices, on_device(): got.append(lax.ppermute(after(sent[d - hops - 1], factor), 'pre', pairs))  2.03 us
  transfers between devices with their start and end apart: 5, of which 5 were waited for; matrix products, arithmetic and copies ran while one was open for 0% of the time, Pallas kernels for 28%

profile of v3, /device:TPU:0, one launch (start us, length us, event | category | flops | bytes accessed | tf_op | source)
XLA Modules:
  0.0 33.6 jit_solution(5188827781520590517)
XLA Ops:
  0.6 3.1 %collective-permute-start.1 = (bf16[512,256]{1,0:T(8,128)(2,1)}, bf16[512,256]{1,0:T(8,128)(2,1)S(1)}, u32[]{:S(2)}, u32[]{:S(2)}) collective-permute-start(bf16[512,256]{1,0:T(8,128)(2,1)} %k_hbm.1), channel_id=1, source_target_pairs={{0,4},{4,8},{8,12},{12,0},{1,5},{5,9},{9,13},{13,1},{2,6},{6,10},{... | collective-permute-start | bytes 786440 | tf_op jit(solution)/shard_map/ppermute | solution.py:371
  3.7 1.6 %collective-permute-start = (bf16[512,256]{1,0:T(8,128)(2,1)}, bf16[512,256]{1,0:T(8,128)(2,1)S(1)}, u32[]{:S(2)}, u32[]{:S(2)}) collective-permute-start(bf16[512,256]{1,0:T(8,128)(2,1)} %v_hbm.1), channel_id=1, source_target_pairs={{0,4},{4,8},{8,12},{12,0},{1,5},{5,9},{9,13},{13,1},{2,6},{6,10},{... | collective-permute-start | bytes 786440 | tf_op jit(solution)/shard_map/ppermute | solution.py:371
  5.3 0.0 copy-start
  5.3 0.7 %copy-done = s32[4]{0:T(128)S(1)} copy-done((s32[4]{0:T(128)S(1)}, s32[4]{0:T(128)}, u32[]{:S(2)}) %copy-start) | copy-done | bytes 40
  5.9 0.0 copy-start.1
  5.9 0.7 %copy-done.1 = s32[128]{0:T(128)S(1)} copy-done((s32[128]{0:T(128)S(1)}, s32[128]{0:T(128)}, u32[]{:S(2)}) %copy-start.1) | copy-done | bytes 536
  6.6 5.1 %own_attention.1 = (bf16[512,1024]{1,0:T(8,128)(2,1)S(1)}, f32[2,128,2048]{2,1,0:T(8,128)S(1)}, f32[2,8,2048]{2,1,0:T(8,128)S(1)}, f32[2,8,2048]{2,1,0:T(8,128)S...) custom-call(s32[4]{0:T(128)S(1)} %copy-done, s32[128]{0:T(128)S(1)} %copy-done.1, ...), custom_call_target="tpu_custom_call" | custom-call | flops 1073741824 | bytes 4194304 | tf_op jit(solution)/shard_map/own_attention/pallas_call | solution.py:377
  11.7 1.4 %collective-permute-done.1.k_ref = bf16[512,256]{1,0:T(8,128)(2,1)S(1)} collective-permute-done((bf16[512,256]{1,0:T(8,128)(2,1)}, bf16[512,256]{1,0:T(8,128)(2,1)S(1)}, u32[]{:S(2)}, u32[]{:S(2)}) %collective-permute-start.1) | collective-permute-done | bytes 262176 | tf_op jit(solution)/shard_map/ppermute | solution.py:371
  13.1 0.3 collective-permute-start.3
  13.3 0.6 %scores.2 = (bf16[2,2,512,1024]{3,2,1,0:T(8,128)(2,1)S(1)}, f32[2,8,2048]{2,1,0:T(8,128)S(1)}, f32[2,8,2048]{2,1,0:T(8,128)S(1)}) custom-call(s32[4]{0:T(128)S(1)} %copy-done, bf16[512,1024]{1,0:T(8,128)(2,1)S(1)} %get-tuple-element.23.q_ref, bf16[512,256]{1,0:T(8,128)(2,1)S(1)} %collective-permute-done.1.k_ref, f32[2,8,2048]{2,1,0:T(8,128)S(1)} %get-tuple-element.24.old_top), custom_call_target="tpu_custom_call" | custom-call | flops 536870912 | bytes 3145728 | tf_op jit(solution)/shard_map/scores/pallas_call | solution.py:403
  13.9 4.8 %collective-permute-done.v_ref = bf16[512,256]{1,0:T(8,128)(2,1)S(1)} collective-permute-done((bf16[512,256]{1,0:T(8,128)(2,1)}, bf16[512,256]{1,0:T(8,128)(2,1)S(1)}, u32[]{:S(2)}, u32[]{:S(2)}) %collective-permute-start) | collective-permute-done | bytes 262176 | tf_op jit(solution)/shard_map/ppermute | solution.py:371
  18.7 0.0 collective-permute-start.2
  18.7 2.9 %values.2 = (bf16[512,1024]{1,0:T(8,128)(2,1)}, bf16[33,16,512]{2,1,0:T(8,128)(2,1)S(1)}, f32[2,128,2048]{2,1,0:T(8,128)S(1)}, f32[2,8,2048]{2,1,0:T(8,128)S(1)}, s32[27]{0:T(128)S(1)}) custom-call(s32[4]{0:T(128)S(1)} %copy-done, s32[128]{0:T(128)S(1)} %copy-done.1, bf16[512,256]{1,0:T(8,128)(2,1)S(1)} %collective-permute-done.v_ref, ...), custom_call_target="tpu_custom_call" | custom-call | flops 536870912 | bytes 3145728 | tf_op jit(solution)/shard_map/values/pallas_call | solution.py:422
  21.7 2.6 %collective-permute-done.3.k_ref = bf16[512,256]{1,0:T(8,128)(2,1)S(1)} collective-permute-done((bf16[512,256]{1,0:T(8,128)(2,1)S(1)}, bf16[512,256]{1,0:T(8,128)(2,1)S(1)}, u32[]{:S(2)}, u32[]{:S(2)}) %collective-permute-start.3) | collective-permute-done | bytes 262176 | tf_op jit(solution)/shard_map/ppermute | solution.py:402
  24.3 0.8 %scores.3 = (bf16[2,2,512,1024]{3,2,1,0:T(8,128)(2,1)S(1)}, f32[2,8,2048]{2,1,0:T(8,128)S(1)}) custom-call(s32[4]{0:T(128)S(1)} %copy-done, bf16[512,1024]{1,0:T(8,128)(2,1)S(1)} %get-tuple-element.23.q_ref, bf16[512,256]{1,0:T(8,128)(2,1)S(1)} %collective-permute-done.3.k_ref, f32[2,8,2048]{2,1,0:T(8,128)S(1)} %get-tuple-element.35.old_top), custom_call_target="tpu_custom_call" | custom-call | flops 536870912 | bytes 3145728 | tf_op jit(solution)/shard_map/scores/pallas_call | solution.py:403
  25.1 2.2 %collective-permute-start.4 = (bf16[8,16,512]{2,1,0:T(8,128)(2,1)S(1)}, bf16[8,16,512]{2,1,0:T(8,128)(2,1)S(1)}, u32[]{:S(2)}, u32[]{:S(2)}) collective-permute-start(bf16[8,16,512]{2,1,0:T(8,128)(2,1)S(1)} %get-tuple-element.43), channel_id=1, source_target_pairs={{0,12},{4,0},{8,4},{12,8},{1,13},{5,1},{9,5},{13,9},{2,14},{6,2},{... | collective-permute-start | bytes 393224 | tf_op jit(solution)/shard_map/ppermute | solution.py:417
  27.2 2.7 %collective-permute-done.2.v_ref = bf16[512,256]{1,0:T(8,128)(2,1)S(1)} collective-permute-done((bf16[512,256]{1,0:T(8,128)(2,1)S(1)}, bf16[512,256]{1,0:T(8,128)(2,1)S(1)}, u32[]{:S(2)}, u32[]{:S(2)}) %collective-permute-start.2) | collective-permute-done | bytes 262176 | tf_op jit(solution)/shard_map/ppermute | solution.py:418
  30.0 2.0 %collective-permute-done.4.refs_1_ = bf16[8,16,512]{2,1,0:T(8,128)(2,1)S(1)} collective-permute-done((bf16[8,16,512]{2,1,0:T(8,128)(2,1)S(1)}, bf16[8,16,512]{2,1,0:T(8,128)(2,1)S(1)}, u32[]{:S(2)}, u32[]{:S(2)}) %collective-permute-start.4) | collective-permute-done | bytes 131104 | tf_op jit(solution)/shard_map/ppermute | solution.py:417
  32.0 1.4 %values.3 = (bf16[512,1024]{1,0:T(8,128)(2,1)}, bf16[32,16,512]{2,1,0:T(8,128)(2,1)}) custom-call(s32[4]{0:T(128)S(1)} %copy-done, s32[27]{0:T(128)S(1)} %get-tuple-element.32.slot_ref, bf16[512,256]{1,0:T(8,128)(2,1)S(1)} %collective-permute-done.2.v_ref, bf16[512,256]{1,0:T(8,128)(2,1)S(1)} %collective-permute-done.3.k_ref, ...), custom_call_target="tpu_custom_call", output_to_operand_aliasing={{0}: (9, {})} | custom-call | flops 536870912 | bytes 3145728 | tf_op jit(solution)/shard_map/values/pallas_call | solution.py:422
Async XLA Ops:
  0.6 12.4 %collective-permute-start.1 = (bf16[512,256]{1,0:T(8,128)(2,1)}, bf16[512,256]{1,0:T(8,128)(2,1)S(1)}, u32[]{:S(2)}, u32[]{:S(2)}) collective-permute-start(bf16[512,256]{1,0:T(8,128)(2,1)} %k_hbm.1), channel_id=1, source_target_pairs={{0,4},{4,8},{8,12},{12,0},{1,5},{5,9},{9,13},{13,1},{2,6},{6,10},{... | collective-permute-start | bytes 786440 | tf_op jit(solution)/shard_map/ppermute | solution.py:371
  3.7 15.0 %collective-permute-start = (bf16[512,256]{1,0:T(8,128)(2,1)}, bf16[512,256]{1,0:T(8,128)(2,1)S(1)}, u32[]{:S(2)}, u32[]{:S(2)}) collective-permute-start(bf16[512,256]{1,0:T(8,128)(2,1)} %v_hbm.1), channel_id=1, source_target_pairs={{0,4},{4,8},{8,12},{12,0},{1,5},{5,9},{9,13},{13,1},{2,6},{6,10},{... | collective-permute-start | bytes 786440 | tf_op jit(solution)/shard_map/ppermute | solution.py:371
  5.3 0.7 %copy-start = (s32[4]{0:T(128)S(1)}, s32[4]{0:T(128)}, u32[]{:S(2)}) copy-start(s32[4]{0:T(128)} %lengths_ref.9) | copy-start | bytes 52
  5.9 0.7 %copy-start.1 = (s32[128]{0:T(128)S(1)}, s32[128]{0:T(128)}, u32[]{:S(2)}) copy-start(s32[128]{0:T(128)} %slot_ref.3) | copy-start | bytes 1540
  13.1 11.2 %collective-permute-start.3 = (bf16[512,256]{1,0:T(8,128)(2,1)S(1)}, bf16[512,256]{1,0:T(8,128)(2,1)S(1)}, u32[]{:S(2)}, u32[]{:S(2)}) collective-permute-start(bf16[512,256]{1,0:T(8,128)(2,1)S(1)} %collective-permute-done.1.k_ref), channel_id=1, source_target_pairs={{0,4},{4,8},{8,12},{12,0},{1,5},{5,9},{9,13},{13,1},{2,6},{6,10},{... | collective-permute-start | bytes 786440 | tf_op jit(solution)/shard_map/ppermute | solution.py:402
  18.7 11.3 %collective-permute-start.2 = (bf16[512,256]{1,0:T(8,128)(2,1)S(1)}, bf16[512,256]{1,0:T(8,128)(2,1)S(1)}, u32[]{:S(2)}, u32[]{:S(2)}) collective-permute-start(bf16[512,256]{1,0:T(8,128)(2,1)S(1)} %collective-permute-done.v_ref), channel_id=1, source_target_pairs={{0,4},{4,8},{8,12},{12,0},{1,5},{5,9},{9,13},{13,1},{2,6},{6,10},{... | collective-permute-start | bytes 786440 | tf_op jit(solution)/shard_map/ppermute | solution.py:418
  25.1 6.9 %collective-permute-start.4 = (bf16[8,16,512]{2,1,0:T(8,128)(2,1)S(1)}, bf16[8,16,512]{2,1,0:T(8,128)(2,1)S(1)}, u32[]{:S(2)}, u32[]{:S(2)}) collective-permute-start(bf16[8,16,512]{2,1,0:T(8,128)(2,1)S(1)} %get-tuple-element.43), channel_id=1, source_target_pairs={{0,12},{4,0},{8,4},{12,8},{1,13},{5,1},{9,5},{13,9},{2,14},{6,2},{... | collective-permute-start | bytes 393224 | tf_op jit(solution)/shard_map/ppermute | solution.py:417

commit v4 on v3

--- a/solution.py
+++ b/solution.py
@@ -411,11 +411,11 @@
             name="scores",
         )(lengths, q, k, top)
         v = after(v, factor)
-        if last:
+        next_v = None if last else lax.ppermute(v, "pre", ring)
+        if first_out:
             for d in range(hops + 1, pre):
                 pairs = [(i, (i + d) % pre) for i in range(pre)]
-                got.append(lax.ppermute(after(sent[d - hops - 1], factor), "pre", pairs))
-        next_v = None if last else lax.ppermute(v, "pre", ring)
+                got.append(lax.ppermute(after(sent[d - hops - 1], v), "pre", pairs))
         places = shape(((pre - hops + 1) * (per_peer + 1),), jnp.int32)
         carry = () if last else (acc_shape, stat_shape)
         extra = ([] if first_out else [attended]) + (got if last else [])

time: 33.7 us -> 33.7 us (level)
  waiting for transfers between devices: 13.6 us -> 11.8 us
  starting transfers between devices: 7.1 us -> 8.73 us
    ppermute x1, waiting for transfers between devices: 2.64 us -> 0.01 us  [on_device(): next_k = None if last else lax.ppermute(k, 'pre', ring)]
    ppermute x1, starting transfers between devices: 2.16 us -> 3.79 us  [on_device(): got.append(lax.ppermute(after(sent[d - hops - 1], v), 'pre', pairs))]
    ppermute x1, waiting for transfers between devices: 2.72 us -> 3.72 us  [on_device(): next_v = None if last else lax.ppermute(v, 'pre', ring)]
  transfers between devices with their start and end apart: 5 -> 5, of which waited for: 5 -> 4; matrix products, arithmetic and copies ran while one was open for 0% -> 0% of each run, Pallas kernels for 28% -> 28%
where the time goes in v4:
time: 33.7 us; the launch traced here: 33.5 us
  waiting for transfers between devices  11.8 us (35%)
  Pallas kernels  10.8 us (32%)
  starting transfers between devices  8.73 us (26%)
  local copies, waits for them, and re-layouts  1.31 us (4%)
  between operations  0.84 us (2%)
    pallas_call x1, Pallas kernels, on_device(): pl.pallas_call(functools.partial(own_kernel, pre, hops), out_shape=(atten...  5.08 us
    ppermute x1, waiting for transfers between devices, on_device(): lax.ppermute(new_values, 'pre', ring)  4.77 us
    pallas_call x2, Pallas kernels, on_device(): pl.pallas_call(functools.partial(values_kernel, hop, hops, pre), out_shap...  4.36 us
    ppermute x1, starting transfers between devices, on_device(): got.append(lax.ppermute(after(sent[d - hops - 1], v), 'pre', pairs))  3.79 us
    ppermute x1, waiting for transfers between devices, on_device(): next_v = None if last else lax.ppermute(v, 'pre', ring)  3.72 us
    ppermute x1, starting transfers between devices, on_device(): lax.ppermute(new_keys, 'pre', ring)  3.08 us
    ppermute x1, waiting for transfers between devices, on_device(): got.append(lax.ppermute(after(sent[d - hops - 1], v), 'pre', pairs))  1.94 us
    ppermute x1, starting transfers between devices, on_device(): lax.ppermute(new_values, 'pre', ring)  1.58 us
  transfers between devices with their start and end apart: 5, of which 4 were waited for; matrix products, arithmetic and copies ran while one was open for 0% of the time, Pallas kernels for 28%

profile of v4, /device:TPU:0, one launch (start us, length us, event | category | flops | bytes accessed | tf_op | source)
XLA Modules:
  0.0 33.5 jit_solution(14259360715361149238)
XLA Ops:
  0.6 3.1 %collective-permute-start.1 = (bf16[512,256]{1,0:T(8,128)(2,1)}, bf16[512,256]{1,0:T(8,128)(2,1)S(1)}, u32[]{:S(2)}, u32[]{:S(2)}) collective-permute-start(bf16[512,256]{1,0:T(8,128)(2,1)} %k_hbm.1), channel_id=1, source_target_pairs={{0,4},{4,8},{8,12},{12,0},{1,5},{5,9},{9,13},{13,1},{2,6},{6,10},{... | collective-permute-start | bytes 786440 | tf_op jit(solution)/shard_map/ppermute | solution.py:371
  3.7 1.6 %collective-permute-start = (bf16[512,256]{1,0:T(8,128)(2,1)}, bf16[512,256]{1,0:T(8,128)(2,1)S(1)}, u32[]{:S(2)}, u32[]{:S(2)}) collective-permute-start(bf16[512,256]{1,0:T(8,128)(2,1)} %v_hbm.1), channel_id=1, source_target_pairs={{0,4},{4,8},{8,12},{12,0},{1,5},{5,9},{9,13},{13,1},{2,6},{6,10},{... | collective-permute-start | bytes 786440 | tf_op jit(solution)/shard_map/ppermute | solution.py:371
  5.3 0.0 copy-start
  5.3 0.7 %copy-done = s32[4]{0:T(128)S(1)} copy-done((s32[4]{0:T(128)S(1)}, s32[4]{0:T(128)}, u32[]{:S(2)}) %copy-start) | copy-done | bytes 40
  5.9 0.0 copy-start.1
  5.9 0.7 %copy-done.1 = s32[128]{0:T(128)S(1)} copy-done((s32[128]{0:T(128)S(1)}, s32[128]{0:T(128)}, u32[]{:S(2)}) %copy-start.1) | copy-done | bytes 536
  6.6 5.1 %own_attention.1 = (bf16[512,1024]{1,0:T(8,128)(2,1)S(1)}, f32[2,128,2048]{2,1,0:T(8,128)S(1)}, f32[2,8,2048]{2,1,0:T(8,128)S(1)}, f32[2,8,2048]{2,1,0:T(8,128)S...) custom-call(s32[4]{0:T(128)S(1)} %copy-done, s32[128]{0:T(128)S(1)} %copy-done.1, ...), custom_call_target="tpu_custom_call" | custom-call | flops 1073741824 | bytes 4194304 | tf_op jit(solution)/shard_map/own_attention/pallas_call | solution.py:377
  11.7 1.4 %collective-permute-done.1.k_ref = bf16[512,256]{1,0:T(8,128)(2,1)S(1)} collective-permute-done((bf16[512,256]{1,0:T(8,128)(2,1)}, bf16[512,256]{1,0:T(8,128)(2,1)S(1)}, u32[]{:S(2)}, u32[]{:S(2)}) %collective-permute-start.1) | collective-permute-done | bytes 262176 | tf_op jit(solution)/shard_map/ppermute | solution.py:371
  13.1 0.3 collective-permute-start.3
  13.3 0.6 %scores.2 = (bf16[2,2,512,1024]{3,2,1,0:T(8,128)(2,1)S(1)}, f32[2,8,2048]{2,1,0:T(8,128)S(1)}, f32[2,8,2048]{2,1,0:T(8,128)S(1)}) custom-call(s32[4]{0:T(128)S(1)} %copy-done, bf16[512,1024]{1,0:T(8,128)(2,1)S(1)} %get-tuple-element.23.q_ref, bf16[512,256]{1,0:T(8,128)(2,1)S(1)} %collective-permute-done.1.k_ref, f32[2,8,2048]{2,1,0:T(8,128)S(1)} %get-tuple-element.24.old_top), custom_call_target="tpu_custom_call" | custom-call | flops 536870912 | bytes 3145728 | tf_op jit(solution)/shard_map/scores/pallas_call | solution.py:403
  13.9 4.8 %collective-permute-done.v_ref = bf16[512,256]{1,0:T(8,128)(2,1)S(1)} collective-permute-done((bf16[512,256]{1,0:T(8,128)(2,1)}, bf16[512,256]{1,0:T(8,128)(2,1)S(1)}, u32[]{:S(2)}, u32[]{:S(2)}) %collective-permute-start) | collective-permute-done | bytes 262176 | tf_op jit(solution)/shard_map/ppermute | solution.py:371
  18.7 0.0 collective-permute-start.2
  18.7 3.8 %collective-permute-start.4 = (bf16[8,16,512]{2,1,0:T(8,128)(2,1)S(1)}, bf16[8,16,512]{2,1,0:T(8,128)(2,1)S(1)}, u32[]{:S(2)}, u32[]{:S(2)}) collective-permute-start(bf16[8,16,512]{2,1,0:T(8,128)(2,1)S(1)} %get-tuple-element.43), channel_id=1, source_target_pairs={{0,12},{4,0},{8,4},{12,8},{1,13},{5,1},{9,5},{13,9},{2,14},{6,2},{... | collective-permute-start | bytes 393224 | tf_op jit(solution)/shard_map/ppermute | solution.py:418
  22.5 2.9 %values.2 = (bf16[512,1024]{1,0:T(8,128)(2,1)}, bf16[33,16,512]{2,1,0:T(8,128)(2,1)S(1)}, f32[2,128,2048]{2,1,0:T(8,128)S(1)}, f32[2,8,2048]{2,1,0:T(8,128)S(1)}, s32[27]{0:T(128)S(1)}) custom-call(s32[4]{0:T(128)S(1)} %copy-done, s32[128]{0:T(128)S(1)} %copy-done.1, bf16[512,256]{1,0:T(8,128)(2,1)S(1)} %collective-permute-done.v_ref, ...), custom_call_target="tpu_custom_call" | custom-call | flops 536870912 | bytes 3145728 | tf_op jit(solution)/shard_map/values/pallas_call | solution.py:422
  25.5 0.0 collective-permute-done.3.k_ref
  25.5 0.8 %scores.3 = (bf16[2,2,512,1024]{3,2,1,0:T(8,128)(2,1)S(1)}, f32[2,8,2048]{2,1,0:T(8,128)S(1)}) custom-call(s32[4]{0:T(128)S(1)} %copy-done, bf16[512,1024]{1,0:T(8,128)(2,1)S(1)} %get-tuple-element.23.q_ref, bf16[512,256]{1,0:T(8,128)(2,1)S(1)} %collective-permute-done.3.k_ref, f32[2,8,2048]{2,1,0:T(8,128)S(1)} %get-tuple-element.35.old_top), custom_call_target="tpu_custom_call" | custom-call | flops 536870912 | bytes 3145728 | tf_op jit(solution)/shard_map/scores/pallas_call | solution.py:403
  26.2 3.7 %collective-permute-done.2.v_ref = bf16[512,256]{1,0:T(8,128)(2,1)S(1)} collective-permute-done((bf16[512,256]{1,0:T(8,128)(2,1)S(1)}, bf16[512,256]{1,0:T(8,128)(2,1)S(1)}, u32[]{:S(2)}, u32[]{:S(2)}) %collective-permute-start.2) | collective-permute-done | bytes 262176 | tf_op jit(solution)/shard_map/ppermute | solution.py:414
  30.0 1.9 %collective-permute-done.4.refs_1_ = bf16[8,16,512]{2,1,0:T(8,128)(2,1)S(1)} collective-permute-done((bf16[8,16,512]{2,1,0:T(8,128)(2,1)S(1)}, bf16[8,16,512]{2,1,0:T(8,128)(2,1)S(1)}, u32[]{:S(2)}, u32[]{:S(2)}) %collective-permute-start.4) | collective-permute-done | bytes 131104 | tf_op jit(solution)/shard_map/ppermute | solution.py:418
  31.9 1.4 %values.3 = (bf16[512,1024]{1,0:T(8,128)(2,1)}, bf16[32,16,512]{2,1,0:T(8,128)(2,1)}) custom-call(s32[4]{0:T(128)S(1)} %copy-done, s32[27]{0:T(128)S(1)} %get-tuple-element.32.slot_ref, bf16[512,256]{1,0:T(8,128)(2,1)S(1)} %collective-permute-done.2.v_ref, bf16[512,256]{1,0:T(8,128)(2,1)S(1)} %collective-permute-done.3.k_ref, ...), custom_call_target="tpu_custom_call", output_to_operand_aliasing={{0}: (9, {})} | custom-call | flops 536870912 | bytes 3145728 | tf_op jit(solution)/shard_map/values/pallas_call | solution.py:422
Async XLA Ops:
  0.6 12.4 %collective-permute-start.1 = (bf16[512,256]{1,0:T(8,128)(2,1)}, bf16[512,256]{1,0:T(8,128)(2,1)S(1)}, u32[]{:S(2)}, u32[]{:S(2)}) collective-permute-start(bf16[512,256]{1,0:T(8,128)(2,1)} %k_hbm.1), channel_id=1, source_target_pairs={{0,4},{4,8},{8,12},{12,0},{1,5},{5,9},{9,13},{13,1},{2,6},{6,10},{... | collective-permute-start | bytes 786440 | tf_op jit(solution)/shard_map/ppermute | solution.py:371
  3.7 15.0 %collective-permute-start = (bf16[512,256]{1,0:T(8,128)(2,1)}, bf16[512,256]{1,0:T(8,128)(2,1)S(1)}, u32[]{:S(2)}, u32[]{:S(2)}) collective-permute-start(bf16[512,256]{1,0:T(8,128)(2,1)} %v_hbm.1), channel_id=1, source_target_pairs={{0,4},{4,8},{8,12},{12,0},{1,5},{5,9},{9,13},{13,1},{2,6},{6,10},{... | collective-permute-start | bytes 786440 | tf_op jit(solution)/shard_map/ppermute | solution.py:371
  5.3 0.7 %copy-start = (s32[4]{0:T(128)S(1)}, s32[4]{0:T(128)}, u32[]{:S(2)}) copy-start(s32[4]{0:T(128)} %lengths_ref.9) | copy-start | bytes 52
  5.9 0.7 %copy-start.1 = (s32[128]{0:T(128)S(1)}, s32[128]{0:T(128)}, u32[]{:S(2)}) copy-start(s32[128]{0:T(128)} %slot_ref.3) | copy-start | bytes 1540
  13.1 12.4 %collective-permute-start.3 = (bf16[512,256]{1,0:T(8,128)(2,1)S(1)}, bf16[512,256]{1,0:T(8,128)(2,1)S(1)}, u32[]{:S(2)}, u32[]{:S(2)}) collective-permute-start(bf16[512,256]{1,0:T(8,128)(2,1)S(1)} %collective-permute-done.1.k_ref), channel_id=1, source_target_pairs={{0,4},{4,8},{8,12},{12,0},{1,5},{5,9},{9,13},{13,1},{2,6},{6,10},{... | collective-permute-start | bytes 786440 | tf_op jit(solution)/shard_map/ppermute | solution.py:402
  18.7 11.3 %collective-permute-start.2 = (bf16[512,256]{1,0:T(8,128)(2,1)S(1)}, bf16[512,256]{1,0:T(8,128)(2,1)S(1)}, u32[]{:S(2)}, u32[]{:S(2)}) collective-permute-start(bf16[512,256]{1,0:T(8,128)(2,1)S(1)} %collective-permute-done.v_ref), channel_id=1, source_target_pairs={{0,4},{4,8},{8,12},{12,0},{1,5},{5,9},{9,13},{13,1},{2,6},{6,10},{... | collective-permute-start | bytes 786440 | tf_op jit(solution)/shard_map/ppermute | solution.py:414
  18.7 13.2 %collective-permute-start.4 = (bf16[8,16,512]{2,1,0:T(8,128)(2,1)S(1)}, bf16[8,16,512]{2,1,0:T(8,128)(2,1)S(1)}, u32[]{:S(2)}, u32[]{:S(2)}) collective-permute-start(bf16[8,16,512]{2,1,0:T(8,128)(2,1)S(1)} %get-tuple-element.43), channel_id=1, source_target_pairs={{0,12},{4,0},{8,4},{12,8},{1,13},{5,1},{9,5},{13,9},{2,14},{6,2},{... | collective-permute-start | bytes 393224 | tf_op jit(solution)/shard_map/ppermute | solution.py:418

commit v5 on v4

--- a/solution.py
+++ b/solution.py
@@ -131,7 +131,7 @@
 
 
 def own_kernel(
-    pre, hops, lengths_ref, slot_ref, q_hbm, k_hbm, v_hbm,
+    pre, lengths_ref, slot_ref, q_hbm, k_hbm, v_hbm,
     q_ref, acc_ref, sum_ref, top_ref, cache_ref, *refs,
 ):
     sent_hbm, (k_ref, v_ref, turned, bias, sent, counts, sems, load_sems) = refs[:-8], refs[-8:]
@@ -157,8 +157,7 @@
         n = counts[owner]
         counts[owner] = n + 1
         distance = lax.rem(owner - me + pre, pre)
-        spare = (pre - 1 - hops) * per_peer
-        at = jnp.where(distance > hops, (distance - hops - 1) * per_peer + n, spare)
+        at = jnp.where(distance > 1, (distance - 2) * per_peer + n, (pre - 2) * per_peer)
         block = block_of(k_ref, v_ref, pl.multiple_of(b * BLK, BLK))
         sent[at] = block
         cache_ref[own_slot(slot, me, blocks)] = block
@@ -240,27 +239,40 @@
 def list_places(places_ref, slot_ref, hops, pre, blocks):
     me = lax.axis_index("pre")
     stride = blocks // pre + 1
-    for i, distance in enumerate(range(hops, pre)):
+    for distance in range(2, pre):
         source = lax.rem(me - distance + pre, pre)
 
         def step(b, n):
             at = own_slot(slot_ref[source * blocks + b], me, blocks)
-            places_ref[i * stride + n] = at
-            if i == 0:
-                places_ref[(pre - hops) * stride + n] = b
+            places_ref[(distance - 2) * stride + n] = at
+            if distance == hops:
+                places_ref[(pre - 2) * stride + n] = b
             return n + jnp.where(at < blocks, 1, 0)
 
         lax.fori_loop(0, blocks, step, jnp.int32(0), unroll=8)
 
 
-def place_listed(cache, places_ref, k_ref, v_ref, got_refs):
+def place_listed(cache, places_ref, hops, k_ref, v_ref, got_refs):
+    me = lax.axis_index("pre")
     per_peer = got_refs[0].shape[0]
     stride = per_peer + 1
-    for n in range(per_peer):
-        b = places_ref[(len(got_refs) + 1) * stride + n]
-        cache[places_ref[n]] = block_of(k_ref, v_ref, pl.multiple_of(b * BLK, BLK))
-        for i, got_ref in enumerate(got_refs):
-            cache[places_ref[(i + 1) * stride + n]] = got_ref[n]
+
+    def packed(distance):
+        for n in range(per_peer):
+            cache[places_ref[(distance - 2) * stride + n]] = got_refs[distance - 2][n]
+
+    def forwarded():
+        for n in range(per_peer):
+            b = places_ref[len(got_refs) * stride + n]
+            at = places_ref[(hops - 2) * stride + n]
+            cache[at] = block_of(k_ref, v_ref, pl.multiple_of(b * BLK, BLK))
+
+    for distance in range(2, len(got_refs) + 2):
+        if distance > hops:
+            packed(distance)
+        else:
+            pl.when(me < distance)(functools.partial(packed, distance))
+    pl.when(me >= hops)(forwarded)
 
 
 def values_kernel(
@@ -271,7 +283,7 @@
     refs = list(refs)
     if not first_out:
         refs.pop(0)
-    got_refs = [refs.pop(0) for _ in range(hops + 1, pre)] if last else []
+    got_refs = [refs.pop(0) for _ in range(2, pre)] if last else []
     out_hbm, cache_out = refs.pop(0), refs.pop(0)
     state = () if last else (refs.pop(0), refs.pop(0))
     places_ref = refs.pop(0) if first_out else None
@@ -284,9 +296,15 @@
     cache = rest[0] if last else cache_out
     cache[...] = cache_in[...]
     if last:
-        place_listed(cache, slot_ref, k_ref, v_ref, got_refs)
+        place_listed(cache, slot_ref, hops, k_ref, v_ref, got_refs)
+    elif first_out:
+        place_blocks(cache, slot_ref, k_ref, v_ref, hop, pre, blocks)
     else:
-        place_blocks(cache, slot_ref, k_ref, v_ref, hop, pre, blocks)
+
+        @pl.when(lax.axis_index("pre") >= hop)
+        def _():
+            place_blocks(cache, slot_ref, k_ref, v_ref, hop, pre, blocks)
+
     if first_out:
         list_places(places_ref, slot_ref, hops, pre, blocks)
     if last:
@@ -375,19 +393,19 @@
         pltpu.with_memory_space_constraint(x, pltpu.HBM) for x in (queries, new_keys, new_values)
     )
     q, acc, total, top, cache, *sent = pl.pallas_call(
-        functools.partial(own_kernel, pre, hops),
+        functools.partial(own_kernel, pre),
         out_shape=(attended_shape, acc_shape, stat_shape, stat_shape, open_cache)
-        + (packed,) * (pre - 1 - hops),
+        + (packed,) * (pre - 2),
         in_specs=[SMEM, SMEM] + [HBM] * 3,
-        out_specs=(VMEM,) * 5 + (HBM,) * (pre - 1 - hops),
+        out_specs=(VMEM,) * 5 + (HBM,) * (pre - 2),
         scratch_shapes=[
             pltpu.VMEM((rows, kv_width), bf16),
             pltpu.VMEM((rows, kv_width), bf16),
             turned,
             bias,
-            pltpu.VMEM(((pre - 1 - hops) * per_peer + 1, BLK, 2 * kv_width), bf16),
+            pltpu.VMEM(((pre - 2) * per_peer + 1, BLK, 2 * kv_width), bf16),
             pltpu.SMEM((pre,), jnp.int32),
-            pltpu.SemaphoreType.DMA((pre - 1 - hops,)),
+            pltpu.SemaphoreType.DMA((pre - 2,)),
             pltpu.SemaphoreType.DMA((3,)),
         ],
         cost_estimate=cost(1, 4),
@@ -399,7 +417,8 @@
     attended = None
     for hop in range(1, hops + 1):
         first_out, last = hop == 1, hop == hops
-        next_k = None if last else lax.ppermute(k, "pre", ring)
+        onward = [(i, i + 1) for i in range(hop, pre - 1)]
+        next_k = None if last else lax.ppermute(k, "pre", onward)
         weights, factor, *tops = pl.pallas_call(
             functools.partial(scores_kernel, hop),
             out_shape=(weights_shape, stat_shape) + (() if last else (stat_shape,)),
@@ -411,12 +430,13 @@
             name="scores",
         )(lengths, q, k, top)
         v = after(v, factor)
-        next_v = None if last else lax.ppermute(v, "pre", ring)
+        next_v = None if last else lax.ppermute(v, "pre", onward)
         if first_out:
-            for d in range(hops + 1, pre):
-                pairs = [(i, (i + d) % pre) for i in range(pre)]
-                got.append(lax.ppermute(after(sent[d - hops - 1], v), "pre", pairs))
-        places = shape(((pre - hops + 1) * (per_peer + 1),), jnp.int32)
+            for d in reversed(range(2, pre)):
+                targets = range(d if d <= hops else pre)
+                pairs = [((i - d) % pre, i) for i in targets]
+                got.insert(0, lax.ppermute(after(sent[d - 2], v), "pre", pairs))
+        places = shape(((pre - 1) * (per_peer + 1),), jnp.int32)
         carry = () if last else (acc_shape, stat_shape)
         extra = ([] if first_out else [attended]) + (got if last else [])
         attended, cache, *state = pl.pallas_call(

time: 33.7 us -> 32.1 us (0.953)
  waiting for transfers between devices: 11.8 us -> 4.7 us
  starting transfers between devices: 8.73 us -> 14 us
    ppermute x3 -> x4, waiting for transfers between devices: 5.66 us -> 0.01 us  [the longest x2 0.01 us: on_device(): got.insert(0, lax.ppermute(after(sent[d - 2], v), 'pre', pairs))]
    ppermute x3 -> x4, starting transfers between devices: 4.08 us -> 9.34 us  [the longest x2 8.01 us: on_device(): got.insert(0, lax.ppermute(after(sent[d - 2], v), 'pre', pairs))]
    ppermute x1, waiting for transfers between devices: 4.77 us -> 3.52 us  [on_device(): lax.ppermute(new_values, 'pre', ring)]
  transfers between devices with their start and end apart: 5 -> 6, of which waited for: 4 -> 2; matrix products, arithmetic and copies ran while one was open for 0% -> 0% of each run, Pallas kernels for 28% -> 30%
where the time goes in v5:
time: 32.1 us; the launch traced here: 31.9 us
  starting transfers between devices  14 us (44%)
  Pallas kernels  11 us (34%)
  waiting for transfers between devices  4.7 us (15%)
  local copies, waits for them, and re-layouts  1.31 us (4%)
  between operations  0.88 us (3%)
    ppermute x2, starting transfers between devices, on_device(): got.insert(0, lax.ppermute(after(sent[d - 2], v), 'pre', pairs))  8.01 us
    pallas_call x1, Pallas kernels, on_device(): pl.pallas_call(functools.partial(own_kernel, pre), out_shape=(attended_sh...  5.3 us
    pallas_call x2, Pallas kernels, on_device(): pl.pallas_call(functools.partial(values_kernel, hop, hops, pre), out_shap...  4.36 us
    ppermute x1, waiting for transfers between devices, on_device(): lax.ppermute(new_values, 'pre', ring)  3.52 us
    ppermute x1, starting transfers between devices, on_device(): lax.ppermute(new_keys, 'pre', ring)  3.08 us
    ppermute x1, starting transfers between devices, on_device(): lax.ppermute(new_values, 'pre', ring)  1.58 us
    pallas_call x2, Pallas kernels, on_device(): pl.pallas_call(functools.partial(scores_kernel, hop), out_shape=(weights_...  1.36 us
    unnamed x4, local copies, waits for them, and re-layouts  1.31 us
  transfers between devices with their start and end apart: 6, of which 2 were waited for; matrix products, arithmetic and copies ran while one was open for 0% of the time, Pallas kernels for 30%

profile of v5, /device:TPU:0, one launch (start us, length us, event | category | flops | bytes accessed | tf_op | source)
XLA Modules:
  0.0 31.9 jit_solution(8820260762142374642)
XLA Ops:
  0.6 3.1 %collective-permute-start.1 = (bf16[512,256]{1,0:T(8,128)(2,1)}, bf16[512,256]{1,0:T(8,128)(2,1)S(1)}, u32[]{:S(2)}, u32[]{:S(2)}) collective-permute-start(bf16[512,256]{1,0:T(8,128)(2,1)} %k_hbm.1), channel_id=1, source_target_pairs={{0,4},{4,8},{8,12},{12,0},{1,5},{5,9},{9,13},{13,1},{2,6},{6,10},{... | collective-permute-start | bytes 786440 | tf_op jit(solution)/shard_map/ppermute | solution.py:389
  3.7 1.6 %collective-permute-start = (bf16[512,256]{1,0:T(8,128)(2,1)}, bf16[512,256]{1,0:T(8,128)(2,1)S(1)}, u32[]{:S(2)}, u32[]{:S(2)}) collective-permute-start(bf16[512,256]{1,0:T(8,128)(2,1)} %v_hbm.1), channel_id=1, source_target_pairs={{0,4},{4,8},{8,12},{12,0},{1,5},{5,9},{9,13},{13,1},{2,6},{6,10},{... | collective-permute-start | bytes 786440 | tf_op jit(solution)/shard_map/ppermute | solution.py:389
  5.3 0.0 copy-start
  5.3 0.7 %copy-done = s32[4]{0:T(128)S(1)} copy-done((s32[4]{0:T(128)S(1)}, s32[4]{0:T(128)}, u32[]{:S(2)}) %copy-start) | copy-done | bytes 40
  5.9 0.0 copy-start.1
  5.9 0.7 %copy-done.1 = s32[128]{0:T(128)S(1)} copy-done((s32[128]{0:T(128)S(1)}, s32[128]{0:T(128)}, u32[]{:S(2)}) %copy-start.1) | copy-done | bytes 536
  6.6 5.3 %own_attention.1 = (bf16[512,1024]{1,0:T(8,128)(2,1)S(1)}, f32[2,128,2048]{2,1,0:T(8,128)S(1)}, f32[2,8,2048]{2,1,0:T(8,128)S(1)}, f32[2,8,2048]{2,1,0:T(8,128)S...) custom-call(s32[4]{0:T(128)S(1)} %copy-done, ...), custom_call_target="tpu_custom_call" | custom-call | flops 1073741824 | bytes 4194304 | tf_op jit(solution)/shard_map/own_attention/pallas_call | solution.py:395
  11.9 1.2 %collective-permute-done.1.k_ref = bf16[512,256]{1,0:T(8,128)(2,1)S(1)} collective-permute-done((bf16[512,256]{1,0:T(8,128)(2,1)}, bf16[512,256]{1,0:T(8,128)(2,1)S(1)}, u32[]{:S(2)}, u32[]{:S(2)}) %collective-permute-start.1) | collective-permute-done | bytes 262176 | tf_op jit(solution)/shard_map/ppermute | solution.py:389
  13.1 0.7 %collective-permute-start.3 = (bf16[512,256]{1,0:T(8,128)(2,1)S(1)}, bf16[512,256]{1,0:T(8,128)(2,1)S(1)}, u32[]{:S(2)}, u32[]{:S(2)}) collective-permute-start(bf16[512,256]{1,0:T(8,128)(2,1)S(1)} %collective-permute-done.1.k_ref), channel_id=1, source_target_pairs={{4,8},{8,12},{5,9},{9,13},{6,10},{10,14},{7,11},{11,15},{20,24},{2... | collective-permute-start | bytes 786440 | tf_op jit(solution)/shard_map/ppermute | solution.py:421
  13.8 0.6 %scores.2 = (bf16[2,2,512,1024]{3,2,1,0:T(8,128)(2,1)S(1)}, f32[2,8,2048]{2,1,0:T(8,128)S(1)}, f32[2,8,2048]{2,1,0:T(8,128)S(1)}) custom-call(s32[4]{0:T(128)S(1)} %copy-done, bf16[512,1024]{1,0:T(8,128)(2,1)S(1)} %get-tuple-element.25.q_ref, bf16[512,256]{1,0:T(8,128)(2,1)S(1)} %collective-permute-done.1.k_ref, f32[2,8,2048]{2,1,0:T(8,128)S(1)} %get-tuple-element.26.old_top), custom_call_target="tpu_custom_call" | custom-call | flops 536870912 | bytes 3145728 | tf_op jit(solution)/shard_map/scores/pallas_call | solution.py:422
  14.3 3.5 %collective-permute-done.v_ref = bf16[512,256]{1,0:T(8,128)(2,1)S(1)} collective-permute-done((bf16[512,256]{1,0:T(8,128)(2,1)}, bf16[512,256]{1,0:T(8,128)(2,1)S(1)}, u32[]{:S(2)}, u32[]{:S(2)}) %collective-permute-start) | collective-permute-done | bytes 262176 | tf_op jit(solution)/shard_map/ppermute | solution.py:389
  17.9 0.7 %collective-permute-start.2 = (bf16[512,256]{1,0:T(8,128)(2,1)S(1)}, bf16[512,256]{1,0:T(8,128)(2,1)S(1)}, u32[]{:S(2)}, u32[]{:S(2)}) collective-permute-start(bf16[512,256]{1,0:T(8,128)(2,1)S(1)} %collective-permute-done.v_ref), channel_id=1, source_target_pairs={{4,8},{8,12},{5,9},{9,13},{6,10},{10,14},{7,11},{11,15},{20,24},{2... | collective-permute-start | bytes 786440 | tf_op jit(solution)/shard_map/ppermute | solution.py:433
  18.5 1.3 %collective-permute-start.4 = (bf16[8,16,512]{2,1,0:T(8,128)(2,1)S(1)}, bf16[8,16,512]{2,1,0:T(8,128)(2,1)S(1)}, u32[]{:S(2)}, u32[]{:S(2)}) collective-permute-start(bf16[8,16,512]{2,1,0:T(8,128)(2,1)S(1)} %get-tuple-element.45), channel_id=1, source_target_pairs={{8,0},{12,4},{9,1},{13,5},{10,2},{14,6},{11,3},{15,7},{24,16},{28,... | collective-permute-start | bytes 393224 | tf_op jit(solution)/shard_map/ppermute | solution.py:438
  19.8 6.7 %collective-permute-start.5 = (bf16[8,16,512]{2,1,0:T(8,128)(2,1)S(1)}, bf16[8,16,512]{2,1,0:T(8,128)(2,1)S(1)}, u32[]{:S(2)}, u32[]{:S(2)}) collective-permute-start(bf16[8,16,512]{2,1,0:T(8,128)(2,1)S(1)} %get-tuple-element.47), channel_id=1, source_target_pairs={{4,0},{8,4},{12,8},{0,12},{5,1},{9,5},{13,9},{1,13},{6,2},{10,6},{... | collective-permute-start | bytes 393224 | tf_op jit(solution)/shard_map/ppermute | solution.py:438
  26.6 2.9 %values.2 = (bf16[512,1024]{1,0:T(8,128)(2,1)}, bf16[33,16,512]{2,1,0:T(8,128)(2,1)S(1)}, f32[2,128,2048]{2,1,0:T(8,128)S(1)}, f32[2,8,2048]{2,1,0:T(8,128)S(1)}, s32[27]{0:T(128)S(1)}) custom-call(s32[4]{0:T(128)S(1)} %copy-done, s32[128]{0:T(128)S(1)} %copy-done.1, bf16[512,256]{1,0:T(8,128)(2,1)S(1)} %collective-permute-done.v_ref, ...), custom_call_target="tpu_custom_call" | custom-call | flops 536870912 | bytes 3145728 | tf_op jit(solution)/shard_map/values/pallas_call | solution.py:442
  29.5 0.0 collective-permute-done.3.k_ref
  29.5 0.8 %scores.3 = (bf16[2,2,512,1024]{3,2,1,0:T(8,128)(2,1)S(1)}, f32[2,8,2048]{2,1,0:T(8,128)S(1)}) custom-call(s32[4]{0:T(128)S(1)} %copy-done, bf16[512,1024]{1,0:T(8,128)(2,1)S(1)} %get-tuple-element.25.q_ref, bf16[512,256]{1,0:T(8,128)(2,1)S(1)} %collective-permute-done.3.k_ref, f32[2,8,2048]{2,1,0:T(8,128)S(1)} %get-tuple-element.37.old_top), custom_call_target="tpu_custom_call" | custom-call | flops 536870912 | bytes 3145728 | tf_op jit(solution)/shard_map/scores/pallas_call | solution.py:422
  30.3 0.0 collective-permute-done.2.v_ref
  30.3 0.0 collective-permute-done.4.refs_1_
  30.3 0.0 collective-permute-done.5.refs_2_
  30.3 1.4 %values.3 = (bf16[512,1024]{1,0:T(8,128)(2,1)}, bf16[32,16,512]{2,1,0:T(8,128)(2,1)}) custom-call(s32[4]{0:T(128)S(1)} %copy-done, s32[27]{0:T(128)S(1)} %get-tuple-element.34.slot_ref, bf16[512,256]{1,0:T(8,128)(2,1)S(1)} %collective-permute-done.2.v_ref, bf16[512,256]{1,0:T(8,128)(2,1)S(1)} %collective-permute-done.3.k_ref, ...), custom_call_target="tpu_custom_call", output_to_operand_aliasing={{0}: (9, {})} | custom-call | flops 536870912 | bytes 3145728 | tf_op jit(solution)/shard_map/values/pallas_call | solution.py:442
Async XLA Ops:
  0.6 12.4 %collective-permute-start.1 = (bf16[512,256]{1,0:T(8,128)(2,1)}, bf16[512,256]{1,0:T(8,128)(2,1)S(1)}, u32[]{:S(2)}, u32[]{:S(2)}) collective-permute-start(bf16[512,256]{1,0:T(8,128)(2,1)} %k_hbm.1), channel_id=1, source_target_pairs={{0,4},{4,8},{8,12},{12,0},{1,5},{5,9},{9,13},{13,1},{2,6},{6,10},{... | collective-permute-start | bytes 786440 | tf_op jit(solution)/shard_map/ppermute | solution.py:389
  3.7 14.2 %collective-permute-start = (bf16[512,256]{1,0:T(8,128)(2,1)}, bf16[512,256]{1,0:T(8,128)(2,1)S(1)}, u32[]{:S(2)}, u32[]{:S(2)}) collective-permute-start(bf16[512,256]{1,0:T(8,128)(2,1)} %v_hbm.1), channel_id=1, source_target_pairs={{0,4},{4,8},{8,12},{12,0},{1,5},{5,9},{9,13},{13,1},{2,6},{6,10},{... | collective-permute-start | bytes 786440 | tf_op jit(solution)/shard_map/ppermute | solution.py:389
  5.3 0.7 %copy-start = (s32[4]{0:T(128)S(1)}, s32[4]{0:T(128)}, u32[]{:S(2)}) copy-start(s32[4]{0:T(128)} %lengths_ref.9) | copy-start | bytes 52
  5.9 0.7 %copy-start.1 = (s32[128]{0:T(128)S(1)}, s32[128]{0:T(128)}, u32[]{:S(2)}) copy-start(s32[128]{0:T(128)} %slot_ref.3) | copy-start | bytes 1540
  13.1 16.4 %collective-permute-start.3 = (bf16[512,256]{1,0:T(8,128)(2,1)S(1)}, bf16[512,256]{1,0:T(8,128)(2,1)S(1)}, u32[]{:S(2)}, u32[]{:S(2)}) collective-permute-start(bf16[512,256]{1,0:T(8,128)(2,1)S(1)} %collective-permute-done.1.k_ref), channel_id=1, source_target_pairs={{4,8},{8,12},{5,9},{9,13},{6,10},{10,14},{7,11},{11,15},{20,24},{2... | collective-permute-start | bytes 786440 | tf_op jit(solution)/shard_map/ppermute | solution.py:421
  17.9 12.4 %collective-permute-start.2 = (bf16[512,256]{1,0:T(8,128)(2,1)S(1)}, bf16[512,256]{1,0:T(8,128)(2,1)S(1)}, u32[]{:S(2)}, u32[]{:S(2)}) collective-permute-start(bf16[512,256]{1,0:T(8,128)(2,1)S(1)} %collective-permute-done.v_ref), channel_id=1, source_target_pairs={{4,8},{8,12},{5,9},{9,13},{6,10},{10,14},{7,11},{11,15},{20,24},{2... | collective-permute-start | bytes 786440 | tf_op jit(solution)/shard_map/ppermute | solution.py:433
  18.5 11.8 %collective-permute-start.4 = (bf16[8,16,512]{2,1,0:T(8,128)(2,1)S(1)}, bf16[8,16,512]{2,1,0:T(8,128)(2,1)S(1)}, u32[]{:S(2)}, u32[]{:S(2)}) collective-permute-start(bf16[8,16,512]{2,1,0:T(8,128)(2,1)S(1)} %get-tuple-element.45), channel_id=1, source_target_pairs={{8,0},{12,4},{9,1},{13,5},{10,2},{14,6},{11,3},{15,7},{24,16},{28,... | collective-permute-start | bytes 393224 | tf_op jit(solution)/shard_map/ppermute | solution.py:438
  19.8 10.5 %collective-permute-start.5 = (bf16[8,16,512]{2,1,0:T(8,128)(2,1)S(1)}, bf16[8,16,512]{2,1,0:T(8,128)(2,1)S(1)}, u32[]{:S(2)}, u32[]{:S(2)}) collective-permute-start(bf16[8,16,512]{2,1,0:T(8,128)(2,1)S(1)} %get-tuple-element.47), channel_id=1, source_target_pairs={{4,0},{8,4},{12,8},{0,12},{5,1},{9,5},{13,9},{1,13},{6,2},{10,6},{... | collective-permute-start | bytes 393224 | tf_op jit(solution)/shard_map/ppermute | solution.py:438

commit v6 on v5

--- a/solution.py
+++ b/solution.py
@@ -283,7 +283,7 @@
     refs = list(refs)
     if not first_out:
         refs.pop(0)
-    got_refs = [refs.pop(0) for _ in range(2, pre)] if last else []
+    got_refs = [refs.pop(0) for _ in range(2, pre)][::-1] if last else []
     out_hbm, cache_out = refs.pop(0), refs.pop(0)
     state = () if last else (refs.pop(0), refs.pop(0))
     places_ref = refs.pop(0) if first_out else None
@@ -438,7 +438,7 @@
                 got.insert(0, lax.ppermute(after(sent[d - 2], v), "pre", pairs))
         places = shape(((pre - 1) * (per_peer + 1),), jnp.int32)
         carry = () if last else (acc_shape, stat_shape)
-        extra = ([] if first_out else [attended]) + (got if last else [])
+        extra = ([] if first_out else [attended]) + (got[::-1] if last else [])
         attended, cache, *state = pl.pallas_call(
             functools.partial(values_kernel, hop, hops, pre),
             out_shape=(attended_shape, cache_shape if last else open_cache)

time: 32.1 us -> 33.5 us (1.044)
  waiting for transfers between devices: 4.7 us -> 9.3 us
  starting transfers between devices: 14 us -> 10.8 us
    ppermute x2, waiting for transfers between devices: 0.01 us -> 4.6 us  [on_device(): got.insert(0, lax.ppermute(after(sent[d - 2], v), 'pre', pairs))]
    ppermute x2, starting transfers between devices: 8.01 us -> 4.83 us  [on_device(): got.insert(0, lax.ppermute(after(sent[d - 2], v), 'pre', pairs))]
  transfers between devices with their start and end apart: 6 -> 6, of which waited for: 2 -> 3; matrix products, arithmetic and copies ran while one was open for 0% -> 0% of each run, Pallas kernels for 30% -> 29%
where the time goes in v6:
time: 33.5 us; the launch traced here: 33.3 us
  Pallas kernels  11 us (33%)
  starting transfers between devices  10.8 us (32%)
  waiting for transfers between devices  9.3 us (28%)
  local copies, waits for them, and re-layouts  1.31 us (4%)
  between operations  0.88 us (3%)
    pallas_call x1, Pallas kernels, on_device(): pl.pallas_call(functools.partial(own_kernel, pre), out_shape=(attended_sh...  5.3 us
    ppermute x2, starting transfers between devices, on_device(): got.insert(0, lax.ppermute(after(sent[d - 2], v), 'pre', pairs))  4.83 us
    ppermute x2, waiting for transfers between devices, on_device(): got.insert(0, lax.ppermute(after(sent[d - 2], v), 'pre', pairs))  4.6 us
    pallas_call x2, Pallas kernels, on_device(): pl.pallas_call(functools.partial(values_kernel, hop, hops, pre), out_shap...  4.36 us
    ppermute x1, waiting for transfers between devices, on_device(): lax.ppermute(new_values, 'pre', ring)  3.52 us
    ppermute x1, starting transfers between devices, on_device(): lax.ppermute(new_keys, 'pre', ring)  3.08 us
    ppermute x1, starting transfers between devices, on_device(): lax.ppermute(new_values, 'pre', ring)  1.58 us
    pallas_call x2, Pallas kernels, on_device(): pl.pallas_call(functools.partial(scores_kernel, hop), out_shape=(weights_...  1.36 us
  transfers between devices with their start and end apart: 6, of which 3 were waited for; matrix products, arithmetic and copies ran while one was open for 0% of the time, Pallas kernels for 29%

profile of v6, /device:TPU:0, one launch (start us, length us, event | category | flops | bytes accessed | tf_op | source)
XLA Modules:
  0.0 33.3 jit_solution(14994791441814300593)
XLA Ops:
  0.6 3.1 %collective-permute-start.1 = (bf16[512,256]{1,0:T(8,128)(2,1)}, bf16[512,256]{1,0:T(8,128)(2,1)S(1)}, u32[]{:S(2)}, u32[]{:S(2)}) collective-permute-start(bf16[512,256]{1,0:T(8,128)(2,1)} %k_hbm.1), channel_id=1, source_target_pairs={{0,4},{4,8},{8,12},{12,0},{1,5},{5,9},{9,13},{13,1},{2,6},{6,10},{... | collective-permute-start | bytes 786440 | tf_op jit(solution)/shard_map/ppermute | solution.py:389
  3.7 1.6 %collective-permute-start = (bf16[512,256]{1,0:T(8,128)(2,1)}, bf16[512,256]{1,0:T(8,128)(2,1)S(1)}, u32[]{:S(2)}, u32[]{:S(2)}) collective-permute-start(bf16[512,256]{1,0:T(8,128)(2,1)} %v_hbm.1), channel_id=1, source_target_pairs={{0,4},{4,8},{8,12},{12,0},{1,5},{5,9},{9,13},{13,1},{2,6},{6,10},{... | collective-permute-start | bytes 786440 | tf_op jit(solution)/shard_map/ppermute | solution.py:389
  5.3 0.0 copy-start
  5.3 0.7 %copy-done = s32[4]{0:T(128)S(1)} copy-done((s32[4]{0:T(128)S(1)}, s32[4]{0:T(128)}, u32[]{:S(2)}) %copy-start) | copy-done | bytes 40
  5.9 0.0 copy-start.1
  5.9 0.7 %copy-done.1 = s32[128]{0:T(128)S(1)} copy-done((s32[128]{0:T(128)S(1)}, s32[128]{0:T(128)}, u32[]{:S(2)}) %copy-start.1) | copy-done | bytes 536
  6.6 5.3 %own_attention.1 = (bf16[512,1024]{1,0:T(8,128)(2,1)S(1)}, f32[2,128,2048]{2,1,0:T(8,128)S(1)}, f32[2,8,2048]{2,1,0:T(8,128)S(1)}, f32[2,8,2048]{2,1,0:T(8,128)S...) custom-call(s32[4]{0:T(128)S(1)} %copy-done, ...), custom_call_target="tpu_custom_call" | custom-call | flops 1073741824 | bytes 4194304 | tf_op jit(solution)/shard_map/own_attention/pallas_call | solution.py:395
  11.9 1.2 %collective-permute-done.1.k_ref = bf16[512,256]{1,0:T(8,128)(2,1)S(1)} collective-permute-done((bf16[512,256]{1,0:T(8,128)(2,1)}, bf16[512,256]{1,0:T(8,128)(2,1)S(1)}, u32[]{:S(2)}, u32[]{:S(2)}) %collective-permute-start.1) | collective-permute-done | bytes 262176 | tf_op jit(solution)/shard_map/ppermute | solution.py:389
  13.1 0.7 %collective-permute-start.3 = (bf16[512,256]{1,0:T(8,128)(2,1)S(1)}, bf16[512,256]{1,0:T(8,128)(2,1)S(1)}, u32[]{:S(2)}, u32[]{:S(2)}) collective-permute-start(bf16[512,256]{1,0:T(8,128)(2,1)S(1)} %collective-permute-done.1.k_ref), channel_id=1, source_target_pairs={{4,8},{8,12},{5,9},{9,13},{6,10},{10,14},{7,11},{11,15},{20,24},{2... | collective-permute-start | bytes 786440 | tf_op jit(solution)/shard_map/ppermute | solution.py:421
  13.8 0.6 %scores.2 = (bf16[2,2,512,1024]{3,2,1,0:T(8,128)(2,1)S(1)}, f32[2,8,2048]{2,1,0:T(8,128)S(1)}, f32[2,8,2048]{2,1,0:T(8,128)S(1)}) custom-call(s32[4]{0:T(128)S(1)} %copy-done, bf16[512,1024]{1,0:T(8,128)(2,1)S(1)} %get-tuple-element.25.q_ref, bf16[512,256]{1,0:T(8,128)(2,1)S(1)} %collective-permute-done.1.k_ref, f32[2,8,2048]{2,1,0:T(8,128)S(1)} %get-tuple-element.26.old_top), custom_call_target="tpu_custom_call" | custom-call | flops 536870912 | bytes 3145728 | tf_op jit(solution)/shard_map/scores/pallas_call | solution.py:422
  14.3 3.5 %collective-permute-done.v_ref = bf16[512,256]{1,0:T(8,128)(2,1)S(1)} collective-permute-done((bf16[512,256]{1,0:T(8,128)(2,1)}, bf16[512,256]{1,0:T(8,128)(2,1)S(1)}, u32[]{:S(2)}, u32[]{:S(2)}) %collective-permute-start) | collective-permute-done | bytes 262176 | tf_op jit(solution)/shard_map/ppermute | solution.py:389
  17.9 0.7 %collective-permute-start.2 = (bf16[512,256]{1,0:T(8,128)(2,1)S(1)}, bf16[512,256]{1,0:T(8,128)(2,1)S(1)}, u32[]{:S(2)}, u32[]{:S(2)}) collective-permute-start(bf16[512,256]{1,0:T(8,128)(2,1)S(1)} %collective-permute-done.v_ref), channel_id=1, source_target_pairs={{4,8},{8,12},{5,9},{9,13},{6,10},{10,14},{7,11},{11,15},{20,24},{2... | collective-permute-start | bytes 786440 | tf_op jit(solution)/shard_map/ppermute | solution.py:433
  18.5 3.6 %collective-permute-start.4 = (bf16[8,16,512]{2,1,0:T(8,128)(2,1)S(1)}, bf16[8,16,512]{2,1,0:T(8,128)(2,1)S(1)}, u32[]{:S(2)}, u32[]{:S(2)}) collective-permute-start(bf16[8,16,512]{2,1,0:T(8,128)(2,1)S(1)} %get-tuple-element.45), channel_id=1, source_target_pairs={{4,0},{8,4},{12,8},{0,12},{5,1},{9,5},{13,9},{1,13},{6,2},{10,6},{... | collective-permute-start | bytes 393224 | tf_op jit(solution)/shard_map/ppermute | solution.py:438
  22.1 1.3 %collective-permute-start.5 = (bf16[8,16,512]{2,1,0:T(8,128)(2,1)S(1)}, bf16[8,16,512]{2,1,0:T(8,128)(2,1)S(1)}, u32[]{:S(2)}, u32[]{:S(2)}) collective-permute-start(bf16[8,16,512]{2,1,0:T(8,128)(2,1)S(1)} %get-tuple-element.47), channel_id=1, source_target_pairs={{8,0},{12,4},{9,1},{13,5},{10,2},{14,6},{11,3},{15,7},{24,16},{28,... | collective-permute-start | bytes 393224 | tf_op jit(solution)/shard_map/ppermute | solution.py:438
  23.4 2.9 %values.2 = (bf16[512,1024]{1,0:T(8,128)(2,1)}, bf16[33,16,512]{2,1,0:T(8,128)(2,1)S(1)}, f32[2,128,2048]{2,1,0:T(8,128)S(1)}, f32[2,8,2048]{2,1,0:T(8,128)S(1)}, s32[27]{0:T(128)S(1)}) custom-call(s32[4]{0:T(128)S(1)} %copy-done, s32[128]{0:T(128)S(1)} %copy-done.1, bf16[512,256]{1,0:T(8,128)(2,1)S(1)} %collective-permute-done.v_ref, ...), custom_call_target="tpu_custom_call" | custom-call | flops 536870912 | bytes 3145728 | tf_op jit(solution)/shard_map/values/pallas_call | solution.py:442
  26.3 0.0 collective-permute-done.3.k_ref
  26.3 0.8 %scores.3 = (bf16[2,2,512,1024]{3,2,1,0:T(8,128)(2,1)S(1)}, f32[2,8,2048]{2,1,0:T(8,128)S(1)}) custom-call(s32[4]{0:T(128)S(1)} %copy-done, bf16[512,1024]{1,0:T(8,128)(2,1)S(1)} %get-tuple-element.25.q_ref, bf16[512,256]{1,0:T(8,128)(2,1)S(1)} %collective-permute-done.3.k_ref, f32[2,8,2048]{2,1,0:T(8,128)S(1)} %get-tuple-element.37.old_top), custom_call_target="tpu_custom_call" | custom-call | flops 536870912 | bytes 3145728 | tf_op jit(solution)/shard_map/scores/pallas_call | solution.py:422
  27.1 0.0 collective-permute-done.2.v_ref
  27.1 0.0 collective-permute-done.4.refs_1_
  27.1 4.6 %collective-permute-done.5.refs_2_ = bf16[8,16,512]{2,1,0:T(8,128)(2,1)S(1)} collective-permute-done((bf16[8,16,512]{2,1,0:T(8,128)(2,1)S(1)}, bf16[8,16,512]{2,1,0:T(8,128)(2,1)S(1)}, u32[]{:S(2)}, u32[]{:S(2)}) %collective-permute-start.5) | collective-permute-done | bytes 131104 | tf_op jit(solution)/shard_map/ppermute | solution.py:438
  31.7 1.4 %values.3 = (bf16[512,1024]{1,0:T(8,128)(2,1)}, bf16[32,16,512]{2,1,0:T(8,128)(2,1)}) custom-call(s32[4]{0:T(128)S(1)} %copy-done, s32[27]{0:T(128)S(1)} %get-tuple-element.34.slot_ref, bf16[512,256]{1,0:T(8,128)(2,1)S(1)} %collective-permute-done.2.v_ref, bf16[512,256]{1,0:T(8,128)(2,1)S(1)} %collective-permute-done.3.k_ref, ...), custom_call_target="tpu_custom_call", output_to_operand_aliasing={{0}: (9, {})} | custom-call | flops 536870912 | bytes 3145728 | tf_op jit(solution)/shard_map/values/pallas_call | solution.py:442
Async XLA Ops:
  0.6 12.4 %collective-permute-start.1 = (bf16[512,256]{1,0:T(8,128)(2,1)}, bf16[512,256]{1,0:T(8,128)(2,1)S(1)}, u32[]{:S(2)}, u32[]{:S(2)}) collective-permute-start(bf16[512,256]{1,0:T(8,128)(2,1)} %k_hbm.1), channel_id=1, source_target_pairs={{0,4},{4,8},{8,12},{12,0},{1,5},{5,9},{9,13},{13,1},{2,6},{6,10},{... | collective-permute-start | bytes 786440 | tf_op jit(solution)/shard_map/ppermute | solution.py:389
  3.7 14.2 %collective-permute-start = (bf16[512,256]{1,0:T(8,128)(2,1)}, bf16[512,256]{1,0:T(8,128)(2,1)S(1)}, u32[]{:S(2)}, u32[]{:S(2)}) collective-permute-start(bf16[512,256]{1,0:T(8,128)(2,1)} %v_hbm.1), channel_id=1, source_target_pairs={{0,4},{4,8},{8,12},{12,0},{1,5},{5,9},{9,13},{13,1},{2,6},{6,10},{... | collective-permute-start | bytes 786440 | tf_op jit(solution)/shard_map/ppermute | solution.py:389
  5.3 0.7 %copy-start = (s32[4]{0:T(128)S(1)}, s32[4]{0:T(128)}, u32[]{:S(2)}) copy-start(s32[4]{0:T(128)} %lengths_ref.9) | copy-start | bytes 52
  5.9 0.7 %copy-start.1 = (s32[128]{0:T(128)S(1)}, s32[128]{0:T(128)}, u32[]{:S(2)}) copy-start(s32[128]{0:T(128)} %slot_ref.3) | copy-start | bytes 1540
  13.1 13.3 %collective-permute-start.3 = (bf16[512,256]{1,0:T(8,128)(2,1)S(1)}, bf16[512,256]{1,0:T(8,128)(2,1)S(1)}, u32[]{:S(2)}, u32[]{:S(2)}) collective-permute-start(bf16[512,256]{1,0:T(8,128)(2,1)S(1)} %collective-permute-done.1.k_ref), channel_id=1, source_target_pairs={{4,8},{8,12},{5,9},{9,13},{6,10},{10,14},{7,11},{11,15},{20,24},{2... | collective-permute-start | bytes 786440 | tf_op jit(solution)/shard_map/ppermute | solution.py:421
  17.9 9.3 %collective-permute-start.2 = (bf16[512,256]{1,0:T(8,128)(2,1)S(1)}, bf16[512,256]{1,0:T(8,128)(2,1)S(1)}, u32[]{:S(2)}, u32[]{:S(2)}) collective-permute-start(bf16[512,256]{1,0:T(8,128)(2,1)S(1)} %collective-permute-done.v_ref), channel_id=1, source_target_pairs={{4,8},{8,12},{5,9},{9,13},{6,10},{10,14},{7,11},{11,15},{20,24},{2... | collective-permute-start | bytes 786440 | tf_op jit(solution)/shard_map/ppermute | solution.py:433
  18.5 8.6 %collective-permute-start.4 = (bf16[8,16,512]{2,1,0:T(8,128)(2,1)S(1)}, bf16[8,16,512]{2,1,0:T(8,128)(2,1)S(1)}, u32[]{:S(2)}, u32[]{:S(2)}) collective-permute-start(bf16[8,16,512]{2,1,0:T(8,128)(2,1)S(1)} %get-tuple-element.45), channel_id=1, source_target_pairs={{4,0},{8,4},{12,8},{0,12},{5,1},{9,5},{13,9},{1,13},{6,2},{10,6},{... | collective-permute-start | bytes 393224 | tf_op jit(solution)/shard_map/ppermute | solution.py:438
  22.1 9.6 %collective-permute-start.5 = (bf16[8,16,512]{2,1,0:T(8,128)(2,1)S(1)}, bf16[8,16,512]{2,1,0:T(8,128)(2,1)S(1)}, u32[]{:S(2)}, u32[]{:S(2)}) collective-permute-start(bf16[8,16,512]{2,1,0:T(8,128)(2,1)S(1)} %get-tuple-element.47), channel_id=1, source_target_pairs={{8,0},{12,4},{9,1},{13,5},{10,2},{14,6},{11,3},{15,7},{24,16},{28,... | collective-permute-start | bytes 393224 | tf_op jit(solution)/shard_map/ppermute | solution.py:438

commit v7 on v4

--- a/solution.py
+++ b/solution.py
@@ -130,11 +130,28 @@
     return jnp.where((local >= 0) & (local < blocks), local, blocks)
 
 
+def list_places(places_ref, slot_ref, hops, pre, blocks):
+    me = lax.axis_index("pre")
+    stride = blocks // pre + 1
+    for distance in range(2, pre):
+        source = lax.rem(me - distance + pre, pre)
+
+        def step(b, n):
+            at = own_slot(slot_ref[source * blocks + b], me, blocks)
+            places_ref[(distance - 2) * stride + n] = at
+            if distance <= hops:
+                places_ref[(pre - 2 + distance - 2) * stride + n] = b
+            return n + jnp.where(at < blocks, 1, 0)
+
+        lax.fori_loop(0, blocks, step, jnp.int32(0), unroll=8)
+
+
 def own_kernel(
     pre, hops, lengths_ref, slot_ref, q_hbm, k_hbm, v_hbm,
-    q_ref, acc_ref, sum_ref, top_ref, cache_ref, *refs,
+    q_ref, acc_ref, sum_ref, top_ref, cache_ref, places_ref, *refs,
 ):
-    sent_hbm, (k_ref, v_ref, turned, bias, sent, counts, sems, load_sems) = refs[:-8], refs[-8:]
+    sent_hbm, refs = refs[: pre - 2], refs[pre - 2 :]
+    k_ref, v_ref, turned, bias, sent_values, sent, counts, sems, load_sems = refs
     loads = [
         pltpu.make_async_copy(src, dst, load_sems.at[n])
         for n, (src, dst) in enumerate(((k_hbm, k_ref), (v_hbm, v_ref), (q_hbm, q_ref)))
@@ -148,6 +165,7 @@
     first = me * rows
     for owner in range(pre):
         counts[owner] = 0
+    list_places(places_ref, slot_ref, hops, pre, blocks)
     loads[0].wait()
     loads[1].wait()
 
@@ -157,17 +175,23 @@
         n = counts[owner]
         counts[owner] = n + 1
         distance = lax.rem(owner - me + pre, pre)
-        spare = (pre - 1 - hops) * per_peer
-        at = jnp.where(distance > hops, (distance - hops - 1) * per_peer + n, spare)
-        block = block_of(k_ref, v_ref, pl.multiple_of(b * BLK, BLK))
+        row = pl.multiple_of(b * BLK, BLK)
+        on_ring = (distance > 1) & (distance <= hops)
+        at = jnp.where(on_ring, (distance - 2) * per_peer + n, (hops - 1) * per_peer)
+        sent_values[at] = v_ref[pl.ds(row, BLK)]
+        beyond = (distance - hops - 1) * per_peer + n
+        at = jnp.where(distance > hops, beyond, (pre - 1 - hops) * per_peer)
+        block = block_of(k_ref, v_ref, row)
         sent[at] = block
         cache_ref[own_slot(slot, me, blocks)] = block
         return 0
 
-    lax.fori_loop(0, blocks, step, 0, unroll=8)
+    lax.fori_loop(0, blocks, step, 0, unroll=4)
+    packed = [sent_values.at[n * per_peer : (n + 1) * per_peer] for n in range(hops - 1)]
+    packed += [sent.at[n * per_peer : (n + 1) * per_peer] for n in range(pre - 1 - hops)]
     stores = [
-        pltpu.make_async_copy(sent.at[n * per_peer : (n + 1) * per_peer], ref, sems.at[n])
-        for n, ref in enumerate(sent_hbm)
+        pltpu.make_async_copy(src, dst, sems.at[n])
+        for n, (src, dst) in enumerate(zip(packed, sent_hbm))
     ]
     for store in stores:
         store.start()
@@ -237,30 +261,31 @@
     lax.fori_loop(0, blocks, step, 0, unroll=8)
 
 
-def list_places(places_ref, slot_ref, hops, pre, blocks):
+def place_listed(cache, places_ref, hop, pre, k_ref, v_ref, got_ref):
     me = lax.axis_index("pre")
-    stride = blocks // pre + 1
-    for i, distance in enumerate(range(hops, pre)):
-        source = lax.rem(me - distance + pre, pre)
-
-        def step(b, n):
-            at = own_slot(slot_ref[source * blocks + b], me, blocks)
-            places_ref[i * stride + n] = at
-            if i == 0:
-                places_ref[(pre - hops) * stride + n] = b
-            return n + jnp.where(at < blocks, 1, 0)
-
-        lax.fori_loop(0, blocks, step, jnp.int32(0), unroll=8)
-
-
-def place_listed(cache, places_ref, k_ref, v_ref, got_refs):
-    per_peer = got_refs[0].shape[0]
+    per_peer = got_ref.shape[0]
     stride = per_peer + 1
+
+    def place(values_at):
+        for n in range(per_peer):
+            at = places_ref[(hop - 2) * stride + n]
+            b = places_ref[(pre - 2 + hop - 2) * stride + n]
+            rows = pl.ds(pl.multiple_of(b * BLK, BLK), BLK)
+            values = values_at(n, rows)
+            parts = []
+            for g in range(k_ref.shape[1] // HD):
+                span = slice(g * HD, (g + 1) * HD)
+                parts += [k_ref[rows, span], values[:, span]]
+            cache[at] = jnp.concatenate(parts, axis=1)
+
+    pl.when(me >= hop)(lambda: place(lambda n, rows: v_ref[rows]))
+    pl.when(me < hop)(lambda: place(lambda n, rows: got_ref[n]))
+
+
+def place_packed(cache, places_ref, distance, got_ref):
+    per_peer = got_ref.shape[0]
     for n in range(per_peer):
-        b = places_ref[(len(got_refs) + 1) * stride + n]
-        cache[places_ref[n]] = block_of(k_ref, v_ref, pl.multiple_of(b * BLK, BLK))
-        for i, got_ref in enumerate(got_refs):
-            cache[places_ref[(i + 1) * stride + n]] = got_ref[n]
+        cache[places_ref[(distance - 2) * (per_peer + 1) + n]] = got_ref[n]
 
 
 def values_kernel(
@@ -271,10 +296,10 @@
     refs = list(refs)
     if not first_out:
         refs.pop(0)
-    got_refs = [refs.pop(0) for _ in range(hops + 1, pre)] if last else []
+    got_far = [refs.pop(0) for _ in range(hops + 1, pre)][::-1] if last else []
+    got_ref = None if first_out else refs.pop(0)
     out_hbm, cache_out = refs.pop(0), refs.pop(0)
     state = () if last else (refs.pop(0), refs.pop(0))
-    places_ref = refs.pop(0) if first_out else None
     turned, out_buf, sems, *rest = refs
     rows = v_ref.shape[0]
     blocks = rows // BLK
@@ -283,13 +308,13 @@
 
     cache = rest[0] if last else cache_out
     cache[...] = cache_in[...]
+    if first_out:
+        place_blocks(cache, slot_ref, k_ref, v_ref, hop, pre, blocks)
+    else:
+        place_listed(cache, slot_ref, hop, pre, k_ref, v_ref, got_ref)
     if last:
-        place_listed(cache, slot_ref, k_ref, v_ref, got_refs)
-    else:
-        place_blocks(cache, slot_ref, k_ref, v_ref, hop, pre, blocks)
-    if first_out:
-        list_places(places_ref, slot_ref, hops, pre, blocks)
-    if last:
+        for n, far_ref in enumerate(got_far):
+            place_packed(cache, slot_ref, hops + 1 + n, far_ref)
         cache_store = pltpu.make_async_copy(cache.at[0:blocks], cache_out, sems.at[tiles])
         cache_store.start()
 
@@ -370,24 +395,27 @@
 
     k, v = lax.ppermute(new_keys, "pre", ring), lax.ppermute(new_values, "pre", ring)
 
-    packed = shape((per_peer, BLK, 2 * kv_width), bf16)
+    packed = (shape((per_peer, BLK, kv_width), bf16),) * (hops - 1)
+    packed += (shape((per_peer, BLK, 2 * kv_width), bf16),) * (pre - 1 - hops)
+    places = shape(((pre - 2 + hops - 1) * (per_peer + 1),), jnp.int32)
     in_hbm = (
         pltpu.with_memory_space_constraint(x, pltpu.HBM) for x in (queries, new_keys, new_values)
     )
-    q, acc, total, top, cache, *sent = pl.pallas_call(
+    q, acc, total, top, cache, places, *sent = pl.pallas_call(
         functools.partial(own_kernel, pre, hops),
-        out_shape=(attended_shape, acc_shape, stat_shape, stat_shape, open_cache)
-        + (packed,) * (pre - 1 - hops),
+        out_shape=(attended_shape, acc_shape, stat_shape, stat_shape, open_cache, places)
+        + packed,
         in_specs=[SMEM, SMEM] + [HBM] * 3,
-        out_specs=(VMEM,) * 5 + (HBM,) * (pre - 1 - hops),
+        out_specs=(VMEM,) * 5 + (SMEM,) + (HBM,) * (pre - 2),
         scratch_shapes=[
             pltpu.VMEM((rows, kv_width), bf16),
             pltpu.VMEM((rows, kv_width), bf16),
             turned,
             bias,
+            pltpu.VMEM(((hops - 1) * per_peer + 1, BLK, kv_width), bf16),
             pltpu.VMEM(((pre - 1 - hops) * per_peer + 1, BLK, 2 * kv_width), bf16),
             pltpu.SMEM((pre,), jnp.int32),
-            pltpu.SemaphoreType.DMA((pre - 1 - hops,)),
+            pltpu.SemaphoreType.DMA((pre - 2,)),
             pltpu.SemaphoreType.DMA((3,)),
         ],
         cost_estimate=cost(1, 4),
@@ -399,6 +427,7 @@
     attended = None
     for hop in range(1, hops + 1):
         first_out, last = hop == 1, hop == hops
+        onward = [(i, i + 1) for i in range(hop, pre - 1)]
         next_k = None if last else lax.ppermute(k, "pre", ring)
         weights, factor, *tops = pl.pallas_call(
             functools.partial(scores_kernel, hop),
@@ -411,26 +440,26 @@
             name="scores",
         )(lengths, q, k, top)
         v = after(v, factor)
-        next_v = None if last else lax.ppermute(v, "pre", ring)
+        next_v = None if last else lax.ppermute(v, "pre", onward)
         if first_out:
-            for d in range(hops + 1, pre):
-                pairs = [(i, (i + d) % pre) for i in range(pre)]
-                got.append(lax.ppermute(after(sent[d - hops - 1], v), "pre", pairs))
-        places = shape(((pre - hops + 1) * (per_peer + 1),), jnp.int32)
+            for d in reversed(range(2, pre)):
+                targets = range(d if d <= hops else pre)
+                pairs = [((i - d) % pre, i) for i in targets]
+                got.insert(0, lax.ppermute(after(sent[d - 2], v), "pre", pairs))
         carry = () if last else (acc_shape, stat_shape)
-        extra = ([] if first_out else [attended]) + (got if last else [])
+        extra = [] if first_out else [attended]
+        extra += got[: hops - 2 : -1] if last else []
+        extra += [] if first_out else [got[hop - 2]]
         attended, cache, *state = pl.pallas_call(
             functools.partial(values_kernel, hop, hops, pre),
             out_shape=(attended_shape, cache_shape if last else open_cache)
-            + carry
-            + ((places,) if first_out else ()),
+            + carry,
             in_specs=[SMEM, SMEM]
             + [VMEM] * 7
             + ([] if first_out else [HBM])
-            + ([VMEM] * len(got) if last else []),
+            + [VMEM] * (len(extra) - 1),
             out_specs=(HBM, HBM if last else VMEM)
-            + (VMEM,) * len(carry)
-            + ((SMEM,) if first_out else ()),
+            + (VMEM,) * len(carry),
             scratch_shapes=[
                 turned,
                 pltpu.VMEM((rows, q_width), bf16),
@@ -441,9 +470,7 @@
             cost_estimate=cost(0.5, 3),
             compiler_params=params,
             name="values",
-        )(lengths, far_places if last else block_slot, v, k, weights, factor, acc, total, cache, *extra)
-        if first_out:
-            far_places = state.pop()
+        )(lengths, block_slot if first_out else places, v, k, weights, factor, acc, total, cache, *extra)
         if not last:
             (top,) = tops
             acc, total = state

time: 33.7 us -> 31.3 us (0.929)
  waiting for transfers between devices: 11.8 us -> 7.97 us
  starting transfers between devices: 8.73 us -> 10.3 us
    ppermute x2 -> x3, waiting for transfers between devices: 5.66 us -> 3.24 us  [the longest x2 3.24 us: on_device(): got.insert(0, lax.ppermute(after(sent[d - 2], v), 'pre', pairs))]
    pallas_call x2, Pallas kernels: 4.36 us -> 3.49 us  [on_device(): pl.pallas_call(functools.partial(values_kernel, hop, hops, pre), out_shap...]
    ppermute x2 -> x3, starting transfers between devices: 3.82 us -> 4.67 us  [the longest x2 4.01 us: on_device(): got.insert(0, lax.ppermute(after(sent[d - 2], v), 'pre', pairs))]
    ppermute x1, waiting for transfers between devices: 1.39 us -> 0.67 us  [on_device(): lax.ppermute(new_keys, 'pre', ring)]
    pallas_call x1, Pallas kernels: 5.08 us -> 5.8 us  [on_device(): pl.pallas_call(functools.partial(own_kernel, pre, hops), out_shape=(atten...]
    ppermute x1, starting transfers between devices: 0.25 us -> 0.97 us  [on_device(): next_k = None if last else lax.ppermute(k, 'pre', ring)]
    ppermute x1, waiting for transfers between devices: 4.77 us -> 4.06 us  [on_device(): lax.ppermute(new_values, 'pre', ring)]
  transfers between devices with their start and end apart: 5 -> 6, of which waited for: 4 -> 3; matrix products, arithmetic and copies ran while one was open for 0% -> 0% of each run, Pallas kernels for 28% -> 30%
where the time goes in v7:
time: 31.3 us; the launch traced here: 31.1 us
  Pallas kernels  10.6 us (34%)
  starting transfers between devices  10.3 us (33%)
  waiting for transfers between devices  7.97 us (25%)
  local copies, waits for them, and re-layouts  1.31 us (4%)
  between operations  0.86 us (3%)
    pallas_call x1, Pallas kernels, on_device(): pl.pallas_call(functools.partial(own_kernel, pre, hops), out_shape=(atten...  5.8 us
    ppermute x1, waiting for transfers between devices, on_device(): lax.ppermute(new_values, 'pre', ring)  4.06 us
    ppermute x2, starting transfers between devices, on_device(): got.insert(0, lax.ppermute(after(sent[d - 2], v), 'pre', pairs))  4.01 us
    pallas_call x2, Pallas kernels, on_device(): pl.pallas_call(functools.partial(values_kernel, hop, hops, pre), out_shap...  3.49 us
    ppermute x2, waiting for transfers between devices, on_device(): got.insert(0, lax.ppermute(after(sent[d - 2], v), 'pre', pairs))  3.24 us
    ppermute x1, starting transfers between devices, on_device(): lax.ppermute(new_keys, 'pre', ring)  3.08 us
    ppermute x1, starting transfers between devices, on_device(): lax.ppermute(new_values, 'pre', ring)  1.58 us
    pallas_call x2, Pallas kernels, on_device(): pl.pallas_call(functools.partial(scores_kernel, hop), out_shape=(weights_...  1.35 us
  transfers between devices with their start and end apart: 6, of which 3 were waited for; matrix products, arithmetic and copies ran while one was open for 0% of the time, Pallas kernels for 30%

profile of v7, /device:TPU:0, one launch (start us, length us, event | category | flops | bytes accessed | tf_op | source)
XLA Modules:
  0.0 31.1 jit_solution(1170457971083205566)
XLA Ops:
  0.6 3.1 %collective-permute-start.1 = (bf16[512,256]{1,0:T(8,128)(2,1)}, bf16[512,256]{1,0:T(8,128)(2,1)S(1)}, u32[]{:S(2)}, u32[]{:S(2)}) collective-permute-start(bf16[512,256]{1,0:T(8,128)(2,1)} %k_hbm.1), channel_id=1, source_target_pairs={{0,4},{4,8},{8,12},{12,0},{1,5},{5,9},{9,13},{13,1},{2,6},{6,10},{... | collective-permute-start | bytes 786440 | tf_op jit(solution)/shard_map/ppermute | solution.py:396
  3.7 1.6 %collective-permute-start = (bf16[512,256]{1,0:T(8,128)(2,1)}, bf16[512,256]{1,0:T(8,128)(2,1)S(1)}, u32[]{:S(2)}, u32[]{:S(2)}) collective-permute-start(bf16[512,256]{1,0:T(8,128)(2,1)} %v_hbm.1), channel_id=1, source_target_pairs={{0,4},{4,8},{8,12},{12,0},{1,5},{5,9},{9,13},{13,1},{2,6},{6,10},{... | collective-permute-start | bytes 786440 | tf_op jit(solution)/shard_map/ppermute | solution.py:396
  5.3 0.0 copy-start
  5.3 0.7 %copy-done = s32[4]{0:T(128)S(1)} copy-done((s32[4]{0:T(128)S(1)}, s32[4]{0:T(128)}, u32[]{:S(2)}) %copy-start) | copy-done | bytes 40
  5.9 0.0 copy-start.1
  5.9 0.7 %copy-done.1 = s32[128]{0:T(128)S(1)} copy-done((s32[128]{0:T(128)S(1)}, s32[128]{0:T(128)}, u32[]{:S(2)}) %copy-start.1) | copy-done | bytes 536
  6.6 5.8 %own_attention.1 = (bf16[512,1024]{1,0:T(8,128)(2,1)S(1)}, f32[2,128,2048]{2,1,0:T(8,128)S(1)}, f32[2,8,2048]{2,1,0:T(8,128)S(1)}, f32[2,8,2048]{2,1,0:T(8,128)S...) custom-call(s32[4]{0:T(128)S(1)} %copy-done, ...), custom_call_target="tpu_custom_call" | custom-call | flops 1073741824 | bytes 4194304 | tf_op jit(solution)/shard_map/own_attention/pallas_call | solution.py:404
  12.4 0.7 %collective-permute-done.1.k_ref = bf16[512,256]{1,0:T(8,128)(2,1)S(1)} collective-permute-done((bf16[512,256]{1,0:T(8,128)(2,1)}, bf16[512,256]{1,0:T(8,128)(2,1)S(1)}, u32[]{:S(2)}, u32[]{:S(2)}) %collective-permute-start.1) | collective-permute-done | bytes 262176 | tf_op jit(solution)/shard_map/ppermute | solution.py:396
  13.1 1.0 %collective-permute-start.3 = (bf16[512,256]{1,0:T(8,128)(2,1)S(1)}, bf16[512,256]{1,0:T(8,128)(2,1)S(1)}, u32[]{:S(2)}, u32[]{:S(2)}) collective-permute-start(bf16[512,256]{1,0:T(8,128)(2,1)S(1)} %collective-permute-done.1.k_ref), channel_id=1, source_target_pairs={{0,4},{4,8},{8,12},{12,0},{1,5},{5,9},{9,13},{13,1},{2,6},{6,10},{... | collective-permute-start | bytes 786440 | tf_op jit(solution)/shard_map/ppermute | solution.py:431
  14.0 0.6 %scores.2 = (bf16[2,2,512,1024]{3,2,1,0:T(8,128)(2,1)S(1)}, f32[2,8,2048]{2,1,0:T(8,128)S(1)}, f32[2,8,2048]{2,1,0:T(8,128)S(1)}) custom-call(s32[4]{0:T(128)S(1)} %copy-done, bf16[512,1024]{1,0:T(8,128)(2,1)S(1)} %get-tuple-element.26.q_ref, bf16[512,256]{1,0:T(8,128)(2,1)S(1)} %collective-permute-done.1.k_ref, f32[2,8,2048]{2,1,0:T(8,128)S(1)} %get-tuple-element.27.old_top), custom_call_target="tpu_custom_call" | custom-call | flops 536870912 | bytes 3145728 | tf_op jit(solution)/shard_map/scores/pallas_call | solution.py:432
  14.6 4.1 %collective-permute-done.v_ref = bf16[512,256]{1,0:T(8,128)(2,1)S(1)} collective-permute-done((bf16[512,256]{1,0:T(8,128)(2,1)}, bf16[512,256]{1,0:T(8,128)(2,1)S(1)}, u32[]{:S(2)}, u32[]{:S(2)}) %collective-permute-start) | collective-permute-done | bytes 262176 | tf_op jit(solution)/shard_map/ppermute | solution.py:396
  18.7 0.7 %collective-permute-start.2 = (bf16[512,256]{1,0:T(8,128)(2,1)S(1)}, bf16[512,256]{1,0:T(8,128)(2,1)S(1)}, u32[]{:S(2)}, u32[]{:S(2)}) collective-permute-start(bf16[512,256]{1,0:T(8,128)(2,1)S(1)} %collective-permute-done.v_ref), channel_id=1, source_target_pairs={{4,8},{8,12},{5,9},{9,13},{6,10},{10,14},{7,11},{11,15},{20,24},{2... | collective-permute-start | bytes 786440 | tf_op jit(solution)/shard_map/ppermute | solution.py:443
  19.4 2.7 %collective-permute-start.4 = (bf16[8,16,512]{2,1,0:T(8,128)(2,1)S(1)}, bf16[8,16,512]{2,1,0:T(8,128)(2,1)S(1)}, u32[]{:S(2)}, u32[]{:S(2)}) collective-permute-start(bf16[8,16,512]{2,1,0:T(8,128)(2,1)S(1)} %get-tuple-element.45), channel_id=1, source_target_pairs={{4,0},{8,4},{12,8},{0,12},{5,1},{9,5},{13,9},{1,13},{6,2},{10,6},{... | collective-permute-start | bytes 393224 | tf_op jit(solution)/shard_map/ppermute | solution.py:448
  22.1 1.3 %collective-permute-start.5 = (bf16[8,16,256]{2,1,0:T(8,128)(2,1)S(1)}, bf16[8,16,256]{2,1,0:T(8,128)(2,1)S(1)}, u32[]{:S(2)}, u32[]{:S(2)}) collective-permute-start(bf16[8,16,256]{2,1,0:T(8,128)(2,1)S(1)} %get-tuple-element.47), channel_id=1, source_target_pairs={{8,0},{12,4},{9,1},{13,5},{10,2},{14,6},{11,3},{15,7},{24,16},{28,... | collective-permute-start | bytes 196616 | tf_op jit(solution)/shard_map/ppermute | solution.py:448
  23.4 2.1 %values.2 = (bf16[512,1024]{1,0:T(8,128)(2,1)}, bf16[33,16,512]{2,1,0:T(8,128)(2,1)S(1)}, f32[2,128,2048]{2,1,0:T(8,128)S(1)}, f32[2,8,2048]{2,1,0:T(8,128)S(1)}) custom-call(s32[4]{0:T(128)S(1)} %copy-done, s32[128]{0:T(128)S(1)} %copy-done.1, bf16[512,256]{1,0:T(8,128)(2,1)S(1)} %collective-permute-done.v_ref, ...), custom_call_target="tpu_custom_call" | custom-call | flops 536870912 | bytes 3145728 | tf_op jit(solution)/shard_map/values/pallas_call | solution.py:453
  25.4 0.0 collective-permute-done.3.k_ref
  25.5 0.8 %scores.3 = (bf16[2,2,512,1024]{3,2,1,0:T(8,128)(2,1)S(1)}, f32[2,8,2048]{2,1,0:T(8,128)S(1)}) custom-call(s32[4]{0:T(128)S(1)} %copy-done, bf16[512,1024]{1,0:T(8,128)(2,1)S(1)} %get-tuple-element.26.q_ref, bf16[512,256]{1,0:T(8,128)(2,1)S(1)} %collective-permute-done.3.k_ref, f32[2,8,2048]{2,1,0:T(8,128)S(1)} %get-tuple-element.37.old_top), custom_call_target="tpu_custom_call" | custom-call | flops 536870912 | bytes 3145728 | tf_op jit(solution)/shard_map/scores/pallas_call | solution.py:432
  26.2 0.0 collective-permute-done.2.v_ref
  26.2 3.2 %collective-permute-done.5.refs_2_ = bf16[8,16,256]{2,1,0:T(8,128)(2,1)S(1)} collective-permute-done((bf16[8,16,256]{2,1,0:T(8,128)(2,1)S(1)}, bf16[8,16,256]{2,1,0:T(8,128)(2,1)S(1)}, u32[]{:S(2)}, u32[]{:S(2)}) %collective-permute-start.5) | collective-permute-done | bytes 65568 | tf_op jit(solution)/shard_map/ppermute | solution.py:448
  29.5 0.0 collective-permute-done.4.refs_1_
  29.5 1.4 %values.3 = (bf16[512,1024]{1,0:T(8,128)(2,1)}, bf16[32,16,512]{2,1,0:T(8,128)(2,1)}) custom-call(s32[4]{0:T(128)S(1)} %copy-done, s32[27]{0:T(128)S(1)} %get-tuple-element.25.slot_ref, bf16[512,256]{1,0:T(8,128)(2,1)S(1)} %collective-permute-done.2.v_ref, bf16[512,256]{1,0:T(8,128)(2,1)S(1)} %collective-permute-done.3.k_ref, ...), custom_call_target="tpu_custom_call", output_to_operand_aliasing={{0}: (9, {})} | custom-call | flops 536870912 | bytes 3145728 | tf_op jit(solution)/shard_map/values/pallas_call | solution.py:453
Async XLA Ops:
  0.6 12.4 %collective-permute-start.1 = (bf16[512,256]{1,0:T(8,128)(2,1)}, bf16[512,256]{1,0:T(8,128)(2,1)S(1)}, u32[]{:S(2)}, u32[]{:S(2)}) collective-permute-start(bf16[512,256]{1,0:T(8,128)(2,1)} %k_hbm.1), channel_id=1, source_target_pairs={{0,4},{4,8},{8,12},{12,0},{1,5},{5,9},{9,13},{13,1},{2,6},{6,10},{... | collective-permute-start | bytes 786440 | tf_op jit(solution)/shard_map/ppermute | solution.py:396
  3.7 15.0 %collective-permute-start = (bf16[512,256]{1,0:T(8,128)(2,1)}, bf16[512,256]{1,0:T(8,128)(2,1)S(1)}, u32[]{:S(2)}, u32[]{:S(2)}) collective-permute-start(bf16[512,256]{1,0:T(8,128)(2,1)} %v_hbm.1), channel_id=1, source_target_pairs={{0,4},{4,8},{8,12},{12,0},{1,5},{5,9},{9,13},{13,1},{2,6},{6,10},{... | collective-permute-start | bytes 786440 | tf_op jit(solution)/shard_map/ppermute | solution.py:396
  5.3 0.7 %copy-start = (s32[4]{0:T(128)S(1)}, s32[4]{0:T(128)}, u32[]{:S(2)}) copy-start(s32[4]{0:T(128)} %lengths_ref.9) | copy-start | bytes 52
  5.9 0.7 %copy-start.1 = (s32[128]{0:T(128)S(1)}, s32[128]{0:T(128)}, u32[]{:S(2)}) copy-start(s32[128]{0:T(128)} %slot_ref.3) | copy-start | bytes 1540
  13.1 12.4 %collective-permute-start.3 = (bf16[512,256]{1,0:T(8,128)(2,1)S(1)}, bf16[512,256]{1,0:T(8,128)(2,1)S(1)}, u32[]{:S(2)}, u32[]{:S(2)}) collective-permute-start(bf16[512,256]{1,0:T(8,128)(2,1)S(1)} %collective-permute-done.1.k_ref), channel_id=1, source_target_pairs={{0,4},{4,8},{8,12},{12,0},{1,5},{5,9},{9,13},{13,1},{2,6},{6,10},{... | collective-permute-start | bytes 786440 | tf_op jit(solution)/shard_map/ppermute | solution.py:431
  18.7 7.5 %collective-permute-start.2 = (bf16[512,256]{1,0:T(8,128)(2,1)S(1)}, bf16[512,256]{1,0:T(8,128)(2,1)S(1)}, u32[]{:S(2)}, u32[]{:S(2)}) collective-permute-start(bf16[512,256]{1,0:T(8,128)(2,1)S(1)} %collective-permute-done.v_ref), channel_id=1, source_target_pairs={{4,8},{8,12},{5,9},{9,13},{6,10},{10,14},{7,11},{11,15},{20,24},{2... | collective-permute-start | bytes 786440 | tf_op jit(solution)/shard_map/ppermute | solution.py:443
  19.4 10.1 %collective-permute-start.4 = (bf16[8,16,512]{2,1,0:T(8,128)(2,1)S(1)}, bf16[8,16,512]{2,1,0:T(8,128)(2,1)S(1)}, u32[]{:S(2)}, u32[]{:S(2)}) collective-permute-start(bf16[8,16,512]{2,1,0:T(8,128)(2,1)S(1)} %get-tuple-element.45), channel_id=1, source_target_pairs={{4,0},{8,4},{12,8},{0,12},{5,1},{9,5},{13,9},{1,13},{6,2},{10,6},{... | collective-permute-start | bytes 393224 | tf_op jit(solution)/shard_map/ppermute | solution.py:448
  22.1 7.4 %collective-permute-start.5 = (bf16[8,16,256]{2,1,0:T(8,128)(2,1)S(1)}, bf16[8,16,256]{2,1,0:T(8,128)(2,1)S(1)}, u32[]{:S(2)}, u32[]{:S(2)}) collective-permute-start(bf16[8,16,256]{2,1,0:T(8,128)(2,1)S(1)} %get-tuple-element.47), channel_id=1, source_target_pairs={{8,0},{12,4},{9,1},{13,5},{10,2},{14,6},{11,3},{15,7},{24,16},{28,... | collective-permute-start | bytes 196616 | tf_op jit(solution)/shard_map/ppermute | solution.py:448

commit v8 on v7

--- a/solution.py
+++ b/solution.py
@@ -146,15 +146,21 @@
         lax.fori_loop(0, blocks, step, jnp.int32(0), unroll=8)
 
 
+def load_kernel(src, dst, sem):
+    copy = pltpu.make_async_copy(src, dst, sem)
+    copy.start()
+    copy.wait()
+
+
 def own_kernel(
-    pre, hops, lengths_ref, slot_ref, q_hbm, k_hbm, v_hbm,
+    pre, hops, lengths_ref, slot_ref, q_hbm, k_hbm, v_ref,
     q_ref, acc_ref, sum_ref, top_ref, cache_ref, places_ref, *refs,
 ):
     sent_hbm, refs = refs[: pre - 2], refs[pre - 2 :]
-    k_ref, v_ref, turned, bias, sent_values, sent, counts, sems, load_sems = refs
+    k_ref, turned, bias, sent_values, sent, counts, sems, load_sems = refs
     loads = [
         pltpu.make_async_copy(src, dst, load_sems.at[n])
-        for n, (src, dst) in enumerate(((k_hbm, k_ref), (v_hbm, v_ref), (q_hbm, q_ref)))
+        for n, (src, dst) in enumerate(((k_hbm, k_ref), (q_hbm, q_ref)))
     ]
     for load in loads:
         load.start()
@@ -167,7 +173,6 @@
         counts[owner] = 0
     list_places(places_ref, slot_ref, hops, pre, blocks)
     loads[0].wait()
-    loads[1].wait()
 
     def step(b, _):
         slot = slot_ref[me * blocks + b]
@@ -196,7 +201,7 @@
     for store in stores:
         store.start()
     turn_values(v_ref, turned)
-    loads[2].wait()
+    loads[1].wait()
     for tile in range(rows // TILE):
         high = (tile + 1) * TILE
         fill_bias(bias, lengths_ref, first + tile * TILE, first, 0, high, True)
@@ -393,22 +398,30 @@
     def after(array, *others):
         return lax.optimization_barrier((array, *others))[0]
 
-    k, v = lax.ppermute(new_keys, "pre", ring), lax.ppermute(new_values, "pre", ring)
+    k = lax.ppermute(new_keys, "pre", ring)
+    near_values = pl.pallas_call(
+        load_kernel,
+        out_shape=shape(new_values.shape, bf16),
+        in_specs=[HBM],
+        out_specs=VMEM,
+        scratch_shapes=[pltpu.SemaphoreType.DMA],
+        cost_estimate=cost(0, 1),
+        compiler_params=params,
+        name="load_values",
+    )(pltpu.with_memory_space_constraint(new_values, pltpu.HBM))
+    v = lax.ppermute(near_values, "pre", ring)
 
     packed = (shape((per_peer, BLK, kv_width), bf16),) * (hops - 1)
     packed += (shape((per_peer, BLK, 2 * kv_width), bf16),) * (pre - 1 - hops)
     places = shape(((pre - 2 + hops - 1) * (per_peer + 1),), jnp.int32)
-    in_hbm = (
-        pltpu.with_memory_space_constraint(x, pltpu.HBM) for x in (queries, new_keys, new_values)
-    )
+    in_hbm = (pltpu.with_memory_space_constraint(x, pltpu.HBM) for x in (queries, new_keys))
     q, acc, total, top, cache, places, *sent = pl.pallas_call(
         functools.partial(own_kernel, pre, hops),
         out_shape=(attended_shape, acc_shape, stat_shape, stat_shape, open_cache, places)
         + packed,
-        in_specs=[SMEM, SMEM] + [HBM] * 3,
+        in_specs=[SMEM, SMEM, HBM, HBM, VMEM],
         out_specs=(VMEM,) * 5 + (SMEM,) + (HBM,) * (pre - 2),
         scratch_shapes=[
-            pltpu.VMEM((rows, kv_width), bf16),
             pltpu.VMEM((rows, kv_width), bf16),
             turned,
             bias,
@@ -416,12 +429,12 @@
             pltpu.VMEM(((pre - 1 - hops) * per_peer + 1, BLK, 2 * kv_width), bf16),
             pltpu.SMEM((pre,), jnp.int32),
             pltpu.SemaphoreType.DMA((pre - 2,)),
-            pltpu.SemaphoreType.DMA((3,)),
+            pltpu.SemaphoreType.DMA((2,)),
         ],
         cost_estimate=cost(1, 4),
         compiler_params=own_params,
         name="own_attention",
-    )(lengths, block_slot, *in_hbm)
+    )(lengths, block_slot, *in_hbm, near_values)
     got = []
     k = after(k, top)
     attended = None

time: 31.3 us -> 31.5 us (level)
  waiting for transfers between devices: 7.97 us -> 6.27 us
  Pallas kernels: 10.6 us -> 11.5 us
  starting transfers between devices: 10.3 us -> 11.1 us
    ppermute x2, waiting for transfers between devices: 4.73 us -> 3.03 us  [the longest x1 3.03 us: on_device(): v = lax.ppermute(near_values, 'pre', ring)]
    pallas_call x0 -> x1, Pallas kernels: none -> 0.96 us  [on_device(): pl.pallas_call(load_kernel, out_shape=shape(new_values.shape, bf16), in_s...]
    ppermute x1, starting transfers between devices: 0.97 us -> 1.63 us  [on_device(): next_k = None if last else lax.ppermute(k, 'pre', ring)]
    unnamed x4 -> x6, local copies, waits for them, and re-layouts: 1.31 us -> 1.32 us
  transfers between devices with their start and end apart: 6 -> 6, of which waited for: 3 -> 2; matrix products, arithmetic and copies ran while one was open for 0% -> 0% of each run, Pallas kernels for 30% -> 32%
where the time goes in v8:
time: 31.5 us; the launch traced here: 31.1 us
  Pallas kernels  11.5 us (37%)
  starting transfers between devices  11.1 us (35%)
  waiting for transfers between devices  6.27 us (20%)
  local copies, waits for them, and re-layouts  1.32 us (4%)
  between operations  0.88 us (3%)
    pallas_call x1, Pallas kernels, on_device(): pl.pallas_call(functools.partial(own_kernel, pre, hops), out_shape=(atten...  5.71 us
    ppermute x2, starting transfers between devices, on_device(): got.insert(0, lax.ppermute(after(sent[d - 2], v), 'pre', pairs))  4.1 us
    pallas_call x2, Pallas kernels, on_device(): pl.pallas_call(functools.partial(values_kernel, hop, hops, pre), out_shap...  3.49 us
    ppermute x2, waiting for transfers between devices, on_device(): got.insert(0, lax.ppermute(after(sent[d - 2], v), 'pre', pairs))  3.24 us
    ppermute x1, starting transfers between devices, on_device(): k = lax.ppermute(new_keys, 'pre', ring)  3.08 us
    ppermute x1, waiting for transfers between devices, on_device(): v = lax.ppermute(near_values, 'pre', ring)  3.03 us
    ppermute x1, starting transfers between devices, on_device(): next_k = None if last else lax.ppermute(k, 'pre', ring)  1.63 us
    ppermute x1, starting transfers between devices, on_device(): v = lax.ppermute(near_values, 'pre', ring)  1.63 us
  transfers between devices with their start and end apart: 6, of which 2 were waited for; matrix products, arithmetic and copies ran while one was open for 0% of the time, Pallas kernels for 32%

profile of v8, /device:TPU:0, one launch (start us, length us, event | category | flops | bytes accessed | tf_op | source)
XLA Modules:
  0.0 31.1 jit_solution(6528265976524579991)
XLA Ops:
  0.6 0.0 copy-start.1
  0.6 3.1 %collective-permute-start.1 = (bf16[512,256]{1,0:T(8,128)(2,1)}, bf16[512,256]{1,0:T(8,128)(2,1)S(1)}, u32[]{:S(2)}, u32[]{:S(2)}) collective-permute-start(bf16[512,256]{1,0:T(8,128)(2,1)} %k_hbm.1), channel_id=1, source_target_pairs={{0,4},{4,8},{8,12},{12,0},{1,5},{5,9},{9,13},{13,1},{2,6},{6,10},{... | collective-permute-start | bytes 786440 | tf_op jit(solution)/shard_map/ppermute | solution.py:401
  3.7 1.0 %load_values.1.v_ref = bf16[512,256]{1,0:T(8,128)(2,1)S(1)} custom-call(bf16[512,256]{1,0:T(8,128)(2,1)} %src.1), custom_call_target="tpu_custom_call" | custom-call | bytes 1048576 | tf_op jit(solution)/shard_map/load_values/pallas_call | solution.py:402
  4.7 1.6 %collective-permute-start = (bf16[512,256]{1,0:T(8,128)(2,1)S(1)}, bf16[512,256]{1,0:T(8,128)(2,1)S(1)}, u32[]{:S(2)}, u32[]{:S(2)}) collective-permute-start(bf16[512,256]{1,0:T(8,128)(2,1)S(1)} %load_values.1.v_ref), channel_id=1, source_target_pairs={{0,4},{4,8},{8,12},{12,0},{1,5},{5,9},{9,13},{13,1},{2,6},{6,10},{... | collective-permute-start | bytes 786440 | tf_op jit(solution)/shard_map/ppermute | solution.py:412
  6.3 0.0 copy-start
  6.3 0.7 %copy-done = s32[4]{0:T(128)S(1)} copy-done((s32[4]{0:T(128)S(1)}, s32[4]{0:T(128)}, u32[]{:S(2)}) %copy-start) | copy-done | bytes 40
  7.0 0.0 copy-start.2
  7.0 0.7 %copy-done.2 = s32[128]{0:T(128)S(1)} copy-done((s32[128]{0:T(128)S(1)}, s32[128]{0:T(128)}, u32[]{:S(2)}) %copy-start.2) | copy-done | bytes 536
  7.6 5.7 %own_attention.1 = (bf16[512,1024]{1,0:T(8,128)(2,1)S(1)}, f32[2,128,2048]{2,1,0:T(8,128)S(1)}, f32[2,8,2048]{2,1,0:T(8,128)S(1)}, f32[2,8,2048]{2,1,0:T(8,128)S...) custom-call(s32[4]{0:T(128)S(1)} %copy-done, ...), custom_call_target="tpu_custom_call" | custom-call | flops 1073741824 | bytes 4194304 | tf_op jit(solution)/shard_map/own_attention/pallas_call | solution.py:418
  13.3 0.0 collective-permute-done.1.k_ref
  13.4 1.6 %collective-permute-start.3 = (bf16[512,256]{1,0:T(8,128)(2,1)S(1)}, bf16[512,256]{1,0:T(8,128)(2,1)S(1)}, u32[]{:S(2)}, u32[]{:S(2)}) collective-permute-start(bf16[512,256]{1,0:T(8,128)(2,1)S(1)} %collective-permute-done.1.k_ref), channel_id=1, source_target_pairs={{0,4},{4,8},{8,12},{12,0},{1,5},{5,9},{9,13},{13,1},{2,6},{6,10},{... | collective-permute-start | bytes 786440 | tf_op jit(solution)/shard_map/ppermute | solution.py:444
  15.0 0.0 copy-done.1
  15.0 0.6 %scores.2 = (bf16[2,2,512,1024]{3,2,1,0:T(8,128)(2,1)S(1)}, f32[2,8,2048]{2,1,0:T(8,128)S(1)}, f32[2,8,2048]{2,1,0:T(8,128)S(1)}) custom-call(s32[4]{0:T(128)S(1)} %copy-done.1, bf16[512,1024]{1,0:T(8,128)(2,1)S(1)} %get-tuple-element.26.q_ref, bf16[512,256]{1,0:T(8,128)(2,1)S(1)} %collective-permute-done.1.k_ref, f32[2,8,2048]{2,1,0:T(8,128)S(1)} %get-tuple-element.27.old_top), custom_call_target="tpu_custom_call" | custom-call | flops 536870912 | bytes 3145728 | tf_op jit(solution)/shard_map/scores/pallas_call | solution.py:445
  15.6 3.0 %collective-permute-done.v_ref = bf16[512,256]{1,0:T(8,128)(2,1)S(1)} collective-permute-done((bf16[512,256]{1,0:T(8,128)(2,1)S(1)}, bf16[512,256]{1,0:T(8,128)(2,1)S(1)}, u32[]{:S(2)}, u32[]{:S(2)}) %collective-permute-start) | collective-permute-done | bytes 262176 | tf_op jit(solution)/shard_map/ppermute | solution.py:412
  18.6 0.7 %collective-permute-start.2 = (bf16[512,256]{1,0:T(8,128)(2,1)S(1)}, bf16[512,256]{1,0:T(8,128)(2,1)S(1)}, u32[]{:S(2)}, u32[]{:S(2)}) collective-permute-start(bf16[512,256]{1,0:T(8,128)(2,1)S(1)} %collective-permute-done.v_ref), channel_id=1, source_target_pairs={{4,8},{8,12},{5,9},{9,13},{6,10},{10,14},{7,11},{11,15},{20,24},{2... | collective-permute-start | bytes 786440 | tf_op jit(solution)/shard_map/ppermute | solution.py:456
  19.3 2.8 %collective-permute-start.4 = (bf16[8,16,512]{2,1,0:T(8,128)(2,1)S(1)}, bf16[8,16,512]{2,1,0:T(8,128)(2,1)S(1)}, u32[]{:S(2)}, u32[]{:S(2)}) collective-permute-start(bf16[8,16,512]{2,1,0:T(8,128)(2,1)S(1)} %get-tuple-element.45), channel_id=1, source_target_pairs={{4,0},{8,4},{12,8},{0,12},{5,1},{9,5},{13,9},{1,13},{6,2},{10,6},{... | collective-permute-start | bytes 393224 | tf_op jit(solution)/shard_map/ppermute | solution.py:461
  22.1 1.3 %collective-permute-start.5 = (bf16[8,16,256]{2,1,0:T(8,128)(2,1)S(1)}, bf16[8,16,256]{2,1,0:T(8,128)(2,1)S(1)}, u32[]{:S(2)}, u32[]{:S(2)}) collective-permute-start(bf16[8,16,256]{2,1,0:T(8,128)(2,1)S(1)} %get-tuple-element.47), channel_id=1, source_target_pairs={{8,0},{12,4},{9,1},{13,5},{10,2},{14,6},{11,3},{15,7},{24,16},{28,... | collective-permute-start | bytes 196616 | tf_op jit(solution)/shard_map/ppermute | solution.py:461
  23.4 2.1 %values.2 = (bf16[512,1024]{1,0:T(8,128)(2,1)}, bf16[33,16,512]{2,1,0:T(8,128)(2,1)S(1)}, f32[2,128,2048]{2,1,0:T(8,128)S(1)}, f32[2,8,2048]{2,1,0:T(8,128)S(1)}) custom-call(s32[4]{0:T(128)S(1)} %copy-done.1, s32[128]{0:T(128)S(1)} %copy-done.2, bf16[512,256]{1,0:T(8,128)(2,1)S(1)} %collective-permute-done.v_ref, ...), custom_call_target="tpu_custom_call" | custom-call | flops 536870912 | bytes 3145728 | tf_op jit(solution)/shard_map/values/pallas_call | solution.py:466
  25.5 0.0 collective-permute-done.3.k_ref
  25.5 0.8 %scores.3 = (bf16[2,2,512,1024]{3,2,1,0:T(8,128)(2,1)S(1)}, f32[2,8,2048]{2,1,0:T(8,128)S(1)}) custom-call(s32[4]{0:T(128)S(1)} %copy-done.1, bf16[512,1024]{1,0:T(8,128)(2,1)S(1)} %get-tuple-element.26.q_ref, bf16[512,256]{1,0:T(8,128)(2,1)S(1)} %collective-permute-done.3.k_ref, f32[2,8,2048]{2,1,0:T(8,128)S(1)} %get-tuple-element.37.old_top), custom_call_target="tpu_custom_call" | custom-call | flops 536870912 | bytes 3145728 | tf_op jit(solution)/shard_map/scores/pallas_call | solution.py:445
  26.2 0.0 collective-permute-done.2.v_ref
  26.3 3.2 %collective-permute-done.5.refs_2_ = bf16[8,16,256]{2,1,0:T(8,128)(2,1)S(1)} collective-permute-done((bf16[8,16,256]{2,1,0:T(8,128)(2,1)S(1)}, bf16[8,16,256]{2,1,0:T(8,128)(2,1)S(1)}, u32[]{:S(2)}, u32[]{:S(2)}) %collective-permute-start.5) | collective-permute-done | bytes 65568 | tf_op jit(solution)/shard_map/ppermute | solution.py:461
  29.5 0.0 collective-permute-done.4.refs_1_
  29.5 1.4 %values.3 = (bf16[512,1024]{1,0:T(8,128)(2,1)}, bf16[32,16,512]{2,1,0:T(8,128)(2,1)}) custom-call(s32[4]{0:T(128)S(1)} %copy-done.1, s32[27]{0:T(128)S(1)} %get-tuple-element.25.slot_ref, bf16[512,256]{1,0:T(8,128)(2,1)S(1)} %collective-permute-done.2.v_ref, bf16[512,256]{1,0:T(8,128)(2,1)S(1)} %collective-permute-done.3.k_ref, ...), custom_call_target="tpu_custom_call", output_to_operand_aliasing={{0}: (9, {})} | custom-call | flops 536870912 | bytes 3145728 | tf_op jit(solution)/shard_map/values/pallas_call | solution.py:466
Async XLA Ops:
  0.6 14.4 %copy-start.1 = (s32[4]{0:T(128)S(1)}, s32[4]{0:T(128)}, u32[]{:S(2)}) copy-start(s32[4]{0:T(128)} %lengths_ref.9) | copy-start | bytes 52
  0.6 12.7 %collective-permute-start.1 = (bf16[512,256]{1,0:T(8,128)(2,1)}, bf16[512,256]{1,0:T(8,128)(2,1)S(1)}, u32[]{:S(2)}, u32[]{:S(2)}) collective-permute-start(bf16[512,256]{1,0:T(8,128)(2,1)} %k_hbm.1), channel_id=1, source_target_pairs={{0,4},{4,8},{8,12},{12,0},{1,5},{5,9},{9,13},{13,1},{2,6},{6,10},{... | collective-permute-start | bytes 786440 | tf_op jit(solution)/shard_map/ppermute | solution.py:401
  4.7 13.9 %collective-permute-start = (bf16[512,256]{1,0:T(8,128)(2,1)S(1)}, bf16[512,256]{1,0:T(8,128)(2,1)S(1)}, u32[]{:S(2)}, u32[]{:S(2)}) collective-permute-start(bf16[512,256]{1,0:T(8,128)(2,1)S(1)} %load_values.1.v_ref), channel_id=1, source_target_pairs={{0,4},{4,8},{8,12},{12,0},{1,5},{5,9},{9,13},{13,1},{2,6},{6,10},{... | collective-permute-start | bytes 786440 | tf_op jit(solution)/shard_map/ppermute | solution.py:412
  6.3 0.7 %copy-start = (s32[4]{0:T(128)S(1)}, s32[4]{0:T(128)}, u32[]{:S(2)}) copy-start(s32[4]{0:T(128)} %lengths_ref.9) | copy-start | bytes 52
  7.0 0.7 %copy-start.2 = (s32[128]{0:T(128)S(1)}, s32[128]{0:T(128)}, u32[]{:S(2)}) copy-start(s32[128]{0:T(128)} %slot_ref.3) | copy-start | bytes 1540
  13.4 12.1 %collective-permute-start.3 = (bf16[512,256]{1,0:T(8,128)(2,1)S(1)}, bf16[512,256]{1,0:T(8,128)(2,1)S(1)}, u32[]{:S(2)}, u32[]{:S(2)}) collective-permute-start(bf16[512,256]{1,0:T(8,128)(2,1)S(1)} %collective-permute-done.1.k_ref), channel_id=1, source_target_pairs={{0,4},{4,8},{8,12},{12,0},{1,5},{5,9},{9,13},{13,1},{2,6},{6,10},{... | collective-permute-start | bytes 786440 | tf_op jit(solution)/shard_map/ppermute | solution.py:444
  18.6 7.6 %collective-permute-start.2 = (bf16[512,256]{1,0:T(8,128)(2,1)S(1)}, bf16[512,256]{1,0:T(8,128)(2,1)S(1)}, u32[]{:S(2)}, u32[]{:S(2)}) collective-permute-start(bf16[512,256]{1,0:T(8,128)(2,1)S(1)} %collective-permute-done.v_ref), channel_id=1, source_target_pairs={{4,8},{8,12},{5,9},{9,13},{6,10},{10,14},{7,11},{11,15},{20,24},{2... | collective-permute-start | bytes 786440 | tf_op jit(solution)/shard_map/ppermute | solution.py:456
  19.3 10.2 %collective-permute-start.4 = (bf16[8,16,512]{2,1,0:T(8,128)(2,1)S(1)}, bf16[8,16,512]{2,1,0:T(8,128)(2,1)S(1)}, u32[]{:S(2)}, u32[]{:S(2)}) collective-permute-start(bf16[8,16,512]{2,1,0:T(8,128)(2,1)S(1)} %get-tuple-element.45), channel_id=1, source_target_pairs={{4,0},{8,4},{12,8},{0,12},{5,1},{9,5},{13,9},{1,13},{6,2},{10,6},{... | collective-permute-start | bytes 393224 | tf_op jit(solution)/shard_map/ppermute | solution.py:461
  22.1 7.4 %collective-permute-start.5 = (bf16[8,16,256]{2,1,0:T(8,128)(2,1)S(1)}, bf16[8,16,256]{2,1,0:T(8,128)(2,1)S(1)}, u32[]{:S(2)}, u32[]{:S(2)}) collective-permute-start(bf16[8,16,256]{2,1,0:T(8,128)(2,1)S(1)} %get-tuple-element.47), channel_id=1, source_target_pairs={{8,0},{12,4},{9,1},{13,5},{10,2},{14,6},{11,3},{15,7},{24,16},{28,... | collective-permute-start | bytes 196616 | tf_op jit(solution)/shard_map/ppermute | solution.py:461
